TPU v7x, 32 devices: a whole 2x2x4 slice. The times are simulated.
32 devices in a mesh: dp: 16 (over z, x, core), tensor: 2 (over y).
Axes of the slice: x: 2, y: 2, z: 4, core: 2. Of those that a mesh axis runs over, the one named last changes fastest.
Arguments:
- tokens: bfloat16 [8192, 1024], P(('dp', 'tensor')), may hold values from -6 to 6
- w_qkv: bfloat16 [1024, 3, 1024], P(None, None, 'tensor'), may hold values from -0.1875 to 0.1875
- b_query: float32 [1024], P('tensor'), may hold values from -3 to 3
- b_value: float32 [1024], P('tensor'), may hold values from -3 to 3
- w_out: bfloat16 [1024, 1024], P('tensor'), may hold values from -1.5 to 1.5
- b_out: float32 [1024], replicated, may hold values from -3 to 3
- gain_one: float32 [1024], replicated, may hold values from 0.25 to 1.75
- shift_one: float32 [1024], replicated, may hold values from -3 to 3
- w_up: bfloat16 [1024, 4096], P(None, 'tensor'), may hold values from -0.1875 to 0.1875
- b_up: float32 [4096], P('tensor'), may hold values from -3 to 3
- w_down: bfloat16 [4096, 1024], P('tensor'), may hold values from -0.09375 to 0.09375
- b_down: float32 [1024], replicated, may hold values from -3 to 3
- gain_two: float32 [1024], replicated, may hold values from 0.25 to 1.75
- shift_two: float32 [1024], replicated, may hold values from -3 to 3
- out_grad: bfloat16 [8192, 1024], P(('dp', 'tensor')), may hold values from -6 to 6
Outputs:
- layer_out: bfloat16 [8192, 1024], P(('dp', 'tensor'))
- grad_tokens: float32 [8192, 1024], P(('dp', 'tensor'))
- grad_w_qkv: float32 [1024, 3, 1024], P(None, None, 'tensor')
- grad_b_query: float32 [1024], P('tensor')
- grad_b_value: float32 [1024], P('tensor')
- grad_w_out: float32 [1024, 1024], P('tensor')
- grad_b_out: float32 [1024], replicated
- grad_gain_one: float32 [1024], replicated
- grad_shift_one: float32 [1024], replicated
- grad_w_up: float32 [1024, 4096], P(None, 'tensor')
- grad_b_up: float32 [4096], P('tensor')
- grad_w_down: float32 [4096, 1024], P('tensor')
- grad_b_down: float32 [1024], replicated
- grad_gain_two: float32 [1024], replicated
- grad_shift_two: float32 [1024], replicated
All inputs are finite; a program needn't handle non-finite values.
Results may differ from a plain program's by a relative error of at most 0.02.
Values may be sent and summed in bfloat16 or wider, within the bound.
No kernel may reach another device: no remote copies, remote signals or barrier semaphores. Data moves between devices by JAX's collectives and lax.ppermute only.
A program may use at most 128 MiB of HBM per device.

v0:
```python
import jax
import jax.numpy as jnp
from jax import lax
from jax.sharding import PartitionSpec as P

HEAD_DIM = 64
LEN = 512


EPSILON = 1e-12


def norm_rows(resid, gain, shift):
    center = jnp.mean(resid, axis=-1, keepdims=True)
    centred = resid - center
    variance = jnp.mean(centred * centred, axis=-1, keepdims=True)
    return centred * lax.rsqrt(variance + EPSILON) * gain + shift


def gelu_exact(upward):
    return jax.nn.gelu(upward, approximate=False)


def contract_rows(left, right):
    return lax.dot_general(
        left, right, (((0,), (0,)), ((), ())), preferred_element_type=jnp.float32
    )


def times_transposed(left, right):
    return lax.dot_general(
        left, right, (((1,), (1,)), ((), ())), preferred_element_type=jnp.float32
    )


def project_qkv(gathered, qkv_flat, b_query, b_value, heads_here):
    row_total = gathered.shape[0]
    seq_count = row_total // LEN
    projected = jnp.dot(gathered, qkv_flat, preferred_element_type=jnp.float32)
    projected = projected.reshape(row_total, 3, heads_here, HEAD_DIM)
    queries = (projected[:, 0] + b_query.reshape(heads_here, HEAD_DIM)).astype(jnp.bfloat16)
    key_rows = projected[:, 1].astype(jnp.bfloat16)
    values = (projected[:, 2] + b_value.reshape(heads_here, HEAD_DIM)).astype(jnp.bfloat16)
    new_shape = (seq_count, LEN, heads_here, HEAD_DIM)
    return (queries.reshape(new_shape), key_rows.reshape(new_shape), values.reshape(new_shape))


def attend(bundle):
    seq_query, seq_keys, seq_values = bundle
    scores = jnp.einsum(
        "qhd,khd->hqk", seq_query, seq_keys, preferred_element_type=jnp.float32
    ) * HEAD_DIM ** (-0.5)
    row_peak = jnp.max(scores, axis=-1, keepdims=True)
    exponent = jnp.exp(scores - row_peak)
    denom_sum = jnp.sum(exponent, axis=-1, keepdims=True)
    prob_rows = (exponent / denom_sum).astype(jnp.bfloat16)
    context = jnp.einsum("hqk,khd->qhd", prob_rows, seq_values, preferred_element_type=jnp.float32)
    return (context.astype(jnp.bfloat16), (row_peak + jnp.log(denom_sum))[..., 0])


def attend_back(bundle):
    seq_query, seq_keys, seq_values, seq_dcontext, seq_lognorm = bundle
    score_scale = HEAD_DIM ** (-0.5)
    scores = (
        jnp.einsum("qhd,khd->hqk", seq_query, seq_keys, preferred_element_type=jnp.float32)
        * score_scale
    )
    prob_rows = jnp.exp(scores - seq_lognorm[..., None])
    d_values = jnp.einsum(
        "hqk,qhd->khd",
        prob_rows.astype(jnp.bfloat16),
        seq_dcontext,
        preferred_element_type=jnp.float32,
    )
    d_probs = jnp.einsum(
        "qhd,khd->hqk", seq_dcontext, seq_values, preferred_element_type=jnp.float32
    )
    d_scores = prob_rows * (d_probs - jnp.sum(prob_rows * d_probs, axis=-1, keepdims=True))
    d_scores = d_scores.astype(jnp.bfloat16)
    d_queries = (
        jnp.einsum("hqk,khd->qhd", d_scores, seq_keys, preferred_element_type=jnp.float32)
        * score_scale
    )
    d_keys = (
        jnp.einsum("hqk,qhd->khd", d_scores, seq_query, preferred_element_type=jnp.float32)
        * score_scale
    )
    return jnp.stack([d_queries, d_keys, d_values], axis=1)


def body(
    tokens,
    w_qkv,
    b_query,
    b_value,
    w_out,
    b_out,
    gain_one,
    shift_one,
    w_up,
    b_up,
    w_down,
    b_down,
    gain_two,
    shift_two,
    out_grad,
):
    own_rows, width = tokens.shape
    local_width = w_out.shape[0]
    heads_here = local_width // HEAD_DIM
    qkv_flat = w_qkv.reshape(width, 3 * local_width)
    gathered = lax.all_gather(tokens, "tensor", axis=0, tiled=True)
    row_total = gathered.shape[0]
    seq_count = row_total // LEN
    queries, key_rows, values = project_qkv(gathered, qkv_flat, b_query, b_value, heads_here)
    context, lognorm = lax.map(attend, (queries, key_rows, values))
    context = context.reshape(row_total, local_width)
    out_whole = lax.all_gather(w_out, "tensor", axis=0, tiled=True)
    own_context = lax.all_to_all(context, "tensor", split_axis=0, concat_axis=1, tiled=True)
    attended = jnp.dot(own_context, out_whole, preferred_element_type=jnp.float32)
    resid_one = attended + b_out + tokens.astype(jnp.float32)
    hidden, pull_one = jax.vjp(norm_rows, resid_one, gain_one, shift_one)
    hidden_low = hidden.astype(jnp.bfloat16)
    spread = lax.all_gather(hidden_low, "tensor", axis=0, tiled=True)
    upward = jnp.dot(spread, w_up, preferred_element_type=jnp.float32) + b_up
    active = gelu_exact(upward).astype(jnp.bfloat16)
    row_block = active
    downward = lax.psum_scatter(
        jnp.dot(row_block, w_down, preferred_element_type=jnp.float32).astype(jnp.bfloat16),
        "tensor",
        scatter_dimension=0,
        tiled=True,
    ).astype(jnp.float32)
    resid_two = downward + b_down + hidden
    result, pull_two = jax.vjp(norm_rows, resid_two, gain_two, shift_two)
    layer_out = result.astype(jnp.bfloat16)
    d_resid_two, grad_gain_two, grad_shift_two = pull_two(out_grad.astype(jnp.float32))
    grad_b_down = jnp.sum(d_resid_two, axis=0)
    ffn_rows = lax.all_gather(d_resid_two.astype(jnp.bfloat16), "tensor", axis=0, tiled=True)
    grad_w_down = contract_rows(active, ffn_rows)
    d_active = times_transposed(ffn_rows, w_down)
    gelu_pull = jax.vjp(gelu_exact, upward)[1]
    d_upward = gelu_pull(d_active)[0]
    grad_b_up = jnp.sum(d_upward, axis=0)
    d_up_low = d_upward.astype(jnp.bfloat16)
    grad_w_up = contract_rows(spread, d_up_low)
    row_block = d_up_low
    d_hidden = d_resid_two + lax.psum_scatter(
        times_transposed(row_block, w_up), "tensor", scatter_dimension=0, tiled=True
    )
    d_resid_one, grad_gain_one, grad_shift_one = pull_one(d_hidden)
    grad_b_out = jnp.sum(d_resid_one, axis=0)
    attn_rows = lax.all_gather(d_resid_one.astype(jnp.bfloat16), "tensor", axis=0, tiled=True)
    grad_w_out = contract_rows(context, attn_rows)
    d_context = times_transposed(attn_rows, w_out).astype(jnp.bfloat16)
    d_context = d_context.reshape(seq_count, LEN, heads_here, HEAD_DIM)
    d_projected = lax.map(attend_back, (queries, key_rows, values, d_context, lognorm))
    d_projected = d_projected.reshape(row_total, 3, local_width)
    grad_b_query = jnp.sum(d_projected[:, 0], axis=0)
    grad_b_value = jnp.sum(d_projected[:, 2], axis=0)
    d_proj_low = d_projected.reshape(row_total, 3 * local_width).astype(jnp.bfloat16)
    grad_w_qkv = contract_rows(gathered, d_proj_low).reshape(width, 3, local_width)
    row_block = d_proj_low
    grad_tokens = d_resid_one + lax.psum_scatter(
        times_transposed(row_block, qkv_flat).astype(jnp.bfloat16),
        "tensor",
        scatter_dimension=0,
        tiled=True,
    ).astype(jnp.float32)
    grad_w_qkv, grad_b_query, grad_b_value, grad_w_out, grad_w_up, grad_b_up, grad_w_down = (
        lax.psum(grad_w_qkv.astype(jnp.bfloat16), "dp").astype(jnp.float32),
        lax.psum(grad_b_query.astype(jnp.bfloat16), "dp").astype(jnp.float32),
        lax.psum(grad_b_value.astype(jnp.bfloat16), "dp").astype(jnp.float32),
        lax.psum(grad_w_out.astype(jnp.bfloat16), "dp").astype(jnp.float32),
        lax.psum(grad_w_up.astype(jnp.bfloat16), "dp").astype(jnp.float32),
        lax.psum(grad_b_up.astype(jnp.bfloat16), "dp").astype(jnp.float32),
        lax.psum(grad_w_down.astype(jnp.bfloat16), "dp").astype(jnp.float32),
    )
    grad_gain_one, grad_shift_one, grad_gain_two, grad_shift_two, grad_b_out, grad_b_down = (
        lax.psum(
            (grad_gain_one, grad_shift_one, grad_gain_two, grad_shift_two, grad_b_out, grad_b_down),
            ("dp", "tensor"),
        )
    )
    return (
        layer_out,
        grad_tokens,
        grad_w_qkv,
        grad_b_query,
        grad_b_value,
        grad_w_out,
        grad_b_out,
        grad_gain_one,
        grad_shift_one,
        grad_w_up,
        grad_b_up,
        grad_w_down,
        grad_b_down,
        grad_gain_two,
        grad_shift_two,
    )


def solution(mesh):
    placed = (
        P(("dp", "tensor"), None),
        P(None, None, "tensor"),
        P("tensor"),
        P("tensor"),
        P("tensor", None),
        P(),
        P(),
        P(),
        P(None, "tensor"),
        P("tensor"),
        P("tensor", None),
        P(),
        P(),
        P(),
        P(("dp", "tensor"), None),
    )
    return jax.shard_map(
        body,
        mesh=mesh,
        in_specs=placed,
        out_specs=(
            P(("dp", "tensor"), None),
            P(("dp", "tensor"), None),
            P(None, None, "tensor"),
            P("tensor"),
            P("tensor"),
            P("tensor", None),
            P(),
            P(),
            P(),
            P(None, "tensor"),
            P("tensor"),
            P("tensor", None),
            P(),
            P(),
            P(),
        ),
        check_vma=False,
    )
```

profile of v0, /device:TPU:0, one launch (start us, length us, event | category | flops | bytes accessed | tf_op | source)
XLA Modules:
  0.0 542.7 jit_solution(7314715689492645864)
XLA Ops:
  7.2 0.7 all-gather.6.cloned.1.call-update
  8.0 0.7 all-gather.8.cloned.1.call-update
  8.7 3.2 copy.35
  12.1 21.5 %all-gather.6.cloned.1.call-done = bf16[512,1024]{1,0:T(8,128)(2,1)} async-done(((bf16[256,1024]{1,0:T(8,128)(2,1)}), bf16[512,1024]{1,0:T(8,128)(2,1)}) %all-gather.6.cloned.1.call-update) | async-done | bytes 1048592 | tf_op jit(solution)/shard_map/all_gather | solution.py:112
  33.6 3.1 fusion.24
  36.8 1.3 multiply_reduce_fusion.1
  38.1 1.4 fusion
  39.5 2.0 copy-done
  41.5 2.0 fusion.15
  43.6 0.1 all_to_all.14
  43.8 17.1 %all_to_all.19 = bf16[2,256,512]{1,2,0:T(8,128)(2,1)S(1)} all-to-all(bf16[2,256,512]{1,2,0:T(8,128)(2,1)S(1)} %copy.37), channel_id=1, replica_groups=mesh['dp'=16,'tensor'=2] {'tensor'}, dimensions={0} | all-to-all | bytes 1048576 | tf_op jit(solution)/shard_map/all_to_all | solution.py:119
  60.9 13.0 %all-gather.8.cloned.1.call-done = bf16[1024,1024]{1,0:T(8,128)(2,1)} async-done(((bf16[512,1024]{1,0:T(8,128)(2,1)}), bf16[1024,1024]{1,0:T(8,128)(2,1)}) %all-gather.8.cloned.1.call-update) | async-done | bytes 2097168 | tf_op jit(solution)/shard_map/all_gather | solution.py:118
  73.9 2.4 fusion.48
  76.4 0.3 multiply_reduce_fusion.5
  76.7 1.0 fusion.29
  77.7 0.6 reduce-scatter.4.cloned.1.call-start
  78.3 20.9 %all-gather.10.cloned.1.call-done = bf16[512,1024]{1,0:T(8,128)(2,1)} async-done(((bf16[256,1024]{1,0:T(8,128)(2,1)}), bf16[512,1024]{1,0:T(8,128)(2,1)}) %all-gather.10.cloned.1.call-update) | async-done | bytes 1048592 | tf_op jit(solution)/shard_map/all_gather | solution.py:124
  99.3 15.0 %multiply_convert_fusion.1 = (bf16[512,2048]{1,0:T(8,128)(2,1)S(1)}, f32[512,2048]{1,0:T(8,128)}, f32[512,2048]{1,0:T(8,128)}) fusion(f32[2048]{0:T(1024)S(1)} %copy-done.26, bf16[512,1024]{1,0:T(8,128)(2,1)} %all-gather.10.cloned.1.call-done, bf16[1024,2048]{1,0:T(8,128)(2,1)} %param.23), kind=kOutput, calls=%fused_computation.13 | convolution fusion | flops 2216689664 | bytes 15736832 | tf_op jit(solution)/shard_map/dot_general | solution.py:125
  114.2 1.3 copy-done.28
  115.6 3.3 convolution_convert_fusion.5
  118.9 20.4 %reduce-scatter.4.cloned.1.call-done = bf16[256,1024]{1,0:T(8,128)(2,1)} async-done(((bf16[512,1024]{1,0:T(8,128)(2,1)}), bf16[256,1024]{1,0:T(8,128)(2,1)}) %reduce-scatter.4.cloned.1.call-update) | async-done | bytes 524304 | tf_op jit(solution)/shard_map/reduce_scatter | solution.py:128
  139.4 1.5 fusion.46
  140.9 0.3 multiply_reduce_fusion.4
  141.1 0.4 fusion.19
  141.6 1.3 fusion.45
  142.9 0.9 add_reduce_fusion.1
  143.8 0.2 reduce-scatter.6.cloned.1.call-start
  144.1 21.2 %all-gather.12.cloned.1.call-done = bf16[512,1024]{1,0:T(8,128)(2,1)} async-done(((bf16[256,1024]{1,0:T(8,128)(2,1)}), bf16[512,1024]{1,0:T(8,128)(2,1)}) %all-gather.12.cloned.1.call-update) | async-done | bytes 1048592 | tf_op jit(solution)/shard_map/all_gather | solution.py:139
  165.3 8.8 %fusion.43 = (bf16[2048]{0:T(1024)(128)(2,1)S(1)}, bf16[512,2048]{1,0:T(8,128)(2,1)S(1)}) fusion(f32[512,2048]{1,0:T(8,128)} %get-tuple-element.83, f32[512,2048]{1,0:T(8,128)} %get-tuple-element.93, f32[2048]{0:T(1024)S(1)} %copy-done.26, bf16[512,1024]{1,0:T(8,128)(2,1)} %all-gather.12.cloned.1.call-done, bf16[2048,1024]{1,0:T(8,128)(2,1)} %param.25), kind=kOutput, calls=%fused_computation.96 | convolution fusion | flops 2164258816 | bytes 15740928 | tf_op jit(solution)/shard_map/dot_general | solution.py:31
  174.1 1.3 copy-done.27
  175.4 3.7 fusion.27
  179.2 31.9 %reduce-scatter.6.cloned.1.call-done = f32[256,1024]{1,0:T(8,128)} async-done(((f32[512,1024]{1,0:T(8,128)}), f32[256,1024]{1,0:T(8,128)}) %reduce-scatter.6.cloned.1.call-update) | async-done | bytes 1048592 | tf_op jit(solution)/shard_map/reduce_scatter | solution.py:148
  211.1 1.8 multiply_reduce_fusion.2
  212.9 0.4 fusion.44
  213.3 1.0 add_reduce_fusion
  214.3 0.3 reduce-scatter.8.cloned.1.call-start
  214.6 21.2 %all-gather.14.cloned.1.call-done = bf16[512,1024]{1,0:T(8,128)(2,1)} async-done(((bf16[256,1024]{1,0:T(8,128)(2,1)}), bf16[512,1024]{1,0:T(8,128)(2,1)}) %all-gather.14.cloned.1.call-update) | async-done | bytes 1048592 | tf_op jit(solution)/shard_map/all_gather | solution.py:153
  235.8 2.0 convolution_convert_fusion.6
  237.8 5.2 bitcast_reduce_fusion
  243.0 4.8 multiply_reduce_fusion
  247.9 2.6 multiply_convert_fusion
  250.5 1.4 fusion.13
  251.9 0.9 bitcast_reduce_fusion.1
  252.8 0.2 maximum_convert_fusion
  253.0 0.8 copy-done.6
  253.8 2.8 convolution_convert_fusion.3
  256.6 0.3 all-reduce.5.cloned.1.call-start
  256.9 6.5 %convolution_convert_fusion.1 = bf16[1024,2048]{1,0:T(8,128)(2,1)} fusion(bf16[512,1024]{1,0:T(8,128)(2,1)} %all-gather.10.cloned.1.call-done, bf16[512,2048]{1,0:T(8,128)(2,1)} %copy-done.27), kind=kOutput, calls=%fused_computation.30 | convolution fusion | flops 2149580800 | bytes 7340032 | tf_op jit(solution)/shard_map/dot_general | solution.py:25
  263.3 4.4 convolution_convert_fusion
  267.7 3.5 convolution_convert_fusion.2
  271.2 4.8 copy.41
  276.0 1.7 convolution_convert_fusion.4
  277.7 41.8 %all-reduce = (f32[1024]{0:T(1024)}, f32[1024]{0:T(1024)}, f32[1024]{0:T(1024)}, f32[1024]{0:T(1024)}, f32[1024]{0:T(1024)}, /*index=5*/f32[1024]{0:T(1024)}) all-reduce(f32[1024]{0:T(1024)S(1)} %get-tuple-element.87, f32[1024]{0:T(1024)S(1)} %get-tuple-element.54, ...), channel_id=1, replica_groups=mesh['dp'=16,'tensor'=2] {'dp','tensor'}, use_global_device_ids=true, to_apply=%region_21.22 | all-reduce | flops 6144 | bytes 49152 | tf_op jit(solution)/shard_map/psum | solution.py:180
  319.5 0.1 convert_element_type.163
  319.6 35.1 %all-reduce.1 = (bf16[512]{0:T(512)(128)(2,1)S(1)}, bf16[512]{0:T(512)(128)(2,1)S(1)}, bf16[2048]{0:T(1024)(128)(2,1)S(1)}) all-reduce(bf16[512]{0:T(512)(128)(2,1)S(1)} %convert_element_type.163, bf16[512]{0:T(512)(128)(2,1)S(1)} %convert_element_type.166, ...), channel_id=1, replica_groups=mesh['dp'=16,'tensor'=2] {'dp'}, use_global_device_ids=true, to_apply=%region_16.17 | all-reduce | flops 3072 | bytes 12288 | tf_op jit(solution)/shard_map/psum | solution.py:172
  354.8 0.6 convert_element_type.164
  355.4 0.6 convert_element_type.167
  356.0 0.6 convert_element_type.173
  356.6 2.2 convert_add_fusion
  358.7 161.0 %all-reduce.5.cloned.1.call-done = (bf16[1024,3,512]{2,0,1:T(8,128)(2,1)}, bf16[512,1024]{1,0:T(8,128)(2,1)}, bf16[1024,2048]{1,0:T(8,128)(2,1)}, bf16[2048,1024]{1,0:T(8,128)(2,1)}) async-done(((bf16[1024,3,512]{2,0,1:T(8,128)(2,1)}, bf16[512,1024]{1,0:T(8,128)(2,1)}, bf16[1024,2048]{1,0:T(8,128)(2,1)}, bf16[2048,1024]{1,0:T(8,128)(2,1)}), (bf16[1024,3,512]{2,0,1:T(8,128)(2,1)}, ...) | async-done | bytes 12582928 | tf_op jit(solution)/shard_map/psum | solution.py:171
  519.8 5.6 %convert_element_type.161 = f32[1024,3,512]{2,0,1:T(8,128)} convert(bf16[1024,3,512]{2,0,1:T(8,128)(2,1)} %get-tuple-element.69) | non-fusion elementwise | flops 1572864 | bytes 9437184 | tf_op jit(solution)/shard_map/convert_element_type | solution.py:171
  525.4 1.6 convert_element_type.169
  527.0 4.4 convert_element_type.171
  531.5 4.4 convert_element_type.175
  (87 shorter events, 0.8 us)
Async XLA Ops:
  7.2 4.7 copy-start.19
  7.2 4.8 copy-start.20
  7.2 26.4 %all-gather.6.cloned.1.call-start = ((), (), s32[]{:S(2)}) async-start(), calls=%async_computation.4 | async-start | bytes 1572864 | tf_op jit(solution)/shard_map/all_gather | solution.py:112
  7.9 66.0 %all-gather.8.cloned.1.call-start = ((), (), s32[]{:S(2)}) async-start(), calls=%async_computation.5 | async-start | bytes 3145728 | tf_op jit(solution)/shard_map/all_gather | solution.py:118
  8.7 90.6 %all-gather.10.cloned.1.call-start = ((), (), s32[]{:S(2)}) async-start(), calls=%async_computation.6 | async-start | bytes 1572864 | tf_op jit(solution)/shard_map/all_gather | solution.py:124
  11.9 24.8 %copy-start.5 = (bf16[1024,3,512]{0,2,1:T(8,128)(2,1)}, bf16[1024,3,512]{0,2,1:T(8,128)(2,1)S(1)}, u32[]{:S(2)}) copy-start(bf16[1024,3,512]{0,2,1:T(8,128)(2,1)S(1)} %copy.35) | copy-start | bytes 9437188
  36.8 2.8 copy-start.1
  38.1 3.4 copy-start
  41.5 32.4 %copy-start.7 = (bf16[256,1024]{1,0:T(8,128)(2,1)S(1)}, bf16[256,1024]{1,0:T(8,128)(2,1)}, u32[]{:S(2)}) copy-start(bf16[256,1024]{1,0:T(8,128)(2,1)} %param.15) | copy-start | bytes 1572868
  41.5 32.4 %copy-start.14 = (f32[1024]{0:T(1024)S(1)}, f32[1024]{0:T(1024)}, u32[]{:S(2)}) copy-start(f32[1024]{0:T(1024)} %param.20) | copy-start | bytes 12292
  43.6 30.4 %copy-start.11 = (bf16[8,64,512]{2,1,0:T(8,128)(2,1)}, bf16[8,64,512]{2,1,0:T(8,128)(2,1)S(1)}, u32[]{:S(2)}) copy-start(bf16[8,64,512]{2,1,0:T(8,128)(2,1)S(1)} %fusion.15) | copy-start | bytes 1572868
  43.6 33.1 %copy-start.13 = (f32[1024]{0:T(1024)S(1)}, f32[1024]{0:T(1024)}, u32[]{:S(2)}) copy-start(f32[1024]{0:T(1024)} %param.21) | copy-start | bytes 12292
  43.6 33.0 %copy-start.15 = (f32[1024]{0:T(1024)S(1)}, f32[1024]{0:T(1024)}, u32[]{:S(2)}) copy-start(f32[1024]{0:T(1024)} %param.22) | copy-start | bytes 12292
  43.8 55.4 %copy-start.26 = (f32[2048]{0:T(1024)S(1)}, f32[2048]{0:T(1024)}, u32[]{:S(2)}) copy-start(f32[2048]{0:T(1024)} %param.24) | copy-start | bytes 24580
  77.7 61.6 %reduce-scatter.4.cloned.1.call-start = ((), (), s32[]{:S(2)}) async-start(), calls=%async_computation.7 | async-start | bytes 1572864 | tf_op jit(solution)/shard_map/reduce_scatter | solution.py:128
  99.3 16.3 %copy-start.21 = (bf16[2048,1024]{1,0:T(8,128)(2,1)S(1)}, bf16[2048,1024]{1,0:T(8,128)(2,1)}, u32[]{:S(2)}) copy-start(bf16[2048,1024]{1,0:T(8,128)(2,1)} %param.25) | copy-start | bytes 12582916
  114.2 1.3 copy-start.28
  115.6 23.8 %copy-start.17 = (f32[1024]{0:T(1024)S(1)}, f32[1024]{0:T(1024)}, u32[]{:S(2)}) copy-start(f32[1024]{0:T(1024)} %param.26) | copy-start | bytes 12292
  118.9 22.3 %copy-start.8 = (bf16[256,1024]{1,0:T(8,128)(2,1)S(1)}, bf16[256,1024]{1,0:T(8,128)(2,1)}, u32[]{:S(2)}) copy-start(bf16[256,1024]{1,0:T(8,128)(2,1)} %param.29) | copy-start | bytes 1572868
  118.9 22.3 %copy-start.16 = (f32[1024]{0:T(1024)S(1)}, f32[1024]{0:T(1024)}, u32[]{:S(2)}) copy-start(f32[1024]{0:T(1024)} %param.27) | copy-start | bytes 12292
  118.9 22.7 %copy-start.18 = (f32[1024]{0:T(1024)S(1)}, f32[1024]{0:T(1024)}, u32[]{:S(2)}) copy-start(f32[1024]{0:T(1024)} %param.28) | copy-start | bytes 12292
  118.9 46.4 %all-gather.12.cloned.1.call-start = ((), (), s32[]{:S(2)}) async-start(), calls=%async_computation.8 | async-start | bytes 1572864 | tf_op jit(solution)/shard_map/all_gather | solution.py:139
  143.8 67.3 %reduce-scatter.6.cloned.1.call-start = ((), (), s32[]{:S(2)}) async-start(), calls=%async_computation.9 | async-start | bytes 3145728 | tf_op jit(solution)/shard_map/reduce_scatter | solution.py:148
  165.3 10.1 %copy-start.22 = (bf16[1024,2048]{1,0:T(8,128)(2,1)S(1)}, bf16[1024,2048]{1,0:T(8,128)(2,1)}, u32[]{:S(2)}) copy-start(bf16[1024,2048]{1,0:T(8,128)(2,1)} %param.23) | copy-start | bytes 12582916
  174.1 1.3 copy-start.27
  179.1 56.6 %copy-start.10 = (bf16[512,1024]{1,0:T(8,128)(2,1)S(1)}, bf16[512,1024]{1,0:T(8,128)(2,1)}, u32[]{:S(2)}) copy-start(bf16[512,1024]{1,0:T(8,128)(2,1)} %param.19) | copy-start | bytes 3145732
  179.1 56.6 %all-gather.14.cloned.1.call-start = ((), (), s32[]{:S(2)}) async-start(), calls=%async_computation.10 | async-start | bytes 1572864 | tf_op jit(solution)/shard_map/all_gather | solution.py:153
  214.3 142.3 %reduce-scatter.8.cloned.1.call-start = ((), (), s32[]{:S(2)}) async-start(), calls=%async_computation.11 | async-start | bytes 1572864 | tf_op jit(solution)/shard_map/reduce_scatter | solution.py:164
  237.7 5.2 copy-start.2
  237.8 10.1 %slice-start = ((s8[8388608]{0:T(1024)(128)(4,1)}), s8[4194304]{0:T(1024)(128)(4,1)S(1)}, s32[]{:S(2)}) async-start(s8[8388608]{0:T(1024)(128)(4,1)} %bitcast.90), calls=%async_computation.13 | async-start | bytes 8388608
  243.0 4.9 slice-start.1
  251.9 1.9 copy-start.6
  256.6 263.2 %all-reduce.5.cloned.1.call-start = ((), (), s32[]{:S(2)}) async-start(), calls=%async_computation.12 | async-start | bytes 25165824 | tf_op jit(solution)/shard_map/psum | solution.py:171
  256.9 6.5 %copy-start.24 = (bf16[512,1024]{1,0:T(8,128)(2,1)S(1)}, bf16[512,1024]{1,0:T(8,128)(2,1)}, u32[]{:S(2)}) copy-start(bf16[512,1024]{1,0:T(8,128)(2,1)} %all-gather.12.cloned.1.call-done) | copy-start | bytes 3145732
  256.9 6.5 %copy-start.29 = (bf16[512,2048]{1,0:T(8,128)(2,1)S(1)}, bf16[512,2048]{1,0:T(8,128)(2,1)}, u32[]{:S(2)}) copy-start(bf16[512,2048]{1,0:T(8,128)(2,1)} %copy-done.28) | copy-start | bytes 6291460
  263.3 4.4 copy-start.23
  271.2 4.8 copy-start.12
  271.2 4.8 copy-start.25
  519.8 5.6 %copy-start.9 = (bf16[512,1024]{1,0:T(8,128)(2,1)S(1)}, bf16[512,1024]{1,0:T(8,128)(2,1)}, u32[]{:S(2)}) copy-start(bf16[512,1024]{1,0:T(8,128)(2,1)} %get-tuple-element.70) | copy-start | bytes 3145732
  519.8 7.2 %copy-start.4 = (bf16[1024,2048]{1,0:T(8,128)(2,1)S(1)}, bf16[1024,2048]{1,0:T(8,128)(2,1)}, u32[]{:S(2)}) copy-start(bf16[1024,2048]{1,0:T(8,128)(2,1)} %get-tuple-element.71) | copy-start | bytes 12582916
  527.0 4.5 copy-start.3
Sparse Core Ops, SparseCore 0:
  9.6 23.9 all-gather.5
  35.2 38.7 all-gather.7
  77.8 21.3 all-gather.9
  119.0 20.3 reduce-scatter.3
  144.0 21.2 all-gather.11
  179.2 31.8 reduce-scatter.5
  214.4 21.2 all-gather.13
  256.7 20.3 reduce-scatter.7
  283.4 236.3 all-reduce.4
where the time goes:
time: 549 us; the launch traced here: 543 us
  waiting for transfers between devices  313 us (57%)
  blocking collectives  94 us (17%)
  matrix products  72.8 us (13%)
  other arithmetic  33 us (6%)
  between operations  14.5 us (3%)
  local copies, waits for them, and re-layouts  14 us (3%)
    psum x1, waiting for transfers between devices, body(): lax.psum(grad_w_qkv.astype(jnp.bfloat16), 'dp').astype(jnp.float32)  161 us
    psum x1, blocking collectives, body(): lax.psum((grad_gain_one, grad_shift_one, grad_gain_two, grad_shift_two, g...  41.8 us
    psum x1, blocking collectives, body(): lax.psum(grad_b_query.astype(jnp.bfloat16), 'dp').astype(jnp.float32)  35.1 us
    reduce_scatter x1, waiting for transfers between devices, body(): lax.psum_scatter(times_transposed(row_block, w_up), 'tensor', scatter_dim...  31.9 us
    all_gather x1, waiting for transfers between devices, body(): gathered = lax.all_gather(tokens, 'tensor', axis=0, tiled=True)  21.5 us
    all_gather x1, waiting for transfers between devices, body(): lax.all_gather(d_resid_two.astype(jnp.bfloat16), 'tensor', axis=0, tiled=...  21.2 us
    all_gather x1, waiting for transfers between devices, body(): lax.all_gather(d_resid_one.astype(jnp.bfloat16), 'tensor', axis=0, tiled=...  21.2 us
    all_gather x1, waiting for transfers between devices, body(): spread = lax.all_gather(hidden_low, 'tensor', axis=0, tiled=True)  20.9 us
  transfers between devices with their start and end apart: 9, of which 8 were waited for; matrix products, arithmetic and copies ran while one was open for 7% of the time, Pallas kernels for 0%

commit v1 on v0

--- a/solution.py
+++ b/solution.py
@@ -1,6 +1,8 @@
 import jax
 import jax.numpy as jnp
 from jax import lax
+from jax.experimental import pallas as pl
+from jax.experimental.pallas import tpu as pltpu
 from jax.sharding import PartitionSpec as P
 
 HEAD_DIM = 64
@@ -8,6 +10,8 @@
 
 
 EPSILON = 1e-12
+BF = jnp.bfloat16
+F32 = jnp.float32
 
 
 def norm_rows(resid, gain, shift):
@@ -88,7 +92,7 @@
     return jnp.stack([d_queries, d_keys, d_values], axis=1)
 
 
-def body(
+def general_body(
     tokens,
     w_qkv,
     b_query,
@@ -201,7 +205,864 @@
     )
 
 
+ANY = pl.BlockSpec(memory_space=pl.ANY)
+VMEM_BYTES = 18 << 20
+
+
+def mm(left, right):
+    return jnp.dot(left, right, preferred_element_type=F32)
+
+
+class Chain:
+    def __init__(self):
+        self.last = None
+        self.count = 0
+        self.arrivals = []
+
+    def swap(self, x, axis, pairs):
+        got = lax.ppermute(x, axis, pairs)
+        self.arrivals.append((got, self.count))
+        return got
+
+    def pause(self):
+        self.call(lambda: None, "pause", [], [], work=10**12)
+
+    def call(self, kernel, name, ins, outs, grid=(1,), scalars=None, scratch=(), work=4 * 10**10):
+        arrays = [x for x, _, _ in ins]
+        if any(x is got and count == self.count for x in arrays for got, count in self.arrivals):
+            self.pause()
+        self.count += 1
+        specs = [pl.BlockSpec(block, index) for _, block, index in ins]
+        n_in = len(arrays)
+        extra = [] if self.last is None else [self.last]
+        lead = 0 if scalars is None else 1
+
+        mark = (like((8, 128), F32), (8, 128), lambda *_: (0, 0))
+        n_out = len(outs)
+
+        def run(*refs):
+            head, rest = refs[:lead], refs[lead:]
+            taken, rest = rest[:n_in], rest[n_in + len(extra) :]
+            rest[n_out][...] = jnp.zeros((8, 128), F32)
+            kernel(*head, *taken, *rest[:n_out], *rest[n_out + 1 :])
+
+        *result, self.last = pl.pallas_call(
+            run,
+            grid_spec=pltpu.PrefetchScalarGridSpec(
+                num_scalar_prefetch=lead,
+                grid=grid,
+                in_specs=specs + [ANY] * len(extra),
+                out_specs=[pl.BlockSpec(block, index) for _, block, index in list(outs) + [mark]],
+                scratch_shapes=list(scratch),
+            ),
+            out_shape=[shape for shape, _, _ in list(outs) + [mark]],
+            compiler_params=pltpu.CompilerParams(vmem_limit_bytes=VMEM_BYTES),
+            cost_estimate=pl.CostEstimate(flops=work, bytes_accessed=10**6, transcendentals=0),
+            name=name,
+        )(*([] if scalars is None else [scalars]), *arrays, *extra)
+        return result
+
+
+def like(shape, dtype):
+    return jax.ShapeDtypeStruct(shape, dtype)
+
+
+def in_hbm(x):
+    return pltpu.with_memory_space_constraint(x, pltpu.HBM)
+
+
+def whole(x):
+    zeros = (0,) * len(x.shape)
+    return (x, x.shape, lambda *_: zeros)
+
+
+def rows_of(x, count):
+    return (x, (x.shape[0] // count,) + x.shape[1:], lambda i, *_: (i,) + (0,) * (len(x.shape) - 1))
+
+
+def columns_of(x, width):
+    return (x, (x.shape[0], width), lambda i, *_: (0, i))
+
+
+def project(chain, rows, w_parts, bias):
+    parts, depth, width = w_parts.shape
+
+    def kernel(x, w, b, out):
+        out[0] = (mm(x[...], w[0]) + b[0]).astype(BF)
+
+    part = lambda i: (i, 0, 0)
+    return chain.call(
+        kernel,
+        "project",
+        [whole(rows), (w_parts, (1, depth, width), part), (bias, (1, 1, width), part)],
+        [(like((parts, rows.shape[0], width), BF), (1, rows.shape[0], width), part)],
+        grid=(parts,),
+    )[0]
+
+
+PAIR = 2 * HEAD_DIM
+
+
+def pick_head(shape):
+    return lax.broadcasted_iota(jnp.int32, shape, 1) < HEAD_DIM
+
+
+def attention(chain, mine, first, second, w_out, out_dtype):
+    _, rows, width = mine.shape
+    depth = w_out.shape[1]
+    steps = width // PAIR
+    scale = HEAD_DIM ** (-0.5)
+
+    def kernel(q, k_a, k_b, v_a, v_b, w, ctx, out, total):
+        step = pl.program_id(0)
+        low = pick_head((rows, PAIR))
+        keys = jnp.concatenate([k_a[0], k_b[0]], axis=0)
+        values = jnp.concatenate([v_a[0], v_b[0]], axis=0)
+        found = []
+        for take in (low, jnp.logical_not(low)):
+            query = jnp.where(take, q[0].astype(F32), 0.0).astype(BF)
+            scores = times_transposed(query, keys) * scale
+            raised = jnp.exp(scores - jnp.max(scores, axis=-1, keepdims=True))
+            share = raised * (1.0 / jnp.sum(raised, axis=-1, keepdims=True))
+            found.append(mm(share.astype(BF), values))
+        context = jnp.where(low, found[0], found[1]).astype(BF)
+        ctx[...] = context
+        term = mm(context, w[...])
+
+        @pl.when(step == 0)
+        def _():
+            total[...] = term
+
+        @pl.when(step > 0)
+        def _():
+            total[...] += term
+
+        @pl.when(step == steps - 1)
+        def _():
+            out[...] = total[...].astype(out_dtype)
+
+    def part(p):
+        return lambda i: (p, 0, i)
+
+    block = (1, rows, PAIR)
+    return chain.call(
+        kernel,
+        "attention",
+        [
+            (mine, block, part(0)),
+            (first, block, part(1)),
+            (second, block, part(1)),
+            (first, block, part(2)),
+            (second, block, part(2)),
+            (w_out, (PAIR, depth), lambda i: (i, 0)),
+        ],
+        [
+            (like((rows, width), BF), (rows, PAIR), lambda i: (0, i)),
+            whole(like((rows, depth), out_dtype)),
+        ],
+        grid=(steps,),
+        scratch=[pltpu.VMEM((rows, depth), F32)],
+    )
+
+
+def centre(resid):
+    centred = resid - jnp.mean(resid, axis=-1, keepdims=True)
+    spread = lax.rsqrt(jnp.mean(centred * centred, axis=-1, keepdims=True) + EPSILON)
+    return centred * spread, spread
+
+
+def norm_back(unit, spread, grad):
+    shared = jnp.mean(grad, axis=-1, keepdims=True)
+    along = jnp.mean(grad * unit, axis=-1, keepdims=True)
+    return spread * (grad - shared - unit * along)
+
+
+def three_sums(sums, step, *terms):
+    found = jnp.concatenate([jnp.sum(t, axis=0, keepdims=True) for t in terms], axis=0)
+
+    @pl.when(step == 0)
+    def _():
+        sums[...] = found
+
+    @pl.when(step > 0)
+    def _():
+        sums[...] += found
+
+
+def first_norm(chain, attended, got, tokens, bias, gain, shift):
+    rows, width = tokens.shape
+
+    def kernel(a, g, t, b, gain_, shift_, resid, hidden, low):
+        value = a[...] + g[...].astype(F32) + b[...] + t[...].astype(F32)
+        resid[...] = value
+        unit, _ = centre(value)
+        out = unit * gain_[...] + shift_[...]
+        hidden[...] = out
+        low[...] = out.astype(BF)
+
+    full, half = like((rows, width), F32), like((rows, width), BF)
+    n = 2
+    return chain.call(
+        kernel,
+        "first_norm",
+        [rows_of(attended, n), rows_of(got, n), rows_of(tokens, n), whole(bias), whole(gain), whole(shift)],
+        [rows_of(full, n), rows_of(full, n), rows_of(half, n)],
+        grid=(n,),
+    )
+
+
+def up_and_down(chain, rows, w_up, b_up, w_down, out_dtype):
+    count, width = rows.shape
+    hidden = w_up.shape[1]
+    block = 512
+    steps = hidden // block
+
+    def kernel(x, up, b, down, active, slope, out, total):
+        step = pl.program_id(0)
+        u = mm(x[...], up[...]) + b[...]
+        below = 0.5 * (1.0 + lax.erf(u * (0.5**0.5)))
+        act = (u * below).astype(BF)
+        active[...] = act
+        slope[...] = (below + u * (jnp.exp(-0.5 * u * u) * (0.5 / jnp.pi) ** 0.5)).astype(BF)
+        term = mm(act, down[...])
+
+        @pl.when(step == 0)
+        def _():
+            total[...] = term
+
+        @pl.when(step > 0)
+        def _():
+            total[...] += term
+
+        @pl.when(step == steps - 1)
+        def _():
+            out[...] = total[...].astype(out_dtype)
+
+    return chain.call(
+        kernel,
+        "up_and_down",
+        [
+            whole(rows),
+            columns_of(w_up, block),
+            columns_of(b_up, block),
+            (w_down, (block, width), lambda i: (i, 0)),
+        ],
+        [
+            columns_of(like((count, hidden), BF), block),
+            columns_of(like((count, hidden), BF), block),
+            whole(like((count, width), out_dtype)),
+        ],
+        grid=(steps,),
+        scratch=[pltpu.VMEM((count, width), F32)],
+    )
+
+
+def second_norm(chain, downward, got, bias, hidden, gain, shift, out_grad):
+    rows, width = hidden.shape
+
+    def kernel(d, g, b, h, gain_, shift_, og, layer, d_resid, d_low, sums):
+        unit, spread = centre(d[...] + g[...].astype(F32) + b[...] + h[...])
+        layer[...] = (unit * gain_[...] + shift_[...]).astype(BF)
+        grad = og[...].astype(F32)
+        back = norm_back(unit, spread, grad * gain_[...])
+        d_resid[...] = back
+        d_low[...] = back.astype(BF)
+        three_sums(sums, pl.program_id(0), grad * unit, grad, back)
+
+    full, half = like((rows, width), F32), like((rows, width), BF)
+    n = 2
+    return chain.call(
+        kernel,
+        "second_norm",
+        [rows_of(downward, n), rows_of(got, n), whole(bias), rows_of(hidden, n), whole(gain), whole(shift), rows_of(out_grad, n)],
+        [rows_of(half, n), rows_of(full, n), rows_of(half, n), whole(like((3, width), F32))],
+        grid=(n,),
+    )
+
+
+def down_and_up_back(chain, d_rows, slope, w_down, w_up, out_dtype):
+    count, width = d_rows.shape
+    hidden = slope.shape[1]
+    block = 512
+    steps = hidden // block
+
+    def kernel(d, s, down, up, d_up, sums, out, total):
+        step = pl.program_id(0)
+        grad = times_transposed(d[...], down[...]) * s[...].astype(F32)
+        sums[...] = jnp.sum(grad, axis=0, keepdims=True)
+        low = grad.astype(BF)
+        d_up[...] = low
+        term = times_transposed(low, up[...])
+
+        @pl.when(step == 0)
+        def _():
+            total[...] = term
+
+        @pl.when(step > 0)
+        def _():
+            total[...] += term
+
+        @pl.when(step == steps - 1)
+        def _():
+            out[...] = total[...].astype(out_dtype)
+
+    return chain.call(
+        kernel,
+        "down_and_up_back",
+        [
+            whole(d_rows),
+            columns_of(slope, block),
+            (w_down, (block, width), lambda i: (i, 0)),
+            columns_of(w_up, block),
+        ],
+        [
+            columns_of(like((count, hidden), BF), block),
+            columns_of(like((1, hidden), F32), block),
+            whole(like((count, width), out_dtype)),
+        ],
+        grid=(steps,),
+        scratch=[pltpu.VMEM((count, width), F32)],
+    )
+
+
+def first_norm_back(chain, d_resid, own, got, resid, gain):
+    rows, width = resid.shape
+
+    def kernel(d, o, g, r, gain_, out, low, sums):
+        unit, spread = centre(r[...])
+        grad = d[...] + o[...] + g[...].astype(F32)
+        back = norm_back(unit, spread, grad * gain_[...])
+        out[...] = back
+        low[...] = back.astype(BF)
+        three_sums(sums, pl.program_id(0), grad * unit, grad, back)
+
+    full, half = like((rows, width), F32), like((rows, width), BF)
+    n = 2
+    return chain.call(
+        kernel,
+        "first_norm_back",
+        [rows_of(d_resid, n), rows_of(own, n), rows_of(got, n), rows_of(resid, n), whole(gain)],
+        [rows_of(full, n), rows_of(half, n), whole(like((3, width), F32))],
+        grid=(n,),
+    )
+
+
+def attention_back(chain, first, second, d_first, d_second, w_out):
+    _, rows, width = first.shape
+    depth = w_out.shape[1]
+    scale = HEAD_DIM ** (-0.5)
+
+    def kernel(qa, qb, ka, kb, va, vb, da, db, w, out_a, out_b, sums):
+        keys = jnp.concatenate([ka[0], kb[0]], axis=0)
+        values = jnp.concatenate([va[0], vb[0]], axis=0)
+        low = pick_head((rows, PAIR))
+        both_low = pick_head((2 * rows, PAIR))
+        d_query, d_keys, d_values = [], [], []
+        for q, d in ((qa, da), (qb, db)):
+            d_context = times_transposed(d[...], w[...]).astype(BF)
+            query = q[0]
+            terms = []
+            for take in (low, jnp.logical_not(low)):
+                some = jnp.where(take, query.astype(F32), 0.0).astype(BF)
+                scores = times_transposed(keys, some) * scale
+                raised = jnp.exp(scores - jnp.max(scores, axis=0, keepdims=True))
+                share = raised * (1.0 / jnp.sum(raised, axis=0, keepdims=True))
+                d_some = jnp.where(take, d_context.astype(F32), 0.0).astype(BF)
+                d_share = times_transposed(values, d_some)
+                inner = jnp.sum(share * d_share, axis=0, keepdims=True)
+                d_scores = (share * (d_share - inner)).astype(BF)
+                terms.append(
+                    (
+                        contract_rows(d_scores, keys),
+                        mm(d_scores, query),
+                        mm(share.astype(BF), d_context),
+                    )
+                )
+            d_query.append(jnp.where(low, terms[0][0], terms[1][0]) * scale)
+            d_keys.append(jnp.where(both_low, terms[0][1], terms[1][1]) * scale)
+            d_values.append(jnp.where(both_low, terms[0][2], terms[1][2]))
+        key_grad = d_keys[0] + d_keys[1]
+        value_grad = d_values[0] + d_values[1]
+        for out, query_grad, cut in ((out_a, d_query[0], 0), (out_b, d_query[1], rows)):
+            out[0] = query_grad.astype(BF)
+            out[1] = key_grad[cut : cut + rows].astype(BF)
+            out[2] = value_grad[cut : cut + rows].astype(BF)
+        query_sum = jnp.sum(d_query[0] + d_query[1], axis=0, keepdims=True)
+        sums[...] = jnp.concatenate([query_sum, jnp.sum(value_grad, axis=0, keepdims=True)], axis=0)
+
+    def part(p):
+        return lambda i: (p, 0, i)
+
+    block = (1, rows, PAIR)
+    out = (like((3, rows, width), BF), (3, rows, PAIR), lambda i: (0, 0, i))
+    return chain.call(
+        kernel,
+        "attention_back",
+        [(x, block, part(p)) for p in range(3) for x in (first, second)]
+        + [whole(d_first), whole(d_second), (w_out, (PAIR, depth), lambda i: (i, 0))],
+        [out, out, (like((2, width), F32), (2, PAIR), lambda i: (0, i))],
+        grid=(width // PAIR,),
+    )
+
+
+def to_tokens(chain, d_parts, w_parts, out_dtype, adds=()):
+    parts, rows, width = d_parts.shape
+    depth = w_parts.shape[1]
+
+    def kernel(d, w, *refs):
+        out, total = refs[-2:]
+        step = pl.program_id(0)
+        term = times_transposed(d[0], w[0])
+
+        @pl.when(step == 0)
+        def _():
+            total[...] = term
+
+        @pl.when(step > 0)
+        def _():
+            total[...] += term
+
+        @pl.when(step == parts - 1)
+        def _():
+            value = total[...]
+            for ref in refs[:-2]:
+                value = value + ref[...].astype(F32)
+            out[...] = value.astype(out_dtype)
+
+    part = lambda i: (i, 0, 0)
+    return chain.call(
+        kernel,
+        "to_tokens",
+        [(d_parts, (1, rows, width), part), (w_parts, (1, depth, width), part)]
+        + [whole(x) for x in adds],
+        [whole(like((rows, depth), out_dtype))],
+        grid=(parts,),
+        scratch=[pltpu.VMEM((rows, depth), F32)],
+    )[0]
+
+
+class Dp:
+    SIZE = 16
+
+    def __init__(self, chain):
+        self.chain = chain
+        self.index = lax.axis_index("dp").astype(jnp.int32)
+
+    def bit(self, k):
+        return (self.index >> k) & 1
+
+    def swap(self, x, k):
+        return self.chain.swap(x, "dp", [(i, i ^ (1 << k)) for i in range(self.SIZE)])
+
+    def hop(self, x, got, rows):
+        def kernel(a, b, out):
+            out[...] = a[...]
+            out[:rows, :] += b[:rows, :]
+
+        return self.chain.call(kernel, "hop", [whole(x), whole(got)], [whole(x)])[0]
+
+
+class WeightSum:
+    ORDERS = ((1, 2), (2, 1))
+
+    def __init__(self, dp, ins, product, groups, rows, columns, step):
+        self.dp, self.ins, self.product, self.step = dp, ins, product, step
+        self.groups, self.rows, self.columns = groups, rows, columns
+        self.orders = self.ORDERS
+
+    def multiply(self, core, got, name):
+        dp, rows, groups, columns, step = self.dp, self.rows, self.groups, self.columns, self.step
+        product, n_in = self.product, len(self.ins)
+        n = len(self.orders)
+        count = 2 * n
+        bits = [dp.bit(order[0]) for order in self.orders]
+        place = [2 * i + 1 - bit for i, bit in enumerate(bits)]
+        place += [2 * i + bit for i, bit in enumerate(bits)]
+        per_group = columns // step
+
+        def kernel(places, *refs):
+            left, rest, total = refs[:n_in], refs[n_in:-1], refs[-1]
+            product(left, total)
+            if got is None:
+                rest[0][0] = total[...].astype(BF)
+                return
+            for i in range(count):
+                at = pl.ds(pl.multiple_of(places[1 + i] * rows, rows), rows)
+                rest[1 + i][0] = (total[at, :] + rest[0][0, at, :].astype(F32)).astype(BF)
+
+        def along(height):
+            return (1, height, step), lambda s, places: (s // per_group, 0, s % per_group)
+
+        ins = list(self.ins)
+        all_rows = like((groups, count * rows, columns), BF)
+        if got is None:
+            outs = [(all_rows, *along(count * rows))]
+        else:
+            ins.append((got, *along(count * rows)))
+            outs = [(like((groups, rows, columns), BF), *along(rows))] * count
+        return dp.chain.call(
+            kernel,
+            name,
+            ins,
+            outs,
+            grid=(groups * per_group,),
+            scalars=jnp.stack([core] + place).astype(jnp.int32),
+            scratch=[pltpu.VMEM((count * rows, step), F32)],
+        )
+
+    def begin(self):
+        other = self.multiply(1 - self.dp.bit(0), None, "other_core_rows")[0]
+        self.other_in = self.dp.swap(other, 0)
+
+    def own(self):
+        pieces = self.multiply(self.dp.bit(0), self.other_in, "own_core_rows")
+        n = len(self.orders)
+        self.send, self.keep = pieces[:n], pieces[n:]
+
+    def start(self, level):
+        self.got = [self.dp.swap(x, order[level]) for x, order in zip(self.send, self.orders)]
+
+    def halve(self):
+        groups, rows, columns, n = self.groups, self.rows, self.columns, len(self.orders)
+        half = rows // 2
+        bits = [self.dp.bit(order[1]) for order in self.orders]
+        block = (groups, half, columns)
+
+        def kernel(places, *refs):
+            p = pl.program_id(0)
+            for i in range(n):
+                value = (refs[i][...].astype(F32) + refs[n + i][...].astype(F32)).astype(BF)
+                for step in range(2):
+
+                    @pl.when(p == step)
+                    def _():
+                        refs[2 * n + n * step + i][...] = value
+
+        def half_of(i):
+            return lambda p, places: (0, jnp.where(p == 0, 1 - places[i], places[i]), 0)
+
+        ins = [(x, block, half_of(i)) for i, x in enumerate(self.keep)]
+        ins += [(x, block, half_of(i)) for i, x in enumerate(self.got)]
+        outs = [whole(like(block, BF))] * (2 * n)
+        pieces = self.dp.chain.call(
+            kernel, "halve", ins, outs, grid=(2,), scalars=jnp.stack(bits).astype(jnp.int32)
+        )
+        self.send, self.keep = pieces[:n], pieces[n:]
+        self.start(1)
+
+    def middle(self):
+        groups, columns, n = self.groups, self.columns, len(self.orders)
+        half = self.rows // 2
+
+        def kernel(*refs):
+            for i in range(n):
+                value = refs[i][...].astype(F32) + refs[n + i][...].astype(F32)
+                refs[2 * n][:, i * half : (i + 1) * half, :] = value.astype(BF)
+
+        ins = [whole(x) for x in list(self.keep) + list(self.got)]
+        outs = [whole(like((groups, n * half, columns), BF))]
+        self.held = self.dp.chain.call(kernel, "middle", ins, outs)[0]
+
+    def cross(self):
+        self.crossed = self.dp.swap(self.held, 3)
+
+    def back(self):
+        groups, columns, n = self.groups, self.columns, len(self.orders)
+        half = self.rows // 2
+
+        def kernel(a, b, *outs):
+            for i in range(n):
+                cut = slice(i * half, (i + 1) * half)
+                outs[i][...] = (a[:, cut, :].astype(F32) + b[:, cut, :].astype(F32)).astype(BF)
+
+        outs = [whole(like((groups, half, columns), BF))] * n
+        self.held = self.dp.chain.call(
+            kernel, "back", [whole(self.held), whole(self.crossed)], outs
+        )
+        self.got = [self.dp.swap(x, order[1]) for x, order in zip(self.held, self.orders)]
+
+    def home(self):
+        groups, columns, n = self.groups, self.columns, len(self.orders)
+        half = self.rows // 2
+        bits = [self.dp.bit(order[1]) for order in self.orders]
+
+        def kernel(places, *refs):
+            for i in range(n):
+                at = pl.multiple_of(places[i] * half, half)
+                other = pl.multiple_of((1 - places[i]) * half, half)
+                out, all_out = refs[2 * n + i], refs[3 * n]
+                start = i * 2 * half
+                for source, place in ((refs[i], at), (refs[n + i], other)):
+                    value = source[...]
+                    out[:, pl.ds(place, half), :] = value
+                    all_out[:, pl.ds(pl.multiple_of(start + place, half), half), :] = value
+
+        ins = [whole(x) for x in list(self.held) + list(self.got)]
+        outs = [whole(like((groups, 2 * half, columns), BF))] * n
+        outs.append(whole(like((groups, 2 * n * half, columns), BF)))
+        *self.held, self.all_held = self.dp.chain.call(
+            kernel, "home", ins, outs, scalars=jnp.stack(bits).astype(jnp.int32)
+        )
+        self.got = [self.dp.swap(x, order[0]) for x, order in zip(self.held, self.orders)]
+        self.all_in = self.dp.swap(self.all_held, 0)
+
+    def result(self, shapes, split):
+        dp, n, groups, columns, rows = self.dp, len(self.orders), self.groups, self.columns, self.rows
+        got_in = [dp.swap(x, 0) for x in self.got]
+        core = dp.bit(0)
+        places = []
+        sources = [(self.all_held, 0, core), (self.all_in, 0, 1 - core)]
+        sources += [(got, 1, core) for got in self.got] + [(got, 1, 1 - core) for got in got_in]
+        bits = [dp.bit(order[0]) for order in self.orders]
+        for which in (core, 1 - core):
+            places += [which * 2 * n + 2 * i + bit for i, bit in enumerate(bits)]
+        for which in (core, 1 - core):
+            places += [which * 2 * n + 2 * i + 1 - bit for i, bit in enumerate(bits)]
+        arrays = [self.all_held, self.all_in] + list(self.got) + got_in
+        owners = [i for i in range(2) for _ in range(n)] + list(range(2, 2 + 2 * n))
+        count = len(owners)
+        block = (groups, rows, columns)
+
+        def kernel(places_ref, *refs):
+            step = pl.program_id(0)
+            outs = refs[len(arrays) :]
+            for i in range(len(arrays)):
+                first, last = owners.index(i), count - 1 - owners[::-1].index(i)
+
+                @pl.when(jnp.logical_and(step >= first, step <= last))
+                def _():
+                    for out, found in zip(outs, split(refs[i])):
+                        out[...] = found.astype(F32)
+
+        def piece_map(i):
+            first = owners.index(i)
+            size = owners.count(i)
+            return lambda p, places_ref: (0, jnp.clip(p - first, 0, size - 1), 0)
+
+        return dp.chain.call(
+            kernel,
+            "assemble",
+            [(x, block, piece_map(i)) for i, x in enumerate(arrays)],
+            shapes,
+            grid=(count,),
+            scalars=jnp.stack(places).astype(jnp.int32),
+        )
+
+
+def pair_body(
+    tokens,
+    w_qkv,
+    b_query,
+    b_value,
+    w_out,
+    b_out,
+    gain_one,
+    shift_one,
+    w_up,
+    b_up,
+    w_down,
+    b_down,
+    gain_two,
+    shift_two,
+    out_grad,
+):
+    chain = Chain()
+    dp = Dp(chain)
+
+    def pair_swap(x):
+        return chain.swap(x, "tensor", [(0, 1), (1, 0)])
+
+    own_rows, width = tokens.shape
+    local_width = w_out.shape[0]
+    hidden_width = w_up.shape[1]
+    w_parts = in_hbm(jnp.transpose(w_qkv, (1, 0, 2)))
+    w_out, w_up, w_down = in_hbm(w_out), in_hbm(w_up), in_hbm(w_down)
+    bias = jnp.stack([b_query, jnp.zeros_like(b_query), b_value])[:, None, :]
+    b_out, gain_one, shift_one, b_up, b_down, gain_two, shift_two = (
+        x[None, :] for x in (b_out, gain_one, shift_one, b_up, b_down, gain_two, shift_two)
+    )
+
+    tokens_p = pair_swap(tokens)
+    qkv_o = project(chain, tokens, w_parts, bias)
+    qkv_p = project(chain, tokens_p, w_parts, bias)
+    ctx_p, out_send = attention(chain, qkv_p, qkv_o, qkv_p, w_out, BF)
+    out_got = pair_swap(out_send)
+    ctx_o, out_own = attention(chain, qkv_o, qkv_o, qkv_p, w_out, F32)
+    resid_one, hidden, hidden_o = first_norm(
+        chain, out_own, out_got, tokens, b_out, gain_one, shift_one
+    )
+    hidden_p = pair_swap(hidden_o)
+    active_o, slope_o, down_own = up_and_down(chain, hidden_o, w_up, b_up, w_down, F32)
+    active_p, slope_p, down_send = up_and_down(chain, hidden_p, w_up, b_up, w_down, BF)
+    down_got = pair_swap(down_send)
+    layer_out, d_two, d_two_o, sums_two = second_norm(
+        chain, down_own, down_got, b_down, hidden, gain_two, shift_two, out_grad
+    )
+    d_two_p = pair_swap(d_two_o)
+    d_up_o, b_up_o, dhid_own = down_and_up_back(chain, d_two_o, slope_o, w_down, w_up, F32)
+
+    def core_half(x):
+        return (x, (own_rows, x.shape[1] // 2), lambda s, places: (0, places[0]))
+
+    def columns_at(x, step):
+        return (x, (own_rows, step), lambda s, places: (0, s))
+
+    def plain_product(refs, total):
+        total[...] = contract_rows(refs[0][...], refs[2][...])
+        total[...] += contract_rows(refs[1][...], refs[3][...])
+
+    def plain_sum(left, right, step):
+        ins = [core_half(x) for x in left] + [columns_at(x, step) for x in right]
+        rows, columns = left[0].shape[1], right[0].shape[1]
+        return WeightSum(dp, ins, plain_product, 1, rows // 8, columns, step)
+
+    def plain_result(total, rows, columns):
+        piece = rows // 8
+        shape = pltpu.HBM((1, rows, columns), F32)
+        block = (1, piece, columns)
+        return total.result(
+            [(shape, block, lambda p, places: (0, places[p], 0))], lambda ref: (ref[...],)
+        )[0][0]
+
+    sum_down = plain_sum((active_o, active_p), (d_two_o, d_two_p), 256)
+    sum_down.begin()
+    d_up_p, b_up_p, dhid_send = down_and_up_back(chain, d_two_p, slope_p, w_down, w_up, BF)
+    dhid_got = pair_swap(dhid_send)
+    sum_down.own()
+    sum_down.start(0)
+    sum_up = plain_sum((hidden_o, hidden_p), (d_up_o, d_up_p), 512)
+    sum_up.begin()
+    d_one, d_one_o, sums_one = first_norm_back(
+        chain, d_two, dhid_own, dhid_got, resid_one, gain_one
+    )
+    d_one_p = pair_swap(d_one_o)
+    sum_down.halve()
+    sum_up.own()
+    sum_up.start(0)
+    sum_down.middle()
+    sum_down.cross()
+    d_qkv_o, d_qkv_p, sums_qv = attention_back(chain, qkv_o, qkv_p, d_one_o, d_one_p, w_out)
+    sum_up.halve()
+
+    def rest_product(refs, total):
+        step = pl.program_id(0)
+
+        @pl.when(step < 3)
+        def _():
+            total[...] = contract_rows(refs[0][...], refs[4][0])
+            total[...] += contract_rows(refs[1][...], refs[5][0])
+
+        @pl.when(step == 3)
+        def _():
+            rows = local_width // 2
+            for i in range(2):
+                at = slice(i * rows, (i + 1) * rows)
+                cut = slice(i * local_width, (i + 1) * local_width)
+                total[at, :] = contract_rows(refs[2][...], refs[6][:, cut])
+                total[at, :] += contract_rows(refs[3][...], refs[7][:, cut])
+
+    def part_at(x):
+        return (x, (1,) + x.shape[1:], lambda s, places: (jnp.minimum(s, 2), 0, 0))
+
+    sum_rest = WeightSum(
+        dp,
+        [core_half(tokens), core_half(tokens_p), core_half(ctx_o), core_half(ctx_p)]
+        + [part_at(d_qkv_o), part_at(d_qkv_p), whole(d_one_o), whole(d_one_p)],
+        rest_product,
+        4,
+        width // 8,
+        local_width,
+        local_width,
+    )
+    sum_rest.begin()
+    shared = jnp.concatenate([sums_two, sums_one], axis=0).reshape(-1)
+    small = jnp.concatenate([shared, sums_qv.reshape(-1), (b_up_o + b_up_p).reshape(-1)])
+    small = small.reshape(-1, 128)
+    sum_up.middle()
+    sum_rest.own()
+    sum_rest.start(0)
+    sum_down.back()
+    sum_up.cross()
+    sum_down.home()
+    sum_rest.halve()
+    sum_up.back()
+    sum_rest.middle()
+    sum_rest.cross()
+    tokens_send = to_tokens(chain, d_qkv_p, w_parts, BF)
+    tokens_got = pair_swap(tokens_send)
+    sum_up.home()
+    grad_w_down = plain_result(sum_down, hidden_width, width)
+    small_got = pair_swap(small)
+    grad_tokens = to_tokens(chain, d_qkv_o, w_parts, F32, (d_one, tokens_got))
+    small = dp.hop(small, small_got, shared.shape[0] // 128)
+    small_got = dp.swap(small, 0)
+    sum_rest.back()
+    small = dp.hop(small, small_got, small.shape[0])
+    small_got = dp.swap(small, 1)
+    grad_w_up = plain_result(sum_up, width, hidden_width)
+    small = dp.hop(small, small_got, small.shape[0])
+    small_got = dp.swap(small, 2)
+    sum_rest.home()
+    small = dp.hop(small, small_got, small.shape[0])
+    small_got = dp.swap(small, 3)
+    small = dp.hop(small, small_got, small.shape[0]).reshape(-1)
+    piece = width // 8
+    grad_w_qkv, grad_w_out = sum_rest.result(
+        [
+            (
+                pltpu.HBM((3, width, local_width), F32),
+                (3, piece, local_width),
+                lambda p, places: (0, places[p], 0),
+            ),
+            (
+                pltpu.HBM((local_width, width), F32),
+                (piece, local_width),
+                lambda p, places: (places[p] // 4 * 2 + places[p] % 2, places[p] % 4 // 2),
+            ),
+        ],
+        lambda ref: (ref[0:3], ref[3]),
+    )
+
+    sizes = [width] * 6 + [local_width, local_width, hidden_width]
+    cuts = [sum(sizes[:i]) for i in range(1, len(sizes))]
+    (
+        grad_gain_two,
+        grad_shift_two,
+        grad_b_down,
+        grad_gain_one,
+        grad_shift_one,
+        grad_b_out,
+        grad_b_query,
+        grad_b_value,
+        grad_b_up,
+    ) = jnp.split(small, cuts)
+    return (
+        layer_out,
+        grad_tokens,
+        jnp.transpose(grad_w_qkv, (1, 0, 2)),
+        grad_b_query,
+        grad_b_value,
+        grad_w_out,
+        grad_b_out,
+        grad_gain_one,
+        grad_shift_one,
+        grad_w_up,
+        grad_b_up,
+        grad_w_down,
+        grad_b_down,
+        grad_gain_two,
+        grad_shift_two,
+    )
+
+
 def solution(mesh):
+    paired = mesh.shape["tensor"] == 2 and mesh.shape["dp"] == Dp.SIZE
+
+    def body(*args):
+        if paired and 2 * args[0].shape[0] == LEN:
+            return pair_body(*args)
+        return general_body(*args)
+
     placed = (
         P(("dp", "tensor"), None),
         P(None, None, "tensor"),

time: 549 us -> 312 us (0.57)
  waiting for transfers between devices: 313 us -> 114 us
  Pallas kernels: 0 us -> 140 us
  blocking collectives: 94 us -> 0 us
  matrix products: 72.8 us -> 0 us
  starting transfers between devices: 1.53 us -> 45.3 us
  other arithmetic: 33 us -> 2.07 us
  between operations: 14.5 us -> 1.27 us
  local copies, waits for them, and re-layouts: 14 us -> 7.62 us
    psum x1 -> x0, waiting for transfers between devices: 161 us -> none  [body(): lax.psum(grad_w_qkv.astype(jnp.bfloat16), 'dp').astype(jnp.float32)]
    pallas_call x0 -> x46, Pallas kernels: none -> 140 us  [call(): pl.pallas_call(run, grid_spec=pltpu.PrefetchScalarGridSpec(num_scalar_pre...]
    ppermute x0 -> x52, waiting for transfers between devices: none -> 114 us  [swap(): got = lax.ppermute(x, axis, pairs)]
    all_gather x5 -> x0, waiting for transfers between devices: 97.9 us -> none  [the longest x1 21.5 us: body(): gathered = lax.all_gather(tokens, 'tensor', axis=0, tiled=True)]
    psum x2 -> x0, blocking collectives: 76.9 us -> none  [the longest x1 41.8 us: body(): lax.psum((grad_gain_one, grad_shift_one, grad_gain_two, grad_shift_two, g...]
    dot_general x18 -> x0, matrix products: 72.8 us -> none  [the longest x4 17.2 us: times_transposed(): lax.dot_general(left, right, (((1,), (1,)), ((), ())), preferred_element_...]
    reduce_scatter x3 -> x0, waiting for transfers between devices: 52.4 us -> none  [the longest x1 31.9 us: body(): lax.psum_scatter(times_transposed(row_block, w_up), 'tensor', scatter_dim...]
    ppermute x0 -> x52, starting transfers between devices: none -> 45.3 us  [swap(): got = lax.ppermute(x, axis, pairs)]
  transfers between devices with their start and end apart: 9 -> 52, of which waited for: 8 -> 24; matrix products, arithmetic and copies ran while one was open for 7% -> 2% of each run, Pallas kernels for 0% -> 35%
where the time goes in v1:
time: 312 us; the launch traced here: 310 us
  Pallas kernels  140 us (45%)
  waiting for transfers between devices  114 us (37%)
  starting transfers between devices  45.3 us (15%)
  local copies, waits for them, and re-layouts  7.62 us (2%)
    pallas_call x46, Pallas kernels, call(): pl.pallas_call(run, grid_spec=pltpu.PrefetchScalarGridSpec(num_scalar_pre...  140 us
    ppermute x52, waiting for transfers between devices, swap(): got = lax.ppermute(x, axis, pairs)  114 us
    ppermute x52, starting transfers between devices, swap(): got = lax.ppermute(x, axis, pairs)  45.3 us
  transfers between devices with their start and end apart: 52, of which 24 were waited for; matrix products, arithmetic and copies ran while one was open for 2% of the time, Pallas kernels for 35%

profile of v1, /device:TPU:0, one launch (start us, length us, event | category | flops | bytes accessed | tf_op | source)
XLA Modules:
  0.0 310.4 jit_solution(4526347273476729624)
XLA Ops:
  0.6 3.0 collective-permute-start
  5.6 3.3 %project.2 = (bf16[3,256,512]{2,1,0:T(8,128)(2,1)S(1)}, f32[8,128]{1,0:T(8,128)S(1)}) custom-call(bf16[256,1024]{1,0:T(8,128)(2,1)S(1)} %copy-done.1, bf16[3,1024,512]{2,1,0:T(8,128)(2,1)} %bitcast.66, f32[3,1,512]{2,1,0:T(1,128)S(1)} %broadcast_in_dim.24.refs_2_), custom_call_target="tpu_custom_call" | custom-call | flops 40000000000 | bytes 1000000 | tf_op jit(solution)/shard_map/project/pallas_call | solution.py:249
  9.3 6.5 %collective-permute-done.refs_0_.refs_2_ = bf16[256,1024]{1,0:T(8,128)(2,1)S(1)} collective-permute-done((bf16[256,1024]{1,0:T(8,128)(2,1)}, bf16[256,1024]{1,0:T(8,128)(2,1)S(1)}, u32[]{:S(2)}, u32[]{:S(2)}) %collective-permute-start) | collective-permute-done | bytes 524320 | tf_op jit(solution)/shard_map/ppermute | solution.py:223
  15.8 3.5 %project.3 = (bf16[3,256,512]{2,1,0:T(8,128)(2,1)S(1)}, f32[8,128]{1,0:T(8,128)S(1)}) custom-call(bf16[256,1024]{1,0:T(8,128)(2,1)S(1)} %collective-permute-done.refs_0_.refs_2_, bf16[3,1024,512]{2,1,0:T(8,128)(2,1)} %bitcast.67, f32[3,1,512]{2,1,0:T(1,128)S(1)} %broadcast_in_dim.24.refs_2_, f32[8,128]{1,0:T(8,128)S(1)} %get-tuple-element.142.refs_3_), custom_call_target="tpu_custom_call" | custom-call | flops 40000000000 | bytes 1000000 | tf_op jit(solution)/shard_map/project/pallas_call | solution.py:249
  19.4 6.7 %attention.2 = (bf16[256,512]{1,0:T(8,128)(2,1)S(1)}, bf16[256,1024]{1,0:T(8,128)(2,1)S(1)}, f32[8,128]{1,0:T(8,128)S(1)}) custom-call(bf16[3,256,512]{2,1,0:T(8,128)(2,1)S(1)} %get-tuple-element.143.refs_0_.refs_2_.refs_4_.refs_1_.refs_3_.refs_5_, bf16[3,256,512]{2,1,0:T(8,128)(2,1)S(1)} %get-tuple-element.141.refs_1_.refs_3_.refs_0_.refs_2_.refs_4_, ...), custom_call_target="tpu_custom_call" | custom-call | flops 40000000000 | bytes 1000000 | tf_op jit(solution)/shard_map/attention/pallas_call | solution.py:249
  26.1 1.8 collective-permute-start.1
  27.9 6.6 %attention.3 = (bf16[256,512]{1,0:T(8,128)(2,1)S(1)}, f32[256,1024]{1,0:T(8,128)S(1)}, f32[8,128]{1,0:T(8,128)S(1)}) custom-call(bf16[3,256,512]{2,1,0:T(8,128)(2,1)S(1)} %get-tuple-element.141.refs_1_.refs_3_.refs_0_.refs_2_.refs_4_, bf16[3,256,512]{2,1,0:T(8,128)(2,1)S(1)} %get-tuple-element.141.refs_1_.refs_3_.refs_0_.refs_2_.refs_4_, ...), custom_call_target="tpu_custom_call" | custom-call | flops 40000000000 | bytes 1000000 | tf_op jit(solution)/shard_map/attention/pallas_call | solution.py:249
  34.6 4.7 %collective-permute-done.1.refs_1_ = bf16[256,1024]{1,0:T(8,128)(2,1)S(1)} collective-permute-done((bf16[256,1024]{1,0:T(8,128)(2,1)S(1)}, bf16[256,1024]{1,0:T(8,128)(2,1)S(1)}, u32[]{:S(2)}, u32[]{:S(2)}) %collective-permute-start.1) | collective-permute-done | bytes 524320 | tf_op jit(solution)/shard_map/ppermute | solution.py:223
  40.0 1.5 collective-permute-start.2
  41.4 6.5 %up_and_down.2 = (bf16[256,2048]{1,0:T(8,128)(2,1)S(1)}, bf16[256,2048]{1,0:T(8,128)(2,1)S(1)}, f32[256,1024]{1,0:T(8,128)S(1)}, f32[8,128]{1,0:T(8,128)S(1)}) custom-call(bf16[256,1024]{1,0:T(8,128)(2,1)S(1)} %get-tuple-element.149.refs_0_.refs_1_, bf16[1024,2048]{1,0:T(8,128)(2,1)} %refs_3_.7, f32[1,2048]{1,0:T(1,128)S(1)} %bitcast.53, ...), custom_call_target="tpu_custom_call" | custom-call | flops 40000000000 | bytes 1000000 | tf_op jit(solution)/shard_map/up_and_down/pallas_call | solution.py:249
  47.9 4.3 %collective-permute-done.2.refs_0_.refs_2_ = bf16[256,1024]{1,0:T(8,128)(2,1)S(1)} collective-permute-done((bf16[256,1024]{1,0:T(8,128)(2,1)S(1)}, bf16[256,1024]{1,0:T(8,128)(2,1)S(1)}, u32[]{:S(2)}, u32[]{:S(2)}) %collective-permute-start.2) | collective-permute-done | bytes 524320 | tf_op jit(solution)/shard_map/ppermute | solution.py:223
  52.2 7.4 %up_and_down.3 = (bf16[256,2048]{1,0:T(8,128)(2,1)S(1)}, bf16[256,2048]{1,0:T(8,128)(2,1)S(1)}, bf16[256,1024]{1,0:T(8,128)(2,1)}, f32[8,128]{1,0:T(8,128)S(1)}) custom-call(bf16[256,1024]{1,0:T(8,128)(2,1)S(1)} %collective-permute-done.2.refs_0_.refs_2_, bf16[1024,2048]{1,0:T(8,128)(2,1)} %refs_3_.7, f32[1,2048]{1,0:T(1,128)S(1)} %bitcast.54, ...), custom_call_target="tpu_custom_call" | custom-call | flops 40000000000 | bytes 1000000 | tf_op jit(solution)/shard_map/up_and_down/pallas_call | solution.py:249
  59.6 1.1 collective-permute-start.3
  60.8 10.4 %collective-permute-done.3.refs_1_ = bf16[256,1024]{1,0:T(8,128)(2,1)} collective-permute-done((bf16[256,1024]{1,0:T(8,128)(2,1)}, bf16[256,1024]{1,0:T(8,128)(2,1)}, u32[]{:S(2)}, u32[]{:S(2)}) %collective-permute-start.3) | collective-permute-done | bytes 524320 | tf_op jit(solution)/shard_map/ppermute | solution.py:223
  71.2 2.7 second_norm.1
  74.8 6.2 %down_and_up_back.2 = (bf16[256,2048]{1,0:T(8,128)(2,1)S(1)}, f32[1,2048]{1,0:T(1,128)S(1)}, f32[256,1024]{1,0:T(8,128)S(1)}, f32[8,128]{1,0:T(8,128)S(1)}) custom-call(bf16[256,1024]{1,0:T(8,128)(2,1)S(1)} %get-tuple-element.158.refs_0_.refs_3_, bf16[256,2048]{1,0:T(8,128)(2,1)S(1)} %get-tuple-element.159.refs_1_, bf16[2048,1024]{1,0:T(8,128)(2,1)} %refs_2_.5, ...), custom_call_target="tpu_custom_call" | custom-call | flops 40000000000 | bytes 1000000 | tf_op jit(solution)/shard_map/down_and_up_back/pallas_call | solution.py:249
  81.0 3.3 %collective-permute-done.4.refs_4_.refs_0_ = bf16[256,1024]{1,0:T(8,128)(2,1)S(1)} collective-permute-done((bf16[256,1024]{1,0:T(8,128)(2,1)S(1)}, bf16[256,1024]{1,0:T(8,128)(2,1)S(1)}, u32[]{:S(2)}, u32[]{:S(2)}) %collective-permute-start.4) | collective-permute-done | bytes 524320 | tf_op jit(solution)/shard_map/ppermute | solution.py:223
  84.3 3.3 %other_core_rows.3 = (bf16[1,1024,1024]{2,1,0:T(8,128)(2,1)S(1)}, f32[8,128]{1,0:T(8,128)S(1)}) custom-call(s32[5]{0:T(128)S(1)} %stack.52.refs_0_, bf16[256,2048]{1,0:T(8,128)(2,1)S(1)} %get-tuple-element.163.refs_1_, bf16[256,2048]{1,0:T(8,128)(2,1)S(1)} %get-tuple-element.164.refs_2_, bf16[256,1024]{1,0:T(8,128)(2,1)S(1)} %get-tuple-element.158.refs_0_.refs_3_, ...), custom_call_target="tpu_custom_call" | custom-call | flops 40000000000 | bytes 1000000 | tf_op jit(solution)/shard_map/other_core_rows/pallas_call | solution.py:249
  87.7 6.2 %down_and_up_back.3 = (bf16[256,2048]{1,0:T(8,128)(2,1)S(1)}, f32[1,2048]{1,0:T(1,128)S(1)}, bf16[256,1024]{1,0:T(8,128)(2,1)S(1)}, f32[8,128]{1,0:T(8,128)S(1)}) custom-call(bf16[256,1024]{1,0:T(8,128)(2,1)S(1)} %collective-permute-done.4.refs_4_.refs_0_, bf16[256,2048]{1,0:T(8,128)(2,1)S(1)} %get-tuple-element.162.refs_1_, bf16[2048,1024]{1,0:T(8,128)(2,1)} %refs_2_.5, ...), custom_call_target="tpu_custom_call" | custom-call | flops 40000000000 | bytes 1000000 | tf_op jit(solution)/shard_map/down_and_up_back/pallas_call | solution.py:249
  95.1 4.4 %own_core_rows.3 = (bf16[1,256,1024]{2,1,0:T(8,128)(2,1)}, bf16[1,256,1024]{2,1,0:T(8,128)(2,1)}, bf16[1,256,1024]{2,1,0:T(8,128)(2,1)S(1)}, bf16[1,256,1024]{2,1,0:T(8,128)(2,1)S(1)}, f32[8,128]{1,0:T(8,128)S(1)}) custom-call(s32[5]{0:T(128)S(1)} %stack.54.refs_0_, bf16[256,2048]{1,0:T(8,128)(2,1)S(1)} %get-tuple-element.163.refs_1_, ...), custom_call_target="tpu_custom_call" | custom-call | flops 40000000000 | bytes 1000000 | tf_op jit(solution)/shard_map/own_core_rows/pallas_call | solution.py:249
  99.5 1.5 collective-permute-start.8
  101.0 1.5 collective-permute-start.9
  102.5 3.0 other_core_rows.4
  105.5 2.7 collective-permute-done.5.refs_2_
  111.4 2.5 collective-permute-done.8.refs_3_
  113.9 1.2 collective-permute-done.9.refs_4_
  117.1 2.3 halve.3
  119.5 1.6 collective-permute-start.10
  121.7 3.9 %own_core_rows.4 = (bf16[1,128,2048]{2,1,0:T(8,128)(2,1)S(1)}, bf16[1,128,2048]{2,1,0:T(8,128)(2,1)S(1)}, bf16[1,128,2048]{2,1,0:T(8,128)(2,1)S(1)}, bf16[1,128,2048]{2,1,0:T(8,128)(2,1)S(1)}, f32[8,128]{1,0:T(8,128)S(1)}) custom-call(s32[5]{0:T(128)S(1)} %stack.54.refs_0_, bf16[256,1024]{1,0:T(8,128)(2,1)S(1)} %copy-done.7, ...), custom_call_target="tpu_custom_call" | custom-call | flops 40000000000 | bytes 1000000 | tf_op jit(solution)/shard_map/own_core_rows/pallas_call | solution.py:249
  125.6 1.5 collective-permute-start.13
  127.6 1.7 collective-permute-done.11.refs_3_
  130.9 15.4 %attention_back.1 = (bf16[3,256,512]{2,1,0:T(8,128)(2,1)S(1)}, bf16[3,256,512]{2,1,0:T(8,128)(2,1)S(1)}, f32[2,512]{1,0:T(2,128)S(1)}, f32[8,128]{1,0:T(8,128)S(1)}) custom-call(bf16[3,256,512]{2,1,0:T(8,128)(2,1)S(1)} %copy-done.26, bf16[3,256,512]{2,1,0:T(8,128)(2,1)S(1)} %copy-done.28, bf16[3,256,512]{2,1,0:T(8,128)(2,1)S(1)} %copy-done.26, ...), custom_call_target="tpu_custom_call" | custom-call | flops 40000000000 | bytes 1000000 | tf_op jit(solution)/shard_map/attention_back/pallas_call | solution.py:249
  147.4 2.7 collective-permute-start.20
  151.8 2.8 other_core_rows.5
  154.7 9.4 %collective-permute-done.16.refs_2_ = bf16[1,64,2048]{2,1,0:T(8,128)(2,1)S(1)} collective-permute-done((bf16[1,64,2048]{2,1,0:T(8,128)(2,1)S(1)}, bf16[1,64,2048]{2,1,0:T(8,128)(2,1)S(1)}, u32[]{:S(2)}, u32[]{:S(2)}) %collective-permute-start.16) | collective-permute-done | bytes 262176 | tf_op jit(solution)/shard_map/ppermute | solution.py:223
  165.0 1.6 collective-permute-start.25
  166.6 3.1 own_core_rows.5
  169.6 12.5 %collective-permute-done.20.refs_1_ = bf16[1,256,1024]{2,1,0:T(8,128)(2,1)} collective-permute-done((bf16[1,256,1024]{2,1,0:T(8,128)(2,1)}, bf16[1,256,1024]{2,1,0:T(8,128)(2,1)}, u32[]{:S(2)}, u32[]{:S(2)}) %collective-permute-start.20) | collective-permute-done | bytes 524320 | tf_op jit(solution)/shard_map/ppermute | solution.py:223
  182.1 2.1 back.3
  185.1 1.3 collective-permute-start.18
  186.4 11.9 %collective-permute-done.21.refs_3_ = bf16[1,128,1024]{2,1,0:T(8,128)(2,1)} collective-permute-done((bf16[1,128,1024]{2,1,0:T(8,128)(2,1)}, bf16[1,128,1024]{2,1,0:T(8,128)(2,1)}, u32[]{:S(2)}, u32[]{:S(2)}) %collective-permute-start.21) | collective-permute-done | bytes 262176 | tf_op jit(solution)/shard_map/ppermute | solution.py:223
  198.3 3.1 %home.3 = (bf16[1,256,1024]{2,1,0:T(8,128)(2,1)}, bf16[1,256,1024]{2,1,0:T(8,128)(2,1)}, bf16[1,512,1024]{2,1,0:T(8,128)(2,1)}, f32[8,128]{1,0:T(8,128)S(1)}) custom-call(s32[2]{0:T(128)S(1)} %pad_add_fusion.refs_0_, bf16[1,128,1024]{2,1,0:T(8,128)(2,1)} %get-tuple-element.213.refs_1_, bf16[1,128,1024]{2,1,0:T(8,128)(2,1)} %get-tuple-element.214.refs_2_, ...), custom_call_target="tpu_custom_call" | custom-call | flops 40000000000 | bytes 1000000 | tf_op jit(solution)/shard_map/home/pallas_call | solution.py:249
  202.8 1.7 collective-permute-start.29
  204.5 8.6 %collective-permute-done.19.refs_4_ = bf16[4,128,512]{2,1,0:T(8,128)(2,1)S(1)} collective-permute-done((bf16[4,128,512]{2,1,0:T(8,128)(2,1)S(1)}, bf16[4,128,512]{2,1,0:T(8,128)(2,1)S(1)}, u32[]{:S(2)}, u32[]{:S(2)}) %collective-permute-start.19) | collective-permute-done | bytes 524320 | tf_op jit(solution)/shard_map/ppermute | solution.py:223
  213.1 1.3 halve.5
  215.6 1.3 back.4
  216.9 12.1 %collective-permute-done.23.refs_2_ = bf16[4,64,512]{2,1,0:T(8,128)(2,1)S(1)} collective-permute-done((bf16[4,64,512]{2,1,0:T(8,128)(2,1)S(1)}, bf16[4,64,512]{2,1,0:T(8,128)(2,1)S(1)}, u32[]{:S(2)}, u32[]{:S(2)}) %collective-permute-start.23) | collective-permute-done | bytes 262176 | tf_op jit(solution)/shard_map/ppermute | solution.py:223
  230.4 4.4 %to_tokens.2 = (bf16[256,1024]{1,0:T(8,128)(2,1)}, f32[8,128]{1,0:T(8,128)S(1)}) custom-call(bf16[3,256,512]{2,1,0:T(8,128)(2,1)S(1)} %get-tuple-element.191.refs_6_.refs_0_, bf16[3,1024,512]{2,1,0:T(8,128)(2,1)} %bitcast.68, f32[8,128]{1,0:T(8,128)S(1)} %get-tuple-element.224.refs_2_), custom_call_target="tpu_custom_call" | custom-call | flops 40000000000 | bytes 1000000 | tf_op jit(solution)/shard_map/to_tokens/pallas_call | solution.py:249
  234.9 1.5 collective-permute-done.32.refs_3_
  236.7 1.4 collective-permute-start.26
  238.6 2.0 home.4
  240.6 3.2 %collective-permute-start.34 = (bf16[4,128,512]{2,1,0:T(8,128)(2,1)S(1)}, bf16[4,128,512]{2,1,0:T(8,128)(2,1)S(1)}, u32[]{:S(2)}, u32[]{:S(2)}) collective-permute-start(bf16[4,128,512]{2,1,0:T(8,128)(2,1)S(1)} %get-tuple-element.235.refs_0_), channel_id=1, source_target_pairs={{0,16},{2,18},{4,20},{6,22},{8,24},{10,26},{12,28},{14,30},{16,0},... | collective-permute-start | bytes 1572872 | tf_op jit(solution)/shard_map/ppermute | solution.py:223
  245.0 7.8 %assemble.3 = (f32[1,2048,1024]{2,1,0:T(8,128)}, f32[8,128]{1,0:T(8,128)S(1)}) custom-call(s32[8]{0:T(128)S(1)} %stack.65.refs_0_, bf16[1,512,1024]{2,1,0:T(8,128)(2,1)} %get-tuple-element.226.refs_1_, bf16[1,512,1024]{2,1,0:T(8,128)(2,1)} %collective-permute-done.27.refs_2_, bf16[1,256,1024]{2,1,0:T(8,128)(2,1)} %collective-permute-done.28.refs_3_, ...), custom_call_target="tpu_custom_call" | custom-call | flops 40000000000 | bytes 1000000 | tf_op jit(solution)/shard_map/assemble/pallas_call | solution.py:249
  252.9 4.8 %to_tokens.3 = (f32[256,1024]{1,0:T(8,128)}, f32[8,128]{1,0:T(8,128)S(1)}) custom-call(bf16[3,256,512]{2,1,0:T(8,128)(2,1)S(1)} %get-tuple-element.189.refs_5_.refs_0_, bf16[3,1024,512]{2,1,0:T(8,128)(2,1)} %bitcast.69, f32[256,1024]{1,0:T(8,128)S(1)} %copy-done.24, bf16[256,1024]{1,0:T(8,128)(2,1)} %collective-permute-done.26.refs_3_, ...), custom_call_target="tpu_custom_call" | custom-call | flops 40000000000 | bytes 1000000 | tf_op jit(solution)/shard_map/to_tokens/pallas_call | solution.py:249
  258.9 8.3 %collective-permute-done.34.refs_1_ = bf16[4,128,512]{2,1,0:T(8,128)(2,1)S(1)} collective-permute-done((bf16[4,128,512]{2,1,0:T(8,128)(2,1)S(1)}, bf16[4,128,512]{2,1,0:T(8,128)(2,1)S(1)}, u32[]{:S(2)}, u32[]{:S(2)}) %collective-permute-start.34) | collective-permute-done | bytes 524320 | tf_op jit(solution)/shard_map/ppermute | solution.py:223
  269.4 1.4 collective-permute-start.39
  271.8 7.8 %assemble.4 = (f32[1,1024,2048]{2,1,0:T(8,128)}, f32[8,128]{1,0:T(8,128)S(1)}) custom-call(s32[8]{0:T(128)S(1)} %stack.65.refs_0_, bf16[1,256,2048]{2,1,0:T(8,128)(2,1)} %get-tuple-element.248.refs_1_, bf16[1,256,2048]{2,1,0:T(8,128)(2,1)} %collective-permute-done.40.refs_2_, bf16[1,128,2048]{2,1,0:T(8,128)(2,1)} %collective-permute-done.41.refs_3_, ...), custom_call_target="tpu_custom_call" | custom-call | flops 40000000000 | bytes 1000000 | tf_op jit(solution)/shard_map/assemble/pallas_call | solution.py:249
  279.6 2.0 collective-permute-start.50
  281.7 3.1 %home.5 = (bf16[4,128,512]{2,1,0:T(8,128)(2,1)}, bf16[4,128,512]{2,1,0:T(8,128)(2,1)}, bf16[4,256,512]{2,1,0:T(8,128)(2,1)}, f32[8,128]{1,0:T(8,128)S(1)}) custom-call(s32[2]{0:T(128)S(1)} %pad_add_fusion.refs_0_, bf16[4,64,512]{2,1,0:T(8,128)(2,1)} %get-tuple-element.243.refs_1_, bf16[4,64,512]{2,1,0:T(8,128)(2,1)} %get-tuple-element.244.refs_2_, ...), custom_call_target="tpu_custom_call" | custom-call | flops 40000000000 | bytes 1000000 | tf_op jit(solution)/shard_map/home/pallas_call | solution.py:249
  284.8 1.4 collective-permute-start.46
  286.9 3.1 %collective-permute-start.51 = (f32[72,128]{1,0:T(8,128)}, f32[72,128]{1,0:T(8,128)}, u32[]{:S(2)}, u32[]{:S(2)}) collective-permute-start(f32[72,128]{1,0:T(8,128)} %get-tuple-element.259.refs_0_), channel_id=1, source_target_pairs={{0,16},{2,18},{4,20},{6,22},{8,24},{10,26},{12,28},{14,30},{16,0},... | collective-permute-start | bytes 110600 | tf_op jit(solution)/shard_map/ppermute | solution.py:223
  290.0 8.6 %collective-permute-done.51.refs_1_ = f32[72,128]{1,0:T(8,128)} collective-permute-done((f32[72,128]{1,0:T(8,128)}, f32[72,128]{1,0:T(8,128)}, u32[]{:S(2)}, u32[]{:S(2)}) %collective-permute-start.51) | collective-permute-done | bytes 36896 | tf_op jit(solution)/shard_map/ppermute | solution.py:223
  299.5 1.3 collective-permute-done.47.refs_4_
  302.9 7.4 %assemble.5 = (f32[3,1024,512]{2,1,0:T(8,128)}, f32[512,1024]{1,0:T(8,128)}, f32[8,128]{1,0:T(8,128)}) custom-call(s32[8]{0:T(128)S(1)} %stack.65.refs_0_, bf16[4,256,512]{2,1,0:T(8,128)(2,1)} %get-tuple-element.254.refs_1_, bf16[4,256,512]{2,1,0:T(8,128)(2,1)} %collective-permute-done.45.refs_2_, bf16[4,128,512]{2,1,0:T(8,128)(2,1)} %collective-permute-done.46.refs_3_, ...), custom_call_target="tpu_custom_call" | custom-call | flops 40000000000 | bytes 1000000 | tf_op jit(solution)/shard_map/assemble/pallas_call | solution.py:249
  (175 shorter events, 31.6 us)
Async XLA Ops:
  0.6 15.2 %collective-permute-start = (bf16[256,1024]{1,0:T(8,128)(2,1)}, bf16[256,1024]{1,0:T(8,128)(2,1)S(1)}, u32[]{:S(2)}, u32[]{:S(2)}) collective-permute-start(bf16[256,1024]{1,0:T(8,128)(2,1)} %refs_1_.7), channel_id=1, source_target_pairs={{0,1},{1,0},{2,3},{3,2},{4,5},{5,4},{6,7},{7,6},{8,9},{9,8},{10,11... | collective-permute-start | bytes 1572872 | tf_op jit(solution)/shard_map/ppermute | solution.py:223
  8.9 19.0 %copy-start.25 = (bf16[3,256,512]{2,1,0:T(8,128)(2,1)}, bf16[3,256,512]{2,1,0:T(8,128)(2,1)S(1)}, u32[]{:S(2)}) copy-start(bf16[3,256,512]{2,1,0:T(8,128)(2,1)S(1)} %get-tuple-element.141.refs_1_.refs_3_.refs_0_.refs_2_.refs_4_) | copy-start | bytes 2359300
  26.1 13.2 %collective-permute-start.1 = (bf16[256,1024]{1,0:T(8,128)(2,1)S(1)}, bf16[256,1024]{1,0:T(8,128)(2,1)S(1)}, u32[]{:S(2)}, u32[]{:S(2)}) collective-permute-start(bf16[256,1024]{1,0:T(8,128)(2,1)S(1)} %get-tuple-element.147), channel_id=1, source_target_pairs={{0,1},{1,0},{2,3},{3,2},{4,5},{5,4},{6,7},{7,6},{8,9},{9,8},{10,11... | collective-permute-start | bytes 1572872 | tf_op jit(solution)/shard_map/ppermute | solution.py:223
  27.9 11.4 %copy-start.2 = (bf16[256,1024]{1,0:T(8,128)(2,1)S(1)}, bf16[256,1024]{1,0:T(8,128)(2,1)}, u32[]{:S(2)}) copy-start(bf16[256,1024]{1,0:T(8,128)(2,1)} %refs_1_.7) | copy-start | bytes 1572868
  27.9 11.4 %copy-start.12 = (f32[1024]{0:T(1024)S(1)}, f32[1024]{0:T(1024)}, u32[]{:S(2)}) copy-start(f32[1024]{0:T(1024)} %param.20) | copy-start | bytes 12292
  27.9 11.4 %copy-start.13 = (f32[1024]{0:T(1024)S(1)}, f32[1024]{0:T(1024)}, u32[]{:S(2)}) copy-start(f32[1024]{0:T(1024)} %param.22) | copy-start | bytes 12292
  27.9 11.4 %copy-start.17 = (f32[1024]{0:T(1024)S(1)}, f32[1024]{0:T(1024)}, u32[]{:S(2)}) copy-start(f32[1024]{0:T(1024)} %param.21) | copy-start | bytes 12292
  40.0 12.3 %collective-permute-start.2 = (bf16[256,1024]{1,0:T(8,128)(2,1)S(1)}, bf16[256,1024]{1,0:T(8,128)(2,1)S(1)}, u32[]{:S(2)}, u32[]{:S(2)}) collective-permute-start(bf16[256,1024]{1,0:T(8,128)(2,1)S(1)} %get-tuple-element.149.refs_0_.refs_1_), channel_id=1, source_target_pairs={{0,1},{1,0},{2,3},{3,2},{4,5},{5,4},{6,7},{7,6},{8,9},{9,8},{10,11... | collective-permute-start | bytes 1572872 | tf_op jit(solution)/shard_map/ppermute | solution.py:223
  59.6 11.6 %collective-permute-start.3 = (bf16[256,1024]{1,0:T(8,128)(2,1)}, bf16[256,1024]{1,0:T(8,128)(2,1)}, u32[]{:S(2)}, u32[]{:S(2)}) collective-permute-start(bf16[256,1024]{1,0:T(8,128)(2,1)} %get-tuple-element.153), channel_id=1, source_target_pairs={{0,1},{1,0},{2,3},{3,2},{4,5},{5,4},{6,7},{7,6},{8,9},{9,8},{10,11... | collective-permute-start | bytes 1572872 | tf_op jit(solution)/shard_map/ppermute | solution.py:223
  60.7 10.5 %copy-start = (bf16[256,1024]{1,0:T(8,128)(2,1)S(1)}, bf16[256,1024]{1,0:T(8,128)(2,1)}, u32[]{:S(2)}) copy-start(bf16[256,1024]{1,0:T(8,128)(2,1)} %refs_6_.1) | copy-start | bytes 1572868
  60.7 10.5 %copy-start.14 = (f32[1024]{0:T(1024)S(1)}, f32[1024]{0:T(1024)}, u32[]{:S(2)}) copy-start(f32[1024]{0:T(1024)} %param.26) | copy-start | bytes 12292
  60.7 10.5 %copy-start.15 = (f32[1024]{0:T(1024)S(1)}, f32[1024]{0:T(1024)}, u32[]{:S(2)}) copy-start(f32[1024]{0:T(1024)} %param.27) | copy-start | bytes 12292
  60.8 10.5 %copy-start.16 = (f32[1024]{0:T(1024)S(1)}, f32[1024]{0:T(1024)}, u32[]{:S(2)}) copy-start(f32[1024]{0:T(1024)} %param.28) | copy-start | bytes 12292
  74.0 10.3 %collective-permute-start.4 = (bf16[256,1024]{1,0:T(8,128)(2,1)S(1)}, bf16[256,1024]{1,0:T(8,128)(2,1)S(1)}, u32[]{:S(2)}, u32[]{:S(2)}) collective-permute-start(bf16[256,1024]{1,0:T(8,128)(2,1)S(1)} %get-tuple-element.158.refs_0_.refs_3_), channel_id=1, source_target_pairs={{0,1},{1,0},{2,3},{3,2},{4,5},{5,4},{6,7},{7,6},{8,9},{9,8},{10,11... | collective-permute-start | bytes 1572872 | tf_op jit(solution)/shard_map/ppermute | solution.py:223
  81.0 21.6 %copy-start.19 = (bf16[256,2048]{1,0:T(8,128)(2,1)}, bf16[256,2048]{1,0:T(8,128)(2,1)S(1)}, u32[]{:S(2)}) copy-start(bf16[256,2048]{1,0:T(8,128)(2,1)S(1)} %get-tuple-element.169.refs_3_) | copy-start | bytes 3145732
  87.6 7.5 %collective-permute-start.6 = (bf16[1,1024,1024]{2,1,0:T(8,128)(2,1)S(1)}, bf16[1,1024,1024]{2,1,0:T(8,128)(2,1)S(1)}, u32[]{:S(2)}, u32[]{:S(2)}) collective-permute-start(bf16[1,1024,1024]{2,1,0:T(8,128)(2,1)S(1)} %get-tuple-element.171), channel_id=1, source_target_pairs={{0,2},{2,0},{4,6},{6,4},{8,10},{10,8},{12,14},{14,12},{16,18},{18,... | collective-permute-start | bytes 6291464 | tf_op jit(solution)/shard_map/ppermute | solution.py:223
  93.9 14.4 %collective-permute-start.5 = (bf16[256,1024]{1,0:T(8,128)(2,1)S(1)}, bf16[256,1024]{1,0:T(8,128)(2,1)S(1)}, u32[]{:S(2)}, u32[]{:S(2)}) collective-permute-start(bf16[256,1024]{1,0:T(8,128)(2,1)S(1)} %get-tuple-element.167), channel_id=1, source_target_pairs={{0,1},{1,0},{2,3},{3,2},{4,5},{5,4},{6,7},{7,6},{8,9},{9,8},{10,11... | collective-permute-start | bytes 1572872 | tf_op jit(solution)/shard_map/ppermute | solution.py:223
  99.5 14.4 %collective-permute-start.8 = (bf16[1,256,1024]{2,1,0:T(8,128)(2,1)}, bf16[1,256,1024]{2,1,0:T(8,128)(2,1)}, u32[]{:S(2)}, u32[]{:S(2)}) collective-permute-start(bf16[1,256,1024]{2,1,0:T(8,128)(2,1)} %get-tuple-element.178), channel_id=1, source_target_pairs={{0,4},{2,6},{4,0},{6,2},{8,12},{10,14},{12,8},{14,10},{16,20},{18,... | collective-permute-start | bytes 1572872 | tf_op jit(solution)/shard_map/ppermute | solution.py:223
  101.0 14.1 %collective-permute-start.9 = (bf16[1,256,1024]{2,1,0:T(8,128)(2,1)}, bf16[1,256,1024]{2,1,0:T(8,128)(2,1)}, u32[]{:S(2)}, u32[]{:S(2)}) collective-permute-start(bf16[1,256,1024]{2,1,0:T(8,128)(2,1)} %get-tuple-element.179), channel_id=1, source_target_pairs={{0,8},{2,10},{4,12},{6,14},{8,0},{10,2},{12,4},{14,6},{16,24},{18,... | collective-permute-start | bytes 1572872 | tf_op jit(solution)/shard_map/ppermute | solution.py:223
  110.9 19.3 %collective-permute-start.7 = (bf16[256,1024]{1,0:T(8,128)(2,1)S(1)}, bf16[256,1024]{1,0:T(8,128)(2,1)S(1)}, u32[]{:S(2)}, u32[]{:S(2)}) collective-permute-start(bf16[256,1024]{1,0:T(8,128)(2,1)S(1)} %get-tuple-element.175.refs_6_.refs_7_), channel_id=1, source_target_pairs={{0,1},{1,0},{2,3},{3,2},{4,5},{5,4},{6,7},{7,6},{8,9},{9,8},{10,11... | collective-permute-start | bytes 1572872 | tf_op jit(solution)/shard_map/ppermute | solution.py:223
  111.4 10.3 %collective-permute-start.12 = (bf16[1,512,2048]{2,1,0:T(8,128)(2,1)S(1)}, bf16[1,512,2048]{2,1,0:T(8,128)(2,1)S(1)}, u32[]{:S(2)}, u32[]{:S(2)}) collective-permute-start(bf16[1,512,2048]{2,1,0:T(8,128)(2,1)S(1)} %get-tuple-element.185), channel_id=1, source_target_pairs={{0,2},{2,0},{4,6},{6,4},{8,10},{10,8},{12,14},{14,12},{16,18},{18,... | collective-permute-start | bytes 6291464 | tf_op jit(solution)/shard_map/ppermute | solution.py:223
  119.5 8.1 %collective-permute-start.10 = (bf16[1,128,1024]{2,1,0:T(8,128)(2,1)S(1)}, bf16[1,128,1024]{2,1,0:T(8,128)(2,1)S(1)}, u32[]{:S(2)}, u32[]{:S(2)}) collective-permute-start(bf16[1,128,1024]{2,1,0:T(8,128)(2,1)S(1)} %get-tuple-element.183), channel_id=1, source_target_pairs={{0,8},{2,10},{4,12},{6,14},{8,0},{10,2},{12,4},{14,6},{16,24},{18,... | collective-permute-start | bytes 786440 | tf_op jit(solution)/shard_map/ppermute | solution.py:223
  121.1 8.2 %collective-permute-start.11 = (bf16[1,128,1024]{2,1,0:T(8,128)(2,1)S(1)}, bf16[1,128,1024]{2,1,0:T(8,128)(2,1)S(1)}, u32[]{:S(2)}, u32[]{:S(2)}) collective-permute-start(bf16[1,128,1024]{2,1,0:T(8,128)(2,1)S(1)} %get-tuple-element.184), channel_id=1, source_target_pairs={{0,4},{2,6},{4,0},{6,2},{8,12},{10,14},{12,8},{14,10},{16,20},{18,... | collective-permute-start | bytes 786440 | tf_op jit(solution)/shard_map/ppermute | solution.py:223
  125.6 24.6 %collective-permute-start.13 = (bf16[1,128,2048]{2,1,0:T(8,128)(2,1)S(1)}, bf16[1,128,2048]{2,1,0:T(8,128)(2,1)S(1)}, u32[]{:S(2)}, u32[]{:S(2)}) collective-permute-start(bf16[1,128,2048]{2,1,0:T(8,128)(2,1)S(1)} %get-tuple-element.196), channel_id=1, source_target_pairs={{0,4},{2,6},{4,0},{6,2},{8,12},{10,14},{12,8},{14,10},{16,20},{18,... | collective-permute-start | bytes 1572872 | tf_op jit(solution)/shard_map/ppermute | solution.py:223
  127.1 23.0 %collective-permute-start.14 = (bf16[1,128,2048]{2,1,0:T(8,128)(2,1)S(1)}, bf16[1,128,2048]{2,1,0:T(8,128)(2,1)S(1)}, u32[]{:S(2)}, u32[]{:S(2)}) collective-permute-start(bf16[1,128,2048]{2,1,0:T(8,128)(2,1)S(1)} %get-tuple-element.197), channel_id=1, source_target_pairs={{0,8},{2,10},{4,12},{6,14},{8,0},{10,2},{12,4},{14,6},{16,24},{18,... | collective-permute-start | bytes 1572872 | tf_op jit(solution)/shard_map/ppermute | solution.py:223
  130.9 15.4 %copy-start.35 = (f32[6144]{0:T(1024)S(1)}, f32[6144]{0:T(1024)}, u32[]{:S(2)}) copy-start(f32[6144]{0:T(1024)} %reshape.52) | copy-start | bytes 73732
  130.9 15.4 %copy-start.36 = (f32[1,2048]{1,0:T(1,128)S(1)}, f32[1,2048]{1,0:T(1,128)}, u32[]{:S(2)}) copy-start(f32[1,2048]{1,0:T(1,128)} %add.39) | copy-start | bytes 24580
  146.9 110.7 %collective-permute-start.35 = (f32[72,128]{1,0:T(8,128)}, f32[72,128]{1,0:T(8,128)}, u32[]{:S(2)}, u32[]{:S(2)}) collective-permute-start(f32[72,128]{1,0:T(8,128)} %maximum_bitcast_fusion.refs_0_), channel_id=1, source_target_pairs={{0,1},{1,0},{2,3},{3,2},{4,5},{5,4},{6,7},{7,6},{8,9},{9,8},{10,11... | collective-permute-start | bytes 110600 | tf_op jit(solution)/shard_map/ppermute | solution.py:223
  147.4 34.7 %collective-permute-start.20 = (bf16[1,256,1024]{2,1,0:T(8,128)(2,1)}, bf16[1,256,1024]{2,1,0:T(8,128)(2,1)}, u32[]{:S(2)}, u32[]{:S(2)}) collective-permute-start(bf16[1,256,1024]{2,1,0:T(8,128)(2,1)} %get-tuple-element.211.refs_0_), channel_id=1, source_target_pairs={{0,16},{2,18},{4,20},{6,22},{8,24},{10,26},{12,28},{14,30},{16,0},... | collective-permute-start | bytes 1572872 | tf_op jit(solution)/shard_map/ppermute | solution.py:223
  151.3 12.8 %collective-permute-start.16 = (bf16[1,64,2048]{2,1,0:T(8,128)(2,1)S(1)}, bf16[1,64,2048]{2,1,0:T(8,128)(2,1)S(1)}, u32[]{:S(2)}, u32[]{:S(2)}) collective-permute-start(bf16[1,64,2048]{2,1,0:T(8,128)(2,1)S(1)} %get-tuple-element.203), channel_id=1, source_target_pairs={{0,8},{2,10},{4,12},{6,14},{8,0},{10,2},{12,4},{14,6},{16,24},{18,... | collective-permute-start | bytes 786440 | tf_op jit(solution)/shard_map/ppermute | solution.py:223
  151.7 12.3 %collective-permute-start.17 = (bf16[1,64,2048]{2,1,0:T(8,128)(2,1)S(1)}, bf16[1,64,2048]{2,1,0:T(8,128)(2,1)S(1)}, u32[]{:S(2)}, u32[]{:S(2)}) collective-permute-start(bf16[1,64,2048]{2,1,0:T(8,128)(2,1)S(1)} %get-tuple-element.204), channel_id=1, source_target_pairs={{0,4},{2,6},{4,0},{6,2},{8,12},{10,14},{12,8},{14,10},{16,20},{18,... | collective-permute-start | bytes 786440 | tf_op jit(solution)/shard_map/ppermute | solution.py:223
  154.6 11.9 %collective-permute-start.15 = (bf16[4,512,512]{2,1,0:T(8,128)(2,1)S(1)}, bf16[4,512,512]{2,1,0:T(8,128)(2,1)S(1)}, u32[]{:S(2)}, u32[]{:S(2)}) collective-permute-start(bf16[4,512,512]{2,1,0:T(8,128)(2,1)S(1)} %get-tuple-element.200), channel_id=1, source_target_pairs={{0,2},{2,0},{4,6},{6,4},{8,10},{10,8},{12,14},{14,12},{16,18},{18,... | collective-permute-start | bytes 6291464 | tf_op jit(solution)/shard_map/ppermute | solution.py:223
  165.0 49.5 %collective-permute-start.25 = (bf16[1,128,2048]{2,1,0:T(8,128)(2,1)}, bf16[1,128,2048]{2,1,0:T(8,128)(2,1)}, u32[]{:S(2)}, u32[]{:S(2)}) collective-permute-start(bf16[1,128,2048]{2,1,0:T(8,128)(2,1)} %get-tuple-element.221.refs_0_), channel_id=1, source_target_pairs={{0,16},{2,18},{4,20},{6,22},{8,24},{10,26},{12,28},{14,30},{16,0},... | collective-permute-start | bytes 1572872 | tf_op jit(solution)/shard_map/ppermute | solution.py:223
  184.2 14.1 %collective-permute-start.21 = (bf16[1,128,1024]{2,1,0:T(8,128)(2,1)}, bf16[1,128,1024]{2,1,0:T(8,128)(2,1)}, u32[]{:S(2)}, u32[]{:S(2)}) collective-permute-start(bf16[1,128,1024]{2,1,0:T(8,128)(2,1)} %get-tuple-element.213.refs_1_), channel_id=1, source_target_pairs={{0,8},{2,10},{4,12},{6,14},{8,0},{10,2},{12,4},{14,6},{16,24},{18,... | collective-permute-start | bytes 786440 | tf_op jit(solution)/shard_map/ppermute | solution.py:223
  184.4 13.9 %collective-permute-start.22 = (bf16[1,128,1024]{2,1,0:T(8,128)(2,1)}, bf16[1,128,1024]{2,1,0:T(8,128)(2,1)}, u32[]{:S(2)}, u32[]{:S(2)}) collective-permute-start(bf16[1,128,1024]{2,1,0:T(8,128)(2,1)} %get-tuple-element.214.refs_2_), channel_id=1, source_target_pairs={{0,4},{2,6},{4,0},{6,2},{8,12},{10,14},{12,8},{14,10},{16,20},{18,... | collective-permute-start | bytes 786440 | tf_op jit(solution)/shard_map/ppermute | solution.py:223
  185.1 17.7 %collective-permute-start.18 = (bf16[4,128,512]{2,1,0:T(8,128)(2,1)S(1)}, bf16[4,128,512]{2,1,0:T(8,128)(2,1)S(1)}, u32[]{:S(2)}, u32[]{:S(2)}) collective-permute-start(bf16[4,128,512]{2,1,0:T(8,128)(2,1)S(1)} %get-tuple-element.209), channel_id=1, source_target_pairs={{0,4},{2,6},{4,0},{6,2},{8,12},{10,14},{12,8},{14,10},{16,20},{18,... | collective-permute-start | bytes 1572872 | tf_op jit(solution)/shard_map/ppermute | solution.py:223
  198.3 14.8 %collective-permute-start.19 = (bf16[4,128,512]{2,1,0:T(8,128)(2,1)S(1)}, bf16[4,128,512]{2,1,0:T(8,128)(2,1)S(1)}, u32[]{:S(2)}, u32[]{:S(2)}) collective-permute-start(bf16[4,128,512]{2,1,0:T(8,128)(2,1)S(1)} %get-tuple-element.210), channel_id=1, source_target_pairs={{0,8},{2,10},{4,12},{6,14},{8,0},{10,2},{12,4},{14,6},{16,24},{18,... | collective-permute-start | bytes 1572872 | tf_op jit(solution)/shard_map/ppermute | solution.py:223
  201.4 36.7 %collective-permute-start.28 = (bf16[1,256,1024]{2,1,0:T(8,128)(2,1)}, bf16[1,256,1024]{2,1,0:T(8,128)(2,1)}, u32[]{:S(2)}, u32[]{:S(2)}) collective-permute-start(bf16[1,256,1024]{2,1,0:T(8,128)(2,1)} %get-tuple-element.227), channel_id=1, source_target_pairs={{0,4},{2,6},{4,0},{6,2},{8,12},{10,14},{12,8},{14,10},{16,20},{18,... | collective-permute-start | bytes 1572872 | tf_op jit(solution)/shard_map/ppermute | solution.py:223
  202.8 35.3 %collective-permute-start.29 = (bf16[1,256,1024]{2,1,0:T(8,128)(2,1)}, bf16[1,256,1024]{2,1,0:T(8,128)(2,1)}, u32[]{:S(2)}, u32[]{:S(2)}) collective-permute-start(bf16[1,256,1024]{2,1,0:T(8,128)(2,1)} %get-tuple-element.228), channel_id=1, source_target_pairs={{0,8},{2,10},{4,12},{6,14},{8,0},{10,2},{12,4},{14,6},{16,24},{18,... | collective-permute-start | bytes 1572872 | tf_op jit(solution)/shard_map/ppermute | solution.py:223
  214.4 14.6 %collective-permute-start.23 = (bf16[4,64,512]{2,1,0:T(8,128)(2,1)S(1)}, bf16[4,64,512]{2,1,0:T(8,128)(2,1)S(1)}, u32[]{:S(2)}, u32[]{:S(2)}) collective-permute-start(bf16[4,64,512]{2,1,0:T(8,128)(2,1)S(1)} %get-tuple-element.219), channel_id=1, source_target_pairs={{0,8},{2,10},{4,12},{6,14},{8,0},{10,2},{12,4},{14,6},{16,24},{18,... | collective-permute-start | bytes 786440 | tf_op jit(solution)/shard_map/ppermute | solution.py:223
  214.5 14.8 %collective-permute-start.24 = (bf16[4,64,512]{2,1,0:T(8,128)(2,1)S(1)}, bf16[4,64,512]{2,1,0:T(8,128)(2,1)S(1)}, u32[]{:S(2)}, u32[]{:S(2)}) collective-permute-start(bf16[4,64,512]{2,1,0:T(8,128)(2,1)S(1)} %get-tuple-element.220), channel_id=1, source_target_pairs={{0,4},{2,6},{4,0},{6,2},{8,12},{10,14},{12,8},{14,10},{16,20},{18,... | collective-permute-start | bytes 786440 | tf_op jit(solution)/shard_map/ppermute | solution.py:223
  229.0 7.4 %collective-permute-start.32 = (bf16[1,64,2048]{2,1,0:T(8,128)(2,1)S(1)}, bf16[1,64,2048]{2,1,0:T(8,128)(2,1)S(1)}, u32[]{:S(2)}, u32[]{:S(2)}) collective-permute-start(bf16[1,64,2048]{2,1,0:T(8,128)(2,1)S(1)} %get-tuple-element.229.refs_1_), channel_id=1, source_target_pairs={{0,8},{2,10},{4,12},{6,14},{8,0},{10,2},{12,4},{14,6},{16,24},{18,... | collective-permute-start | bytes 786440 | tf_op jit(solution)/shard_map/ppermute | solution.py:223
  229.3 7.4 %collective-permute-start.33 = (bf16[1,64,2048]{2,1,0:T(8,128)(2,1)S(1)}, bf16[1,64,2048]{2,1,0:T(8,128)(2,1)S(1)}, u32[]{:S(2)}, u32[]{:S(2)}) collective-permute-start(bf16[1,64,2048]{2,1,0:T(8,128)(2,1)S(1)} %get-tuple-element.230.refs_2_), channel_id=1, source_target_pairs={{0,4},{2,6},{4,0},{6,2},{8,12},{10,14},{12,8},{14,10},{16,20},{18,... | collective-permute-start | bytes 786440 | tf_op jit(solution)/shard_map/ppermute | solution.py:223
  236.4 4.2 %collective-permute-start.27 = (bf16[1,512,1024]{2,1,0:T(8,128)(2,1)}, bf16[1,512,1024]{2,1,0:T(8,128)(2,1)}, u32[]{:S(2)}, u32[]{:S(2)}) collective-permute-start(bf16[1,512,1024]{2,1,0:T(8,128)(2,1)} %get-tuple-element.226.refs_1_), channel_id=1, source_target_pairs={{0,2},{2,0},{4,6},{6,4},{8,10},{10,8},{12,14},{14,12},{16,18},{18,... | collective-permute-start | bytes 3145736 | tf_op jit(solution)/shard_map/ppermute | solution.py:223
  236.7 16.1 %collective-permute-start.26 = (bf16[256,1024]{1,0:T(8,128)(2,1)}, bf16[256,1024]{1,0:T(8,128)(2,1)}, u32[]{:S(2)}, u32[]{:S(2)}) collective-permute-start(bf16[256,1024]{1,0:T(8,128)(2,1)} %get-tuple-element.225), channel_id=1, source_target_pairs={{0,1},{1,0},{2,3},{3,2},{4,5},{5,4},{6,7},{7,6},{8,9},{9,8},{10,11... | collective-permute-start | bytes 1572872 | tf_op jit(solution)/shard_map/ppermute | solution.py:223
  238.1 5.7 %collective-permute-start.30 = (bf16[1,256,1024]{2,1,0:T(8,128)(2,1)}, bf16[1,256,1024]{2,1,0:T(8,128)(2,1)}, u32[]{:S(2)}, u32[]{:S(2)}) collective-permute-start(bf16[1,256,1024]{2,1,0:T(8,128)(2,1)} %collective-permute-done.28.refs_3_), channel_id=1, source_target_pairs={{0,2},{2,0},{4,6},{6,4},{8,10},{10,8},{12,14},{14,12},{16,18},{18,... | collective-permute-start | bytes 1572872 | tf_op jit(solution)/shard_map/ppermute | solution.py:223
  238.1 6.3 %collective-permute-start.31 = (bf16[1,256,1024]{2,1,0:T(8,128)(2,1)}, bf16[1,256,1024]{2,1,0:T(8,128)(2,1)}, u32[]{:S(2)}, u32[]{:S(2)}) collective-permute-start(bf16[1,256,1024]{2,1,0:T(8,128)(2,1)} %collective-permute-done.29.refs_4_), channel_id=1, source_target_pairs={{0,2},{2,0},{4,6},{6,4},{8,10},{10,8},{12,14},{14,12},{16,18},{18,... | collective-permute-start | bytes 1572872 | tf_op jit(solution)/shard_map/ppermute | solution.py:223
  240.6 26.7 %collective-permute-start.34 = (bf16[4,128,512]{2,1,0:T(8,128)(2,1)S(1)}, bf16[4,128,512]{2,1,0:T(8,128)(2,1)S(1)}, u32[]{:S(2)}, u32[]{:S(2)}) collective-permute-start(bf16[4,128,512]{2,1,0:T(8,128)(2,1)S(1)} %get-tuple-element.235.refs_0_), channel_id=1, source_target_pairs={{0,16},{2,18},{4,20},{6,22},{8,24},{10,26},{12,28},{14,30},{16,0},... | collective-permute-start | bytes 1572872 | tf_op jit(solution)/shard_map/ppermute | solution.py:223
  243.8 24.4 %collective-permute-start.41 = (bf16[1,128,2048]{2,1,0:T(8,128)(2,1)}, bf16[1,128,2048]{2,1,0:T(8,128)(2,1)}, u32[]{:S(2)}, u32[]{:S(2)}) collective-permute-start(bf16[1,128,2048]{2,1,0:T(8,128)(2,1)} %get-tuple-element.249), channel_id=1, source_target_pairs={{0,4},{2,6},{4,0},{6,2},{8,12},{10,14},{12,8},{14,10},{16,20},{18,... | collective-permute-start | bytes 1572872 | tf_op jit(solution)/shard_map/ppermute | solution.py:223
  244.4 24.5 %collective-permute-start.42 = (bf16[1,128,2048]{2,1,0:T(8,128)(2,1)}, bf16[1,128,2048]{2,1,0:T(8,128)(2,1)}, u32[]{:S(2)}, u32[]{:S(2)}) collective-permute-start(bf16[1,128,2048]{2,1,0:T(8,128)(2,1)} %get-tuple-element.250), channel_id=1, source_target_pairs={{0,8},{2,10},{4,12},{6,14},{8,0},{10,2},{12,4},{14,6},{16,24},{18,... | collective-permute-start | bytes 1572872 | tf_op jit(solution)/shard_map/ppermute | solution.py:223
  252.8 16.6 %collective-permute-start.40 = (bf16[1,256,2048]{2,1,0:T(8,128)(2,1)}, bf16[1,256,2048]{2,1,0:T(8,128)(2,1)}, u32[]{:S(2)}, u32[]{:S(2)}) collective-permute-start(bf16[1,256,2048]{2,1,0:T(8,128)(2,1)} %get-tuple-element.248.refs_1_), channel_id=1, source_target_pairs={{0,2},{2,0},{4,6},{6,4},{8,10},{10,8},{12,14},{14,12},{16,18},{18,... | collective-permute-start | bytes 3145736 | tf_op jit(solution)/shard_map/ppermute | solution.py:223
  258.5 10.4 %collective-permute-start.38 = (f32[72,128]{1,0:T(8,128)S(1)}, f32[72,128]{1,0:T(8,128)S(1)}, u32[]{:S(2)}, u32[]{:S(2)}) collective-permute-start(f32[72,128]{1,0:T(8,128)S(1)} %get-tuple-element.245.refs_0_), channel_id=1, source_target_pairs={{0,2},{2,0},{4,6},{6,4},{8,10},{10,8},{12,14},{14,12},{16,18},{18,... | collective-permute-start | bytes 110600 | tf_op jit(solution)/shard_map/ppermute | solution.py:223
  268.1 13.5 %collective-permute-start.36 = (bf16[4,64,512]{2,1,0:T(8,128)(2,1)}, bf16[4,64,512]{2,1,0:T(8,128)(2,1)}, u32[]{:S(2)}, u32[]{:S(2)}) collective-permute-start(bf16[4,64,512]{2,1,0:T(8,128)(2,1)} %get-tuple-element.243.refs_1_), channel_id=1, source_target_pairs={{0,8},{2,10},{4,12},{6,14},{8,0},{10,2},{12,4},{14,6},{16,24},{18,... | collective-permute-start | bytes 786440 | tf_op jit(solution)/shard_map/ppermute | solution.py:223
  268.2 13.5 %collective-permute-start.37 = (bf16[4,64,512]{2,1,0:T(8,128)(2,1)}, bf16[4,64,512]{2,1,0:T(8,128)(2,1)}, u32[]{:S(2)}, u32[]{:S(2)}) collective-permute-start(bf16[4,64,512]{2,1,0:T(8,128)(2,1)} %get-tuple-element.244.refs_2_), channel_id=1, source_target_pairs={{0,4},{2,6},{4,0},{6,2},{8,12},{10,14},{12,8},{14,10},{16,20},{18,... | collective-permute-start | bytes 786440 | tf_op jit(solution)/shard_map/ppermute | solution.py:223
  268.8 2.3 collective-permute-start.43
  268.8 3.0 collective-permute-start.44
  269.4 10.3 %collective-permute-start.39 = (f32[72,128]{1,0:T(8,128)S(1)}, f32[72,128]{1,0:T(8,128)S(1)}, u32[]{:S(2)}, u32[]{:S(2)}) collective-permute-start(f32[72,128]{1,0:T(8,128)S(1)} %get-tuple-element.247.refs_0_), channel_id=1, source_target_pairs={{0,4},{2,6},{4,0},{6,2},{8,12},{10,14},{12,8},{14,10},{16,20},{18,... | collective-permute-start | bytes 110600 | tf_op jit(solution)/shard_map/ppermute | solution.py:223
  279.6 6.6 %collective-permute-start.50 = (f32[72,128]{1,0:T(8,128)S(1)}, f32[72,128]{1,0:T(8,128)S(1)}, u32[]{:S(2)}, u32[]{:S(2)}) collective-permute-start(f32[72,128]{1,0:T(8,128)S(1)} %get-tuple-element.257.refs_0_), channel_id=1, source_target_pairs={{0,8},{2,10},{4,12},{6,14},{8,0},{10,2},{12,4},{14,6},{16,24},{18,... | collective-permute-start | bytes 110600 | tf_op jit(solution)/shard_map/ppermute | solution.py:223
  284.8 14.6 %collective-permute-start.46 = (bf16[4,128,512]{2,1,0:T(8,128)(2,1)}, bf16[4,128,512]{2,1,0:T(8,128)(2,1)}, u32[]{:S(2)}, u32[]{:S(2)}) collective-permute-start(bf16[4,128,512]{2,1,0:T(8,128)(2,1)} %get-tuple-element.255), channel_id=1, source_target_pairs={{0,4},{2,6},{4,0},{6,2},{8,12},{10,14},{12,8},{14,10},{16,20},{18,... | collective-permute-start | bytes 1572872 | tf_op jit(solution)/shard_map/ppermute | solution.py:223
  286.2 14.5 %collective-permute-start.47 = (bf16[4,128,512]{2,1,0:T(8,128)(2,1)}, bf16[4,128,512]{2,1,0:T(8,128)(2,1)}, u32[]{:S(2)}, u32[]{:S(2)}) collective-permute-start(bf16[4,128,512]{2,1,0:T(8,128)(2,1)} %get-tuple-element.256), channel_id=1, source_target_pairs={{0,8},{2,10},{4,12},{6,14},{8,0},{10,2},{12,4},{14,6},{16,24},{18,... | collective-permute-start | bytes 1572872 | tf_op jit(solution)/shard_map/ppermute | solution.py:223
  286.3 16.3 %collective-permute-start.45 = (bf16[4,256,512]{2,1,0:T(8,128)(2,1)}, bf16[4,256,512]{2,1,0:T(8,128)(2,1)}, u32[]{:S(2)}, u32[]{:S(2)}) collective-permute-start(bf16[4,256,512]{2,1,0:T(8,128)(2,1)} %get-tuple-element.254.refs_1_), channel_id=1, source_target_pairs={{0,2},{2,0},{4,6},{6,4},{8,10},{10,8},{12,14},{14,12},{16,18},{18,... | collective-permute-start | bytes 3145736 | tf_op jit(solution)/shard_map/ppermute | solution.py:223
  286.9 11.7 %collective-permute-start.51 = (f32[72,128]{1,0:T(8,128)}, f32[72,128]{1,0:T(8,128)}, u32[]{:S(2)}, u32[]{:S(2)}) collective-permute-start(f32[72,128]{1,0:T(8,128)} %get-tuple-element.259.refs_0_), channel_id=1, source_target_pairs={{0,16},{2,18},{4,20},{6,22},{8,24},{10,26},{12,28},{14,30},{16,0},... | collective-permute-start | bytes 110600 | tf_op jit(solution)/shard_map/ppermute | solution.py:223
  299.4 3.2 %collective-permute-start.48 = (bf16[4,128,512]{2,1,0:T(8,128)(2,1)}, bf16[4,128,512]{2,1,0:T(8,128)(2,1)S(1)}, u32[]{:S(2)}, u32[]{:S(2)}) collective-permute-start(bf16[4,128,512]{2,1,0:T(8,128)(2,1)} %collective-permute-done.46.refs_3_), channel_id=1, source_target_pairs={{0,2},{2,0},{4,6},{6,4},{8,10},{10,8},{12,14},{14,12},{16,18},{18,... | collective-permute-start | bytes 1572872 | tf_op jit(solution)/shard_map/ppermute | solution.py:223
  300.8 2.1 collective-permute-start.49
  (25 other events, 110.2 us)

commit v2 on v1

--- a/solution.py
+++ b/solution.py
@@ -547,8 +547,10 @@
     )
 
 
-def attention_back(chain, first, second, d_first, d_second, w_out):
+def attention_back(chain, first, second, d_first, d_second, w_out, half):
     _, rows, width = first.shape
+    width = width // 2
+    skip = half * (width // PAIR)
     depth = w_out.shape[1]
     scale = HEAD_DIM ** (-0.5)
 
@@ -591,7 +593,7 @@
         sums[...] = jnp.concatenate([query_sum, jnp.sum(value_grad, axis=0, keepdims=True)], axis=0)
 
     def part(p):
-        return lambda i: (p, 0, i)
+        return lambda i: (p, 0, i + skip)
 
     block = (1, rows, PAIR)
     out = (like((3, rows, width), BF), (3, rows, PAIR), lambda i: (0, 0, i))
@@ -599,20 +601,20 @@
         kernel,
         "attention_back",
         [(x, block, part(p)) for p in range(3) for x in (first, second)]
-        + [whole(d_first), whole(d_second), (w_out, (PAIR, depth), lambda i: (i, 0))],
+        + [whole(d_first), whole(d_second), (w_out, (PAIR, depth), lambda i: (i + skip, 0))],
         [out, out, (like((2, width), F32), (2, PAIR), lambda i: (0, i))],
         grid=(width // PAIR,),
     )
 
 
-def to_tokens(chain, d_parts, w_parts, out_dtype, adds=()):
-    parts, rows, width = d_parts.shape
+def to_tokens(chain, d_halves, w_parts, out_dtype, adds=()):
+    parts, rows, width = d_halves[0].shape
     depth = w_parts.shape[1]
 
-    def kernel(d, w, *refs):
+    def kernel(d_a, d_b, w, *refs):
         out, total = refs[-2:]
         step = pl.program_id(0)
-        term = times_transposed(d[0], w[0])
+        term = times_transposed(d_a[0], w[0, :, :width]) + times_transposed(d_b[0], w[0, :, width:])
 
         @pl.when(step == 0)
         def _():
@@ -633,7 +635,8 @@
     return chain.call(
         kernel,
         "to_tokens",
-        [(d_parts, (1, rows, width), part), (w_parts, (1, depth, width), part)]
+        [(d, (1, rows, width), part) for d in d_halves]
+        + [(w_parts, (1, depth, 2 * width), part)]
         + [whole(x) for x in adds],
         [whole(like((rows, depth), out_dtype))],
         grid=(parts,),
@@ -781,7 +784,7 @@
         )
         self.got = [self.dp.swap(x, order[1]) for x, order in zip(self.held, self.orders)]
 
-    def home(self):
+    def home(self, early=False):
         groups, columns, n = self.groups, self.columns, len(self.orders)
         half = self.rows // 2
         bits = [self.dp.bit(order[1]) for order in self.orders]
@@ -790,36 +793,61 @@
             for i in range(n):
                 at = pl.multiple_of(places[i] * half, half)
                 other = pl.multiple_of((1 - places[i]) * half, half)
-                out, all_out = refs[2 * n + i], refs[3 * n]
                 start = i * 2 * half
                 for source, place in ((refs[i], at), (refs[n + i], other)):
                     value = source[...]
-                    out[:, pl.ds(place, half), :] = value
-                    all_out[:, pl.ds(pl.multiple_of(start + place, half), half), :] = value
+                    refs[2 * n + i][:, pl.ds(place, half), :] = value
+                    if early:
+                        both = pl.ds(pl.multiple_of(start + place, half), half)
+                        refs[3 * n][:, both, :] = value
 
         ins = [whole(x) for x in list(self.held) + list(self.got)]
         outs = [whole(like((groups, 2 * half, columns), BF))] * n
-        outs.append(whole(like((groups, 2 * n * half, columns), BF)))
-        *self.held, self.all_held = self.dp.chain.call(
+        if early:
+            outs.append(whole(like((groups, 2 * n * half, columns), BF)))
+        found = self.dp.chain.call(
             kernel, "home", ins, outs, scalars=jnp.stack(bits).astype(jnp.int32)
         )
+        self.held, self.all_held = found[:n], found[n:]
         self.got = [self.dp.swap(x, order[0]) for x, order in zip(self.held, self.orders)]
-        self.all_in = self.dp.swap(self.all_held, 0)
+
+        self.all_in = [self.dp.swap(x, 0) for x in self.all_held]
+
+    def join(self):
+        groups, columns, n, rows = self.groups, self.columns, len(self.orders), self.rows
+        bits = [self.dp.bit(order[0]) for order in self.orders]
+
+        def kernel(places, *refs):
+            for i in range(n):
+                for source, which in ((refs[i], places[i]), (refs[n + i], 1 - places[i])):
+                    at = pl.multiple_of((2 * i + which) * rows, rows)
+                    refs[2 * n][:, pl.ds(at, rows), :] = source[...]
+
+        ins = [whole(x) for x in list(self.held) + list(self.got)]
+        outs = [whole(like((groups, 2 * n * rows, columns), BF))]
+        self.half = self.dp.chain.call(
+            kernel, "join", ins, outs, scalars=jnp.stack(bits).astype(jnp.int32)
+        )[0]
+        self.half_in = self.dp.swap(self.half, 0)
 
     def result(self, shapes, split):
         dp, n, groups, columns, rows = self.dp, len(self.orders), self.groups, self.columns, self.rows
-        got_in = [dp.swap(x, 0) for x in self.got]
         core = dp.bit(0)
         places = []
-        sources = [(self.all_held, 0, core), (self.all_in, 0, 1 - core)]
-        sources += [(got, 1, core) for got in self.got] + [(got, 1, 1 - core) for got in got_in]
-        bits = [dp.bit(order[0]) for order in self.orders]
-        for which in (core, 1 - core):
-            places += [which * 2 * n + 2 * i + bit for i, bit in enumerate(bits)]
-        for which in (core, 1 - core):
-            places += [which * 2 * n + 2 * i + 1 - bit for i, bit in enumerate(bits)]
-        arrays = [self.all_held, self.all_in] + list(self.got) + got_in
-        owners = [i for i in range(2) for _ in range(n)] + list(range(2, 2 + 2 * n))
+        if self.all_held:
+            got_in = [dp.swap(x, 0) for x in self.got]
+            arrays = self.all_held + self.all_in + list(self.got) + got_in
+            owners = [i for i in range(2) for _ in range(n)] + list(range(2, 2 + 2 * n))
+            bits = [dp.bit(order[0]) for order in self.orders]
+            for which in (core, 1 - core):
+                places += [which * 2 * n + 2 * i + bit for i, bit in enumerate(bits)]
+            for which in (core, 1 - core):
+                places += [which * 2 * n + 2 * i + 1 - bit for i, bit in enumerate(bits)]
+        else:
+            arrays = [self.half, self.half_in]
+            owners = [i for i in range(2) for _ in range(2 * n)]
+            for which in (core, 1 - core):
+                places += [which * 2 * n + i for i in range(2 * n)]
         count = len(owners)
         block = (groups, rows, columns)
 
@@ -875,8 +903,8 @@
     own_rows, width = tokens.shape
     local_width = w_out.shape[0]
     hidden_width = w_up.shape[1]
-    w_parts = in_hbm(jnp.transpose(w_qkv, (1, 0, 2)))
-    w_out, w_up, w_down = in_hbm(w_out), in_hbm(w_up), in_hbm(w_down)
+    w_parts = jnp.transpose(w_qkv, (1, 0, 2))
+    w_up_back, w_down_back = in_hbm(w_up), in_hbm(w_down)
     bias = jnp.stack([b_query, jnp.zeros_like(b_query), b_value])[:, None, :]
     b_out, gain_one, shift_one, b_up, b_down, gain_two, shift_two = (
         x[None, :] for x in (b_out, gain_one, shift_one, b_up, b_down, gain_two, shift_two)
@@ -899,7 +927,9 @@
         chain, down_own, down_got, b_down, hidden, gain_two, shift_two, out_grad
     )
     d_two_p = pair_swap(d_two_o)
-    d_up_o, b_up_o, dhid_own = down_and_up_back(chain, d_two_o, slope_o, w_down, w_up, F32)
+    d_up_o, b_up_o, dhid_own = down_and_up_back(
+        chain, d_two_o, slope_o, w_down_back, w_up_back, F32
+    )
 
     def core_half(x):
         return (x, (own_rows, x.shape[1] // 2), lambda s, places: (0, places[0]))
@@ -926,7 +956,9 @@
 
     sum_down = plain_sum((active_o, active_p), (d_two_o, d_two_p), 256)
     sum_down.begin()
-    d_up_p, b_up_p, dhid_send = down_and_up_back(chain, d_two_p, slope_p, w_down, w_up, BF)
+    d_up_p, b_up_p, dhid_send = down_and_up_back(
+        chain, d_two_p, slope_p, w_down_back, w_up_back, BF
+    )
     dhid_got = pair_swap(dhid_send)
     sum_down.own()
     sum_down.start(0)
@@ -937,20 +969,24 @@
     )
     d_one_p = pair_swap(d_one_o)
     sum_down.halve()
+    early = attention_back(chain, qkv_o, qkv_p, d_one_o, d_one_p, w_out, 0)
+    sum_down.middle()
+    sum_down.cross()
     sum_up.own()
     sum_up.start(0)
-    sum_down.middle()
-    sum_down.cross()
-    d_qkv_o, d_qkv_p, sums_qv = attention_back(chain, qkv_o, qkv_p, d_one_o, d_one_p, w_out)
-    sum_up.halve()
+    late = attention_back(chain, qkv_o, qkv_p, d_one_o, d_one_p, w_out, 1)
+    d_qkv_o, d_qkv_p = (early[0], late[0]), (early[1], late[1])
+    sums_qv = jnp.concatenate([early[2], late[2]], axis=1)
 
     def rest_product(refs, total):
         step = pl.program_id(0)
 
         @pl.when(step < 3)
         def _():
-            total[...] = contract_rows(refs[0][...], refs[4][0])
-            total[...] += contract_rows(refs[1][...], refs[5][0])
+            for i in range(2):
+                cut = slice(i * local_width // 2, (i + 1) * local_width // 2)
+                total[:, cut] = contract_rows(refs[0][...], refs[4 + i][0])
+                total[:, cut] += contract_rows(refs[1][...], refs[6 + i][0])
 
         @pl.when(step == 3)
         def _():
@@ -958,8 +994,8 @@
             for i in range(2):
                 at = slice(i * rows, (i + 1) * rows)
                 cut = slice(i * local_width, (i + 1) * local_width)
-                total[at, :] = contract_rows(refs[2][...], refs[6][:, cut])
-                total[at, :] += contract_rows(refs[3][...], refs[7][:, cut])
+                total[at, :] = contract_rows(refs[2][...], refs[8][:, cut])
+                total[at, :] += contract_rows(refs[3][...], refs[9][:, cut])
 
     def part_at(x):
         return (x, (1,) + x.shape[1:], lambda s, places: (jnp.minimum(s, 2), 0, 0))
@@ -967,7 +1003,8 @@
     sum_rest = WeightSum(
         dp,
         [core_half(tokens), core_half(tokens_p), core_half(ctx_o), core_half(ctx_p)]
-        + [part_at(d_qkv_o), part_at(d_qkv_p), whole(d_one_o), whole(d_one_p)],
+        + [part_at(x) for x in d_qkv_o + d_qkv_p]
+        + [whole(d_one_o), whole(d_one_p)],
         rest_product,
         4,
         width // 8,
@@ -978,33 +1015,38 @@
     shared = jnp.concatenate([sums_two, sums_one], axis=0).reshape(-1)
     small = jnp.concatenate([shared, sums_qv.reshape(-1), (b_up_o + b_up_p).reshape(-1)])
     small = small.reshape(-1, 128)
-    sum_up.middle()
+    sum_up.halve()
     sum_rest.own()
     sum_rest.start(0)
+    sum_up.middle()
     sum_down.back()
     sum_up.cross()
+    sum_rest.halve()
     sum_down.home()
-    sum_rest.halve()
     sum_up.back()
     sum_rest.middle()
+    small, sum_rest.held = lax.optimization_barrier((small, sum_rest.held))
     sum_rest.cross()
+    sum_up.home()
+    sum_down.join()
+    small_got = pair_swap(small)
     tokens_send = to_tokens(chain, d_qkv_p, w_parts, BF)
     tokens_got = pair_swap(tokens_send)
-    sum_up.home()
     grad_w_down = plain_result(sum_down, hidden_width, width)
-    small_got = pair_swap(small)
-    grad_tokens = to_tokens(chain, d_qkv_o, w_parts, F32, (d_one, tokens_got))
     small = dp.hop(small, small_got, shared.shape[0] // 128)
     small_got = dp.swap(small, 0)
     sum_rest.back()
+    sum_up.join()
     small = dp.hop(small, small_got, small.shape[0])
     small_got = dp.swap(small, 1)
-    grad_w_up = plain_result(sum_up, width, hidden_width)
+    grad_tokens = to_tokens(chain, d_qkv_o, w_parts, F32, (d_one, tokens_got))
     small = dp.hop(small, small_got, small.shape[0])
     small_got = dp.swap(small, 2)
-    sum_rest.home()
+    sum_rest.home(early=True)
     small = dp.hop(small, small_got, small.shape[0])
     small_got = dp.swap(small, 3)
+    grad_w_up = plain_result(sum_up, width, hidden_width)
+    sum_rest.got, chain.last = lax.optimization_barrier((sum_rest.got, chain.last))
     small = dp.hop(small, small_got, small.shape[0]).reshape(-1)
     piece = width // 8
     grad_w_qkv, grad_w_out = sum_rest.result(

time: 312 us -> 290 us (0.929)
  waiting for transfers between devices: 114 us -> 95.5 us
  Pallas kernels: 140 us -> 127 us
  local copies, waits for them, and re-layouts: 7.62 us -> 16.3 us
    ppermute x52 -> x48, waiting for transfers between devices: 114 us -> 95.5 us  [swap(): got = lax.ppermute(x, axis, pairs)]
    pallas_call x46 -> x45, Pallas kernels: 140 us -> 127 us  [call(): pl.pallas_call(run, grid_spec=pltpu.PrefetchScalarGridSpec(num_scalar_pre...]
    unnamed x75 -> x99, local copies, waits for them, and re-layouts: 4.87 us -> 13.5 us
    ppermute x52 -> x48, starting transfers between devices: 45.3 us -> 46.6 us  [swap(): got = lax.ppermute(x, axis, pairs)]
  transfers between devices with their start and end apart: 52 -> 48, of which waited for: 24 -> 22; matrix products, arithmetic and copies ran while one was open for 2% -> 2% of each run, Pallas kernels for 35% -> 34%
where the time goes in v2:
time: 290 us; the launch traced here: 289 us
  Pallas kernels  127 us (44%)
  waiting for transfers between devices  95.5 us (33%)
  starting transfers between devices  46.6 us (16%)
  local copies, waits for them, and re-layouts  16.3 us (6%)
    pallas_call x45, Pallas kernels, call(): pl.pallas_call(run, grid_spec=pltpu.PrefetchScalarGridSpec(num_scalar_pre...  127 us
    ppermute x48, waiting for transfers between devices, swap(): got = lax.ppermute(x, axis, pairs)  95.5 us
    ppermute x48, starting transfers between devices, swap(): got = lax.ppermute(x, axis, pairs)  46.6 us
    unnamed x99, local copies, waits for them, and re-layouts  13.5 us
  transfers between devices with their start and end apart: 48, of which 22 were waited for; matrix products, arithmetic and copies ran while one was open for 2% of the time, Pallas kernels for 34%

profile of v2, /device:TPU:0, one launch (start us, length us, event | category | flops | bytes accessed | tf_op | source)
XLA Modules:
  0.0 288.7 jit_solution(9706489215968513755)
XLA Ops:
  0.6 3.0 %collective-permute-start = (bf16[256,1024]{1,0:T(8,128)(2,1)}, bf16[256,1024]{1,0:T(8,128)(2,1)}, u32[]{:S(2)}, u32[]{:S(2)}) collective-permute-start(bf16[256,1024]{1,0:T(8,128)(2,1)} %refs_1_.7), channel_id=1, source_target_pairs={{0,1},{1,0},{2,3},{3,2},{4,5},{5,4},{6,7},{7,6},{8,9},{9,8},{10,11... | collective-permute-start | bytes 1572872 | tf_op jit(solution)/shard_map/ppermute | solution.py:223
  4.5 1.9 copy-done.2
  7.5 1.3 project.2
  10.2 5.7 %collective-permute-done.refs_0_.refs_2_ = bf16[256,1024]{1,0:T(8,128)(2,1)} collective-permute-done((bf16[256,1024]{1,0:T(8,128)(2,1)}, bf16[256,1024]{1,0:T(8,128)(2,1)}, u32[]{:S(2)}, u32[]{:S(2)}) %collective-permute-start) | collective-permute-done | bytes 524320 | tf_op jit(solution)/shard_map/ppermute | solution.py:223
  15.9 2.5 project.3
  18.5 5.6 %attention.2 = (bf16[256,512]{1,0:T(8,128)(2,1)S(1)}, bf16[256,1024]{1,0:T(8,128)(2,1)S(1)}, f32[8,128]{1,0:T(8,128)S(1)}) custom-call(bf16[3,256,512]{2,1,0:T(8,128)(2,1)S(1)} %get-tuple-element.154.refs_0_.refs_2_.refs_4_.refs_1_.refs_3_.refs_5_, bf16[3,256,512]{2,1,0:T(8,128)(2,1)S(1)} %copy-done.35, ...), custom_call_target="tpu_custom_call" | custom-call | flops 40000000000 | bytes 1000000 | tf_op jit(solution)/shard_map/attention/pallas_call | solution.py:249
  24.1 1.8 collective-permute-start.1
  26.0 5.7 %attention.3 = (bf16[256,512]{1,0:T(8,128)(2,1)S(1)}, f32[256,1024]{1,0:T(8,128)S(1)}, f32[8,128]{1,0:T(8,128)S(1)}) custom-call(bf16[3,256,512]{2,1,0:T(8,128)(2,1)S(1)} %copy-done.35, bf16[3,256,512]{2,1,0:T(8,128)(2,1)S(1)} %copy-done.35, bf16[3,256,512]{2,1,0:T(8,128)(2,1)S(1)} %get-tuple-element.154.refs_0_.refs_2_.refs_4_.refs_1_.refs_3_.refs_5_, ...), custom_call_target="tpu_custom_call" | custom-call | flops 40000000000 | bytes 1000000 | tf_op jit(solution)/shard_map/attention/pallas_call | solution.py:249
  32.3 5.0 %collective-permute-done.1.refs_1_ = bf16[256,1024]{1,0:T(8,128)(2,1)S(1)} collective-permute-done((bf16[256,1024]{1,0:T(8,128)(2,1)S(1)}, bf16[256,1024]{1,0:T(8,128)(2,1)S(1)}, u32[]{:S(2)}, u32[]{:S(2)}) %collective-permute-start.1) | collective-permute-done | bytes 524320 | tf_op jit(solution)/shard_map/ppermute | solution.py:223
  38.0 1.5 collective-permute-start.2
  41.0 4.7 %up_and_down.2 = (bf16[256,2048]{1,0:T(8,128)(2,1)S(1)}, bf16[256,2048]{1,0:T(8,128)(2,1)S(1)}, f32[256,1024]{1,0:T(8,128)S(1)}, f32[8,128]{1,0:T(8,128)S(1)}) custom-call(bf16[256,1024]{1,0:T(8,128)(2,1)S(1)} %get-tuple-element.160.refs_0_.refs_1_, bf16[1024,2048]{1,0:T(8,128)(2,1)S(1)} %copy-done, f32[1,2048]{1,0:T(1,128)S(1)} %bitcast.65, ...), custom_call_target="tpu_custom_call" | custom-call | flops 40000000000 | bytes 1000000 | tf_op jit(solution)/shard_map/up_and_down/pallas_call | solution.py:249
  45.7 4.6 %collective-permute-done.2.refs_0_.refs_2_ = bf16[256,1024]{1,0:T(8,128)(2,1)S(1)} collective-permute-done((bf16[256,1024]{1,0:T(8,128)(2,1)S(1)}, bf16[256,1024]{1,0:T(8,128)(2,1)S(1)}, u32[]{:S(2)}, u32[]{:S(2)}) %collective-permute-start.2) | collective-permute-done | bytes 524320 | tf_op jit(solution)/shard_map/ppermute | solution.py:223
  50.3 5.5 %up_and_down.3 = (bf16[256,2048]{1,0:T(8,128)(2,1)S(1)}, bf16[256,2048]{1,0:T(8,128)(2,1)S(1)}, bf16[256,1024]{1,0:T(8,128)(2,1)}, f32[8,128]{1,0:T(8,128)S(1)}) custom-call(bf16[256,1024]{1,0:T(8,128)(2,1)S(1)} %collective-permute-done.2.refs_0_.refs_2_, bf16[1024,2048]{1,0:T(8,128)(2,1)S(1)} %copy-done, f32[1,2048]{1,0:T(1,128)S(1)} %bitcast.66, ...), custom_call_target="tpu_custom_call" | custom-call | flops 40000000000 | bytes 1000000 | tf_op jit(solution)/shard_map/up_and_down/pallas_call | solution.py:249
  56.9 10.5 %collective-permute-done.3.refs_1_ = bf16[256,1024]{1,0:T(8,128)(2,1)} collective-permute-done((bf16[256,1024]{1,0:T(8,128)(2,1)}, bf16[256,1024]{1,0:T(8,128)(2,1)}, u32[]{:S(2)}, u32[]{:S(2)}) %collective-permute-start.3) | collective-permute-done | bytes 524320 | tf_op jit(solution)/shard_map/ppermute | solution.py:223
  67.4 2.8 second_norm.1
  70.9 6.2 %down_and_up_back.2 = (bf16[256,2048]{1,0:T(8,128)(2,1)S(1)}, f32[1,2048]{1,0:T(1,128)S(1)}, f32[256,1024]{1,0:T(8,128)S(1)}, f32[8,128]{1,0:T(8,128)S(1)}) custom-call(bf16[256,1024]{1,0:T(8,128)(2,1)S(1)} %get-tuple-element.169.refs_0_.refs_3_, bf16[256,2048]{1,0:T(8,128)(2,1)S(1)} %get-tuple-element.170.refs_1_, bf16[2048,1024]{1,0:T(8,128)(2,1)} %refs_2_.5, ...), custom_call_target="tpu_custom_call" | custom-call | flops 40000000000 | bytes 1000000 | tf_op jit(solution)/shard_map/down_and_up_back/pallas_call | solution.py:249
  77.1 3.4 %collective-permute-done.4.refs_4_.refs_0_ = bf16[256,1024]{1,0:T(8,128)(2,1)S(1)} collective-permute-done((bf16[256,1024]{1,0:T(8,128)(2,1)S(1)}, bf16[256,1024]{1,0:T(8,128)(2,1)S(1)}, u32[]{:S(2)}, u32[]{:S(2)}) %collective-permute-start.4) | collective-permute-done | bytes 524320 | tf_op jit(solution)/shard_map/ppermute | solution.py:223
  80.5 3.3 %other_core_rows.3 = (bf16[1,1024,1024]{2,1,0:T(8,128)(2,1)S(1)}, f32[8,128]{1,0:T(8,128)S(1)}) custom-call(s32[5]{0:T(128)S(1)} %stack.72.refs_0_, bf16[256,2048]{1,0:T(8,128)(2,1)S(1)} %get-tuple-element.174.refs_1_, bf16[256,2048]{1,0:T(8,128)(2,1)S(1)} %get-tuple-element.175.refs_2_, bf16[256,1024]{1,0:T(8,128)(2,1)S(1)} %get-tuple-element.169.refs_0_.refs_3_, ...), custom_call_target="tpu_custom_call" | custom-call | flops 40000000000 | bytes 1000000 | tf_op jit(solution)/shard_map/other_core_rows/pallas_call | solution.py:249
  83.8 6.2 %down_and_up_back.3 = (bf16[256,2048]{1,0:T(8,128)(2,1)S(1)}, f32[1,2048]{1,0:T(1,128)S(1)}, bf16[256,1024]{1,0:T(8,128)(2,1)S(1)}, f32[8,128]{1,0:T(8,128)S(1)}) custom-call(bf16[256,1024]{1,0:T(8,128)(2,1)S(1)} %collective-permute-done.4.refs_4_.refs_0_, bf16[256,2048]{1,0:T(8,128)(2,1)S(1)} %get-tuple-element.173.refs_1_, bf16[2048,1024]{1,0:T(8,128)(2,1)} %refs_2_.5, ...), custom_call_target="tpu_custom_call" | custom-call | flops 40000000000 | bytes 1000000 | tf_op jit(solution)/shard_map/down_and_up_back/pallas_call | solution.py:249
  91.1 4.5 %own_core_rows.3 = (bf16[1,256,1024]{2,1,0:T(8,128)(2,1)}, bf16[1,256,1024]{2,1,0:T(8,128)(2,1)}, bf16[1,256,1024]{2,1,0:T(8,128)(2,1)S(1)}, bf16[1,256,1024]{2,1,0:T(8,128)(2,1)S(1)}, f32[8,128]{1,0:T(8,128)S(1)}) custom-call(s32[5]{0:T(128)S(1)} %stack.74.refs_0_, bf16[256,2048]{1,0:T(8,128)(2,1)S(1)} %get-tuple-element.174.refs_1_, ...), custom_call_target="tpu_custom_call" | custom-call | flops 40000000000 | bytes 1000000 | tf_op jit(solution)/shard_map/own_core_rows/pallas_call | solution.py:249
  95.6 1.5 collective-permute-start.8
  97.1 1.6 collective-permute-start.9
  98.7 3.0 %other_core_rows.4 = (bf16[1,512,2048]{2,1,0:T(8,128)(2,1)S(1)}, f32[8,128]{1,0:T(8,128)S(1)}) custom-call(s32[5]{0:T(128)S(1)} %stack.72.refs_0_, bf16[256,1024]{1,0:T(8,128)(2,1)S(1)} %get-tuple-element.160.refs_0_.refs_1_, bf16[256,1024]{1,0:T(8,128)(2,1)S(1)} %collective-permute-done.2.refs_0_.refs_2_, bf16[256,2048]{1,0:T(8,128)(2,1)S(1)} %get-tuple-element.180.refs_3_, ...), custom_call_target="tpu_custom_call" | custom-call | flops 40000000000 | bytes 1000000 | tf_op jit(solution)/shard_map/other_core_rows/pallas_call | solution.py:249
  103.1 1.3 collective-permute-done.5.refs_2_
  108.3 1.8 collective-permute-done.8.refs_3_
  113.3 2.4 halve.3
  115.7 1.6 collective-permute-start.11
  117.9 3.8 %collective-permute-done.7.refs_7_.refs_10_ = bf16[256,1024]{1,0:T(8,128)(2,1)S(1)} collective-permute-done((bf16[256,1024]{1,0:T(8,128)(2,1)}, bf16[256,1024]{1,0:T(8,128)(2,1)S(1)}, u32[]{:S(2)}, u32[]{:S(2)}) %collective-permute-start.7) | collective-permute-done | bytes 524320 | tf_op jit(solution)/shard_map/ppermute | solution.py:223
  121.7 7.5 %attention_back.2 = (bf16[3,256,256]{2,1,0:T(8,128)(2,1)S(1)}, bf16[3,256,256]{2,1,0:T(8,128)(2,1)S(1)}, f32[2,256]{1,0:T(2,128)S(1)}, f32[8,128]{1,0:T(8,128)S(1)}) custom-call(bf16[3,256,512]{2,1,0:T(8,128)(2,1)S(1)} %copy-done.36, bf16[3,256,512]{2,1,0:T(8,128)(2,1)S(1)} %copy-done.38, bf16[3,256,512]{2,1,0:T(8,128)(2,1)S(1)} %copy-done.36, ...), custom_call_target="tpu_custom_call" | custom-call | flops 40000000000 | bytes 1000000 | tf_op jit(solution)/shard_map/attention_back/pallas_call | solution.py:249
  130.2 1.5 collective-permute-start.13
  131.7 3.8 %own_core_rows.4 = (bf16[1,128,2048]{2,1,0:T(8,128)(2,1)S(1)}, bf16[1,128,2048]{2,1,0:T(8,128)(2,1)S(1)}, bf16[1,128,2048]{2,1,0:T(8,128)(2,1)S(1)}, bf16[1,128,2048]{2,1,0:T(8,128)(2,1)S(1)}, f32[8,128]{1,0:T(8,128)S(1)}) custom-call(s32[5]{0:T(128)S(1)} %stack.74.refs_0_, bf16[256,1024]{1,0:T(8,128)(2,1)S(1)} %copy-done.12, ...), custom_call_target="tpu_custom_call" | custom-call | flops 40000000000 | bytes 1000000 | tf_op jit(solution)/shard_map/own_core_rows/pallas_call | solution.py:249
  135.5 1.5 collective-permute-start.14
  137.0 1.6 collective-permute-start.15
  138.6 7.3 %attention_back.3 = (bf16[3,256,256]{2,1,0:T(8,128)(2,1)S(1)}, bf16[3,256,256]{2,1,0:T(8,128)(2,1)S(1)}, f32[2,256]{1,0:T(2,128)S(1)}, f32[8,128]{1,0:T(8,128)S(1)}) custom-call(bf16[3,256,512]{2,1,0:T(8,128)(2,1)S(1)} %copy-done.36, bf16[3,256,512]{2,1,0:T(8,128)(2,1)S(1)} %copy-done.38, bf16[3,256,512]{2,1,0:T(8,128)(2,1)S(1)} %copy-done.36, ...), custom_call_target="tpu_custom_call" | custom-call | flops 40000000000 | bytes 1000000 | tf_op jit(solution)/shard_map/attention_back/pallas_call | solution.py:249
  146.0 3.8 %other_core_rows.5 = (bf16[4,512,512]{2,1,0:T(8,128)(2,1)S(1)}, f32[8,128]{1,0:T(8,128)S(1)}) custom-call(s32[5]{0:T(128)S(1)} %stack.72.refs_0_, bf16[256,1024]{1,0:T(8,128)(2,1)S(1)} %copy-done.10, bf16[256,1024]{1,0:T(8,128)(2,1)} %collective-permute-done.refs_0_.refs_2_, bf16[256,512]{1,0:T(8,128)(2,1)S(1)} %copy-done.46, ...), custom_call_target="tpu_custom_call" | custom-call | flops 40000000000 | bytes 1000000 | tf_op jit(solution)/shard_map/other_core_rows/pallas_call | solution.py:249
  150.5 9.8 %collective-permute-done.15.refs_4_ = bf16[1,128,2048]{2,1,0:T(8,128)(2,1)S(1)} collective-permute-done((bf16[1,128,2048]{2,1,0:T(8,128)(2,1)S(1)}, bf16[1,128,2048]{2,1,0:T(8,128)(2,1)S(1)}, u32[]{:S(2)}, u32[]{:S(2)}) %collective-permute-start.15) | collective-permute-done | bytes 524320 | tf_op jit(solution)/shard_map/ppermute | solution.py:223
  161.6 4.2 %own_core_rows.5 = (bf16[4,128,512]{2,1,0:T(8,128)(2,1)S(1)}, bf16[4,128,512]{2,1,0:T(8,128)(2,1)S(1)}, bf16[4,128,512]{2,1,0:T(8,128)(2,1)S(1)}, bf16[4,128,512]{2,1,0:T(8,128)(2,1)S(1)}, f32[8,128]{1,0:T(8,128)S(1)}) custom-call(s32[5]{0:T(128)S(1)} %stack.74.refs_0_, bf16[256,1024]{1,0:T(8,128)(2,1)S(1)} %copy-done.10, ...), custom_call_target="tpu_custom_call" | custom-call | flops 40000000000 | bytes 1000000 | tf_op jit(solution)/shard_map/own_core_rows/pallas_call | solution.py:249
  165.8 2.1 collective-permute-start.21
  167.9 1.9 collective-permute-start.22
  171.5 2.4 collective-permute-start.19
  174.8 6.4 %collective-permute-done.21.refs_3_ = bf16[4,128,512]{2,1,0:T(8,128)(2,1)S(1)} collective-permute-done((bf16[4,128,512]{2,1,0:T(8,128)(2,1)S(1)}, bf16[4,128,512]{2,1,0:T(8,128)(2,1)S(1)}, u32[]{:S(2)}, u32[]{:S(2)}) %collective-permute-start.21) | collective-permute-done | bytes 524320 | tf_op jit(solution)/shard_map/ppermute | solution.py:223
  181.3 12.7 %collective-permute-done.22.refs_4_ = bf16[4,128,512]{2,1,0:T(8,128)(2,1)S(1)} collective-permute-done((bf16[4,128,512]{2,1,0:T(8,128)(2,1)S(1)}, bf16[4,128,512]{2,1,0:T(8,128)(2,1)S(1)}, u32[]{:S(2)}, u32[]{:S(2)}) %collective-permute-start.22) | collective-permute-done | bytes 524320 | tf_op jit(solution)/shard_map/ppermute | solution.py:223
  194.0 1.5 halve.5
  195.7 3.9 %collective-permute-done.19.refs_3_ = bf16[1,128,1024]{2,1,0:T(8,128)(2,1)S(1)} collective-permute-done((bf16[1,128,1024]{2,1,0:T(8,128)(2,1)S(1)}, bf16[1,128,1024]{2,1,0:T(8,128)(2,1)S(1)}, u32[]{:S(2)}, u32[]{:S(2)}) %collective-permute-start.19) | collective-permute-done | bytes 262176 | tf_op jit(solution)/shard_map/ppermute | solution.py:223
  200.4 2.3 collective-permute-start.26
  203.2 1.5 collective-permute-start.23
  205.2 1.9 collective-permute-start.24
  208.6 7.9 %collective-permute-done.26.refs_3_ = bf16[1,64,2048]{2,1,0:T(8,128)(2,1)S(1)} collective-permute-done((bf16[1,64,2048]{2,1,0:T(8,128)(2,1)S(1)}, bf16[1,64,2048]{2,1,0:T(8,128)(2,1)S(1)}, u32[]{:S(2)}, u32[]{:S(2)}) %collective-permute-start.26) | collective-permute-done | bytes 262176 | tf_op jit(solution)/shard_map/ppermute | solution.py:223
  216.9 1.6 home.4
  219.0 3.0 %collective-permute-done.23.refs_3_ = bf16[1,256,1024]{2,1,0:T(8,128)(2,1)S(1)} collective-permute-done((bf16[1,256,1024]{2,1,0:T(8,128)(2,1)S(1)}, bf16[1,256,1024]{2,1,0:T(8,128)(2,1)S(1)}, u32[]{:S(2)}, u32[]{:S(2)}) %collective-permute-start.23) | collective-permute-done | bytes 524320 | tf_op jit(solution)/shard_map/ppermute | solution.py:223
  222.9 8.5 %collective-permute-done.24.refs_4_ = bf16[1,256,1024]{2,1,0:T(8,128)(2,1)S(1)} collective-permute-done((bf16[1,256,1024]{2,1,0:T(8,128)(2,1)S(1)}, bf16[1,256,1024]{2,1,0:T(8,128)(2,1)S(1)}, u32[]{:S(2)}, u32[]{:S(2)}) %collective-permute-start.24) | collective-permute-done | bytes 524320 | tf_op jit(solution)/shard_map/ppermute | solution.py:223
  232.4 2.5 to_tokens.2
  234.9 1.4 collective-permute-done.32.refs_2_
  236.8 5.1 %assemble.3 = (f32[1,2048,1024]{2,1,0:T(8,128)}, f32[8,128]{1,0:T(8,128)S(1)}) custom-call(s32[8]{0:T(128)S(1)} %stack.86.refs_0_, bf16[1,1024,1024]{2,1,0:T(8,128)(2,1)S(1)} %get-tuple-element.254.refs_1_, bf16[1,1024,1024]{2,1,0:T(8,128)(2,1)S(1)} %collective-permute-done.32.refs_2_, f32[8,128]{1,0:T(8,128)S(1)} %get-tuple-element.255.refs_3_), custom_call_target="tpu_custom_call" | custom-call | flops 40000000000 | bytes 1000000 | tf_op jit(solution)/shard_map/assemble/pallas_call | solution.py:249
  242.7 2.1 back.5
  245.4 3.5 %join.3 = (bf16[1,512,2048]{2,1,0:T(8,128)(2,1)}, f32[8,128]{1,0:T(8,128)S(1)}) custom-call(s32[2]{0:T(128)S(1)} %pad_add_fusion.1.refs_0_, bf16[1,128,2048]{2,1,0:T(8,128)(2,1)} %get-tuple-element.258.refs_1_, bf16[1,128,2048]{2,1,0:T(8,128)(2,1)} %get-tuple-element.259.refs_2_, bf16[1,128,2048]{2,1,0:T(8,128)(2,1)} %collective-permute-done.34.refs_3_, ...), custom_call_target="tpu_custom_call" | custom-call | flops 40000000000 | bytes 1000000 | tf_op jit(solution)/shard_map/join/pallas_call | solution.py:249
  249.2 1.6 collective-permute-start.39
  250.7 3.9 %to_tokens.3 = (f32[256,1024]{1,0:T(8,128)}, f32[8,128]{1,0:T(8,128)S(1)}) custom-call(bf16[3,256,256]{2,1,0:T(8,128)(2,1)S(1)} %get-tuple-element.193.refs_5_.refs_0_, bf16[3,256,256]{2,1,0:T(8,128)(2,1)S(1)} %get-tuple-element.202.refs_6_.refs_1_, bf16[3,1024,512]{2,1,0:T(8,128)(2,1)S(1)} %bitcast.64, f32[256,1024]{1,0:T(8,128)S(1)} %copy-done.33, ...), custom_call_target="tpu_custom_call" | custom-call | flops 40000000000 | bytes 1000000 | tf_op jit(solution)/shard_map/to_tokens/pallas_call | solution.py:249
  254.6 1.8 collective-permute-start.44
  256.5 2.8 home.5
  259.3 3.9 %collective-permute-start.47 = (f32[72,128]{1,0:T(8,128)S(1)}, f32[72,128]{1,0:T(8,128)S(1)}, u32[]{:S(2)}, u32[]{:S(2)}) collective-permute-start(f32[72,128]{1,0:T(8,128)S(1)} %get-tuple-element.281.refs_0_), channel_id=1, source_target_pairs={{0,16},{2,18},{4,20},{6,22},{8,24},{10,26},{12,28},{14,30},{16,0},... | collective-permute-start | bytes 110600 | tf_op jit(solution)/shard_map/ppermute | solution.py:223
  265.2 8.2 %assemble.4 = (f32[1,1024,2048]{2,1,0:T(8,128)}, f32[8,128]{1,0:T(8,128)S(1)}) custom-call(s32[8]{0:T(128)S(1)} %stack.86.refs_0_, bf16[1,512,2048]{2,1,0:T(8,128)(2,1)} %get-tuple-element.274.refs_1_, bf16[1,512,2048]{2,1,0:T(8,128)(2,1)} %collective-permute-done.43.refs_2_, f32[8,128]{1,0:T(8,128)S(1)} %get-tuple-element.277.refs_3_), custom_call_target="tpu_custom_call" | custom-call | flops 40000000000 | bytes 1000000 | tf_op jit(solution)/shard_map/assemble/pallas_call | solution.py:249
  273.4 2.5 collective-permute-done.41.refs_3_
  281.5 7.1 %assemble.5 = (f32[3,1024,512]{2,1,0:T(8,128)}, f32[512,1024]{1,0:T(8,128)}, f32[8,128]{1,0:T(8,128)}) custom-call(s32[8]{0:T(128)S(1)} %stack.185.refs_0_, bf16[4,256,512]{2,1,0:T(8,128)(2,1)} %get-tuple-element.271.refs_1_, bf16[4,256,512]{2,1,0:T(8,128)(2,1)} %collective-permute-done.40.refs_2_, bf16[4,128,512]{2,1,0:T(8,128)(2,1)S(1)} %copy-done.18, ...), custom_call_target="tpu_custom_call" | custom-call | flops 40000000000 | bytes 1000000 | tf_op jit(solution)/shard_map/assemble/pallas_call | solution.py:249
  (193 shorter events, 39.8 us)
Async XLA Ops:
  0.6 15.3 %collective-permute-start = (bf16[256,1024]{1,0:T(8,128)(2,1)}, bf16[256,1024]{1,0:T(8,128)(2,1)}, u32[]{:S(2)}, u32[]{:S(2)}) collective-permute-start(bf16[256,1024]{1,0:T(8,128)(2,1)} %refs_1_.7), channel_id=1, source_target_pairs={{0,1},{1,0},{2,3},{3,2},{4,5},{5,4},{6,7},{7,6},{8,9},{9,8},{10,11... | collective-permute-start | bytes 1572872 | tf_op jit(solution)/shard_map/ppermute | solution.py:223
  7.5 8.5 %copy-start.3 = (bf16[1024,3,512]{2,0,1:T(8,128)(2,1)S(1)}, bf16[1024,3,512]{2,0,1:T(8,128)(2,1)}, u32[]{:S(2)}) copy-start(bf16[1024,3,512]{2,0,1:T(8,128)(2,1)} %param.16) | copy-start | bytes 9437188
  24.1 13.2 %collective-permute-start.1 = (bf16[256,1024]{1,0:T(8,128)(2,1)S(1)}, bf16[256,1024]{1,0:T(8,128)(2,1)S(1)}, u32[]{:S(2)}, u32[]{:S(2)}) collective-permute-start(bf16[256,1024]{1,0:T(8,128)(2,1)S(1)} %get-tuple-element.158), channel_id=1, source_target_pairs={{0,1},{1,0},{2,3},{3,2},{4,5},{5,4},{6,7},{7,6},{8,9},{9,8},{10,11... | collective-permute-start | bytes 1572872 | tf_op jit(solution)/shard_map/ppermute | solution.py:223
  25.9 11.4 %copy-start.9 = (bf16[256,1024]{1,0:T(8,128)(2,1)S(1)}, bf16[256,1024]{1,0:T(8,128)(2,1)}, u32[]{:S(2)}) copy-start(bf16[256,1024]{1,0:T(8,128)(2,1)} %refs_1_.7) | copy-start | bytes 1572868
  25.9 11.4 %copy-start.22 = (f32[1024]{0:T(1024)S(1)}, f32[1024]{0:T(1024)}, u32[]{:S(2)}) copy-start(f32[1024]{0:T(1024)} %param.20) | copy-start | bytes 12292
  25.9 11.4 %copy-start.23 = (f32[1024]{0:T(1024)S(1)}, f32[1024]{0:T(1024)}, u32[]{:S(2)}) copy-start(f32[1024]{0:T(1024)} %param.22) | copy-start | bytes 12292
  25.9 11.4 %copy-start.27 = (f32[1024]{0:T(1024)S(1)}, f32[1024]{0:T(1024)}, u32[]{:S(2)}) copy-start(f32[1024]{0:T(1024)} %param.21) | copy-start | bytes 12292
  38.0 60.7 %copy-start.11 = (bf16[256,1024]{1,0:T(8,128)(2,1)}, bf16[256,1024]{1,0:T(8,128)(2,1)S(1)}, u32[]{:S(2)}) copy-start(bf16[256,1024]{1,0:T(8,128)(2,1)S(1)} %get-tuple-element.160.refs_0_.refs_1_) | copy-start | bytes 1572868
  38.0 12.3 %collective-permute-start.2 = (bf16[256,1024]{1,0:T(8,128)(2,1)S(1)}, bf16[256,1024]{1,0:T(8,128)(2,1)S(1)}, u32[]{:S(2)}, u32[]{:S(2)}) collective-permute-start(bf16[256,1024]{1,0:T(8,128)(2,1)S(1)} %get-tuple-element.160.refs_0_.refs_1_), channel_id=1, source_target_pairs={{0,1},{1,0},{2,3},{3,2},{4,5},{5,4},{6,7},{7,6},{8,9},{9,8},{10,11... | collective-permute-start | bytes 1572872 | tf_op jit(solution)/shard_map/ppermute | solution.py:223
  50.3 48.4 %copy-start.13 = (bf16[256,1024]{1,0:T(8,128)(2,1)}, bf16[256,1024]{1,0:T(8,128)(2,1)S(1)}, u32[]{:S(2)}) copy-start(bf16[256,1024]{1,0:T(8,128)(2,1)S(1)} %collective-permute-done.2.refs_0_.refs_2_) | copy-start | bytes 1572868
  55.8 11.6 %collective-permute-start.3 = (bf16[256,1024]{1,0:T(8,128)(2,1)}, bf16[256,1024]{1,0:T(8,128)(2,1)}, u32[]{:S(2)}, u32[]{:S(2)}) collective-permute-start(bf16[256,1024]{1,0:T(8,128)(2,1)} %get-tuple-element.164), channel_id=1, source_target_pairs={{0,1},{1,0},{2,3},{3,2},{4,5},{5,4},{6,7},{7,6},{8,9},{9,8},{10,11... | collective-permute-start | bytes 1572872 | tf_op jit(solution)/shard_map/ppermute | solution.py:223
  56.9 10.5 %copy-start.7 = (bf16[256,1024]{1,0:T(8,128)(2,1)S(1)}, bf16[256,1024]{1,0:T(8,128)(2,1)}, u32[]{:S(2)}) copy-start(bf16[256,1024]{1,0:T(8,128)(2,1)} %refs_6_.1) | copy-start | bytes 1572868
  56.9 10.5 %copy-start.24 = (f32[1024]{0:T(1024)S(1)}, f32[1024]{0:T(1024)}, u32[]{:S(2)}) copy-start(f32[1024]{0:T(1024)} %param.26) | copy-start | bytes 12292
  56.9 10.5 %copy-start.25 = (f32[1024]{0:T(1024)S(1)}, f32[1024]{0:T(1024)}, u32[]{:S(2)}) copy-start(f32[1024]{0:T(1024)} %param.27) | copy-start | bytes 12292
  56.9 10.5 %copy-start.26 = (f32[1024]{0:T(1024)S(1)}, f32[1024]{0:T(1024)}, u32[]{:S(2)}) copy-start(f32[1024]{0:T(1024)} %param.28) | copy-start | bytes 12292
  70.1 10.3 %collective-permute-start.4 = (bf16[256,1024]{1,0:T(8,128)(2,1)S(1)}, bf16[256,1024]{1,0:T(8,128)(2,1)S(1)}, u32[]{:S(2)}, u32[]{:S(2)}) collective-permute-start(bf16[256,1024]{1,0:T(8,128)(2,1)S(1)} %get-tuple-element.169.refs_0_.refs_3_), channel_id=1, source_target_pairs={{0,1},{1,0},{2,3},{3,2},{4,5},{5,4},{6,7},{7,6},{8,9},{9,8},{10,11... | collective-permute-start | bytes 1572872 | tf_op jit(solution)/shard_map/ppermute | solution.py:223
  77.1 21.7 %copy-start.28 = (bf16[256,2048]{1,0:T(8,128)(2,1)}, bf16[256,2048]{1,0:T(8,128)(2,1)S(1)}, u32[]{:S(2)}) copy-start(bf16[256,2048]{1,0:T(8,128)(2,1)S(1)} %get-tuple-element.180.refs_3_) | copy-start | bytes 3145732
  83.7 7.4 %collective-permute-start.6 = (bf16[1,1024,1024]{2,1,0:T(8,128)(2,1)S(1)}, bf16[1,1024,1024]{2,1,0:T(8,128)(2,1)S(1)}, u32[]{:S(2)}, u32[]{:S(2)}) collective-permute-start(bf16[1,1024,1024]{2,1,0:T(8,128)(2,1)S(1)} %get-tuple-element.182), channel_id=1, source_target_pairs={{0,2},{2,0},{4,6},{6,4},{8,10},{10,8},{12,14},{14,12},{16,18},{18,... | collective-permute-start | bytes 6291464 | tf_op jit(solution)/shard_map/ppermute | solution.py:223
  90.0 8.7 %copy-start.30 = (bf16[256,2048]{1,0:T(8,128)(2,1)}, bf16[256,2048]{1,0:T(8,128)(2,1)S(1)}, u32[]{:S(2)}) copy-start(bf16[256,2048]{1,0:T(8,128)(2,1)S(1)} %get-tuple-element.181.refs_4_) | copy-start | bytes 3145732
  90.0 14.4 %collective-permute-start.5 = (bf16[256,1024]{1,0:T(8,128)(2,1)S(1)}, bf16[256,1024]{1,0:T(8,128)(2,1)S(1)}, u32[]{:S(2)}, u32[]{:S(2)}) collective-permute-start(bf16[256,1024]{1,0:T(8,128)(2,1)S(1)} %get-tuple-element.178), channel_id=1, source_target_pairs={{0,1},{1,0},{2,3},{3,2},{4,5},{5,4},{6,7},{7,6},{8,9},{9,8},{10,11... | collective-permute-start | bytes 1572872 | tf_op jit(solution)/shard_map/ppermute | solution.py:223
  95.6 14.5 %collective-permute-start.8 = (bf16[1,256,1024]{2,1,0:T(8,128)(2,1)}, bf16[1,256,1024]{2,1,0:T(8,128)(2,1)}, u32[]{:S(2)}, u32[]{:S(2)}) collective-permute-start(bf16[1,256,1024]{2,1,0:T(8,128)(2,1)} %get-tuple-element.189), channel_id=1, source_target_pairs={{0,4},{2,6},{4,0},{6,2},{8,12},{10,14},{12,8},{14,10},{16,20},{18,... | collective-permute-start | bytes 1572872 | tf_op jit(solution)/shard_map/ppermute | solution.py:223
  97.1 14.1 %collective-permute-start.9 = (bf16[1,256,1024]{2,1,0:T(8,128)(2,1)}, bf16[1,256,1024]{2,1,0:T(8,128)(2,1)}, u32[]{:S(2)}, u32[]{:S(2)}) collective-permute-start(bf16[1,256,1024]{2,1,0:T(8,128)(2,1)} %get-tuple-element.190), channel_id=1, source_target_pairs={{0,8},{2,10},{4,12},{6,14},{8,0},{10,2},{12,4},{14,6},{16,24},{18,... | collective-permute-start | bytes 1572872 | tf_op jit(solution)/shard_map/ppermute | solution.py:223
  107.8 13.8 %collective-permute-start.7 = (bf16[256,1024]{1,0:T(8,128)(2,1)}, bf16[256,1024]{1,0:T(8,128)(2,1)S(1)}, u32[]{:S(2)}, u32[]{:S(2)}) collective-permute-start(bf16[256,1024]{1,0:T(8,128)(2,1)} %copy-done.15), channel_id=1, source_target_pairs={{0,1},{1,0},{2,3},{3,2},{4,5},{5,4},{6,7},{7,6},{8,9},{9,8},{10,11... | collective-permute-start | bytes 1572872 | tf_op jit(solution)/shard_map/ppermute | solution.py:223
  108.3 23.4 %collective-permute-start.10 = (bf16[1,512,2048]{2,1,0:T(8,128)(2,1)}, bf16[1,512,2048]{2,1,0:T(8,128)(2,1)S(1)}, u32[]{:S(2)}, u32[]{:S(2)}) collective-permute-start(bf16[1,512,2048]{2,1,0:T(8,128)(2,1)} %copy-done.4), channel_id=1, source_target_pairs={{0,2},{2,0},{4,6},{6,4},{8,10},{10,8},{12,14},{14,12},{16,18},{18,... | collective-permute-start | bytes 6291464 | tf_op jit(solution)/shard_map/ppermute | solution.py:223
  113.3 8.4 %copy-start.36 = (bf16[3,256,512]{2,1,0:T(8,128)(2,1)S(1)}, bf16[3,256,512]{2,1,0:T(8,128)(2,1)}, u32[]{:S(2)}) copy-start(bf16[3,256,512]{2,1,0:T(8,128)(2,1)} %copy-done.34) | copy-start | bytes 2359300
  113.3 8.4 %copy-start.38 = (bf16[3,256,512]{2,1,0:T(8,128)(2,1)S(1)}, bf16[3,256,512]{2,1,0:T(8,128)(2,1)}, u32[]{:S(2)}) copy-start(bf16[3,256,512]{2,1,0:T(8,128)(2,1)} %copy-done.37) | copy-start | bytes 2359300
  115.7 13.5 %collective-permute-start.11 = (bf16[1,128,1024]{2,1,0:T(8,128)(2,1)S(1)}, bf16[1,128,1024]{2,1,0:T(8,128)(2,1)S(1)}, u32[]{:S(2)}, u32[]{:S(2)}) collective-permute-start(bf16[1,128,1024]{2,1,0:T(8,128)(2,1)S(1)} %get-tuple-element.197), channel_id=1, source_target_pairs={{0,8},{2,10},{4,12},{6,14},{8,0},{10,2},{12,4},{14,6},{16,24},{18,... | collective-permute-start | bytes 786440 | tf_op jit(solution)/shard_map/ppermute | solution.py:223
  117.3 11.8 %collective-permute-start.12 = (bf16[1,128,1024]{2,1,0:T(8,128)(2,1)S(1)}, bf16[1,128,1024]{2,1,0:T(8,128)(2,1)S(1)}, u32[]{:S(2)}, u32[]{:S(2)}) collective-permute-start(bf16[1,128,1024]{2,1,0:T(8,128)(2,1)S(1)} %get-tuple-element.198), channel_id=1, source_target_pairs={{0,4},{2,6},{4,0},{6,2},{8,12},{10,14},{12,8},{14,10},{16,20},{18,... | collective-permute-start | bytes 786440 | tf_op jit(solution)/shard_map/ppermute | solution.py:223
  130.2 40.0 %collective-permute-start.13 = (bf16[1,256,1024]{2,1,0:T(8,128)(2,1)}, bf16[1,256,1024]{2,1,0:T(8,128)(2,1)}, u32[]{:S(2)}, u32[]{:S(2)}) collective-permute-start(bf16[1,256,1024]{2,1,0:T(8,128)(2,1)} %get-tuple-element.206.refs_0_), channel_id=1, source_target_pairs={{0,16},{2,18},{4,20},{6,22},{8,24},{10,26},{12,28},{14,30},{16,0},... | collective-permute-start | bytes 1572872 | tf_op jit(solution)/shard_map/ppermute | solution.py:223
  135.5 15.0 %collective-permute-start.14 = (bf16[1,128,2048]{2,1,0:T(8,128)(2,1)S(1)}, bf16[1,128,2048]{2,1,0:T(8,128)(2,1)S(1)}, u32[]{:S(2)}, u32[]{:S(2)}) collective-permute-start(bf16[1,128,2048]{2,1,0:T(8,128)(2,1)S(1)} %get-tuple-element.209), channel_id=1, source_target_pairs={{0,4},{2,6},{4,0},{6,2},{8,12},{10,14},{12,8},{14,10},{16,20},{18,... | collective-permute-start | bytes 1572872 | tf_op jit(solution)/shard_map/ppermute | solution.py:223
  137.0 23.3 %collective-permute-start.15 = (bf16[1,128,2048]{2,1,0:T(8,128)(2,1)S(1)}, bf16[1,128,2048]{2,1,0:T(8,128)(2,1)S(1)}, u32[]{:S(2)}, u32[]{:S(2)}) collective-permute-start(bf16[1,128,2048]{2,1,0:T(8,128)(2,1)S(1)} %get-tuple-element.210), channel_id=1, source_target_pairs={{0,8},{2,10},{4,12},{6,14},{8,0},{10,2},{12,4},{14,6},{16,24},{18,... | collective-permute-start | bytes 1572872 | tf_op jit(solution)/shard_map/ppermute | solution.py:223
  145.9 15.7 %copy-start.43 = (bf16[3,256,256]{2,1,0:T(8,128)(2,1)}, bf16[3,256,256]{2,1,0:T(8,128)(2,1)S(1)}, u32[]{:S(2)}) copy-start(bf16[3,256,256]{2,1,0:T(8,128)(2,1)S(1)} %get-tuple-element.205.refs_8_.refs_1_) | copy-start | bytes 1179652
  149.8 11.8 %collective-permute-start.18 = (bf16[4,512,512]{2,1,0:T(8,128)(2,1)S(1)}, bf16[4,512,512]{2,1,0:T(8,128)(2,1)S(1)}, u32[]{:S(2)}, u32[]{:S(2)}) collective-permute-start(bf16[4,512,512]{2,1,0:T(8,128)(2,1)S(1)} %get-tuple-element.219), channel_id=1, source_target_pairs={{0,2},{2,0},{4,6},{6,4},{8,10},{10,8},{12,14},{14,12},{16,18},{18,... | collective-permute-start | bytes 6291464 | tf_op jit(solution)/shard_map/ppermute | solution.py:223
  161.4 8.4 %collective-permute-start.16 = (bf16[1,64,2048]{2,1,0:T(8,128)(2,1)S(1)}, bf16[1,64,2048]{2,1,0:T(8,128)(2,1)S(1)}, u32[]{:S(2)}, u32[]{:S(2)}) collective-permute-start(bf16[1,64,2048]{2,1,0:T(8,128)(2,1)S(1)} %get-tuple-element.217), channel_id=1, source_target_pairs={{0,8},{2,10},{4,12},{6,14},{8,0},{10,2},{12,4},{14,6},{16,24},{18,... | collective-permute-start | bytes 786440 | tf_op jit(solution)/shard_map/ppermute | solution.py:223
  161.5 8.5 %collective-permute-start.17 = (bf16[1,64,2048]{2,1,0:T(8,128)(2,1)S(1)}, bf16[1,64,2048]{2,1,0:T(8,128)(2,1)S(1)}, u32[]{:S(2)}, u32[]{:S(2)}) collective-permute-start(bf16[1,64,2048]{2,1,0:T(8,128)(2,1)S(1)} %get-tuple-element.218), channel_id=1, source_target_pairs={{0,4},{2,6},{4,0},{6,2},{8,12},{10,14},{12,8},{14,10},{16,20},{18,... | collective-permute-start | bytes 786440 | tf_op jit(solution)/shard_map/ppermute | solution.py:223
  165.8 15.5 %collective-permute-start.21 = (bf16[4,128,512]{2,1,0:T(8,128)(2,1)S(1)}, bf16[4,128,512]{2,1,0:T(8,128)(2,1)S(1)}, u32[]{:S(2)}, u32[]{:S(2)}) collective-permute-start(bf16[4,128,512]{2,1,0:T(8,128)(2,1)S(1)} %get-tuple-element.227), channel_id=1, source_target_pairs={{0,4},{2,6},{4,0},{6,2},{8,12},{10,14},{12,8},{14,10},{16,20},{18,... | collective-permute-start | bytes 1572872 | tf_op jit(solution)/shard_map/ppermute | solution.py:223
  167.9 26.1 %collective-permute-start.22 = (bf16[4,128,512]{2,1,0:T(8,128)(2,1)S(1)}, bf16[4,128,512]{2,1,0:T(8,128)(2,1)S(1)}, u32[]{:S(2)}, u32[]{:S(2)}) collective-permute-start(bf16[4,128,512]{2,1,0:T(8,128)(2,1)S(1)} %get-tuple-element.228), channel_id=1, source_target_pairs={{0,8},{2,10},{4,12},{6,14},{8,0},{10,2},{12,4},{14,6},{16,24},{18,... | collective-permute-start | bytes 1572872 | tf_op jit(solution)/shard_map/ppermute | solution.py:223
  171.5 28.1 %collective-permute-start.19 = (bf16[1,128,1024]{2,1,0:T(8,128)(2,1)S(1)}, bf16[1,128,1024]{2,1,0:T(8,128)(2,1)S(1)}, u32[]{:S(2)}, u32[]{:S(2)}) collective-permute-start(bf16[1,128,1024]{2,1,0:T(8,128)(2,1)S(1)} %get-tuple-element.223.refs_1_), channel_id=1, source_target_pairs={{0,8},{2,10},{4,12},{6,14},{8,0},{10,2},{12,4},{14,6},{16,24},{18,... | collective-permute-start | bytes 786440 | tf_op jit(solution)/shard_map/ppermute | solution.py:223
  173.8 25.8 %collective-permute-start.20 = (bf16[1,128,1024]{2,1,0:T(8,128)(2,1)S(1)}, bf16[1,128,1024]{2,1,0:T(8,128)(2,1)S(1)}, u32[]{:S(2)}, u32[]{:S(2)}) collective-permute-start(bf16[1,128,1024]{2,1,0:T(8,128)(2,1)S(1)} %get-tuple-element.224.refs_2_), channel_id=1, source_target_pairs={{0,4},{2,6},{4,0},{6,2},{8,12},{10,14},{12,8},{14,10},{16,20},{18,... | collective-permute-start | bytes 786440 | tf_op jit(solution)/shard_map/ppermute | solution.py:223
  173.8 26.4 %collective-permute-start.25 = (bf16[1,128,2048]{2,1,0:T(8,128)(2,1)S(1)}, bf16[1,128,2048]{2,1,0:T(8,128)(2,1)S(1)}, u32[]{:S(2)}, u32[]{:S(2)}) collective-permute-start(bf16[1,128,2048]{2,1,0:T(8,128)(2,1)S(1)} %get-tuple-element.233.refs_0_), channel_id=1, source_target_pairs={{0,16},{2,18},{4,20},{6,22},{8,24},{10,26},{12,28},{14,30},{16,0},... | collective-permute-start | bytes 1572872 | tf_op jit(solution)/shard_map/ppermute | solution.py:223
  195.5 9.7 %collective-permute-start.28 = (bf16[4,64,512]{2,1,0:T(8,128)(2,1)S(1)}, bf16[4,64,512]{2,1,0:T(8,128)(2,1)S(1)}, u32[]{:S(2)}, u32[]{:S(2)}) collective-permute-start(bf16[4,64,512]{2,1,0:T(8,128)(2,1)S(1)} %get-tuple-element.239), channel_id=1, source_target_pairs={{0,8},{2,10},{4,12},{6,14},{8,0},{10,2},{12,4},{14,6},{16,24},{18,... | collective-permute-start | bytes 786440 | tf_op jit(solution)/shard_map/ppermute | solution.py:223
  195.6 11.6 %collective-permute-start.29 = (bf16[4,64,512]{2,1,0:T(8,128)(2,1)S(1)}, bf16[4,64,512]{2,1,0:T(8,128)(2,1)S(1)}, u32[]{:S(2)}, u32[]{:S(2)}) collective-permute-start(bf16[4,64,512]{2,1,0:T(8,128)(2,1)S(1)} %get-tuple-element.240), channel_id=1, source_target_pairs={{0,4},{2,6},{4,0},{6,2},{8,12},{10,14},{12,8},{14,10},{16,20},{18,... | collective-permute-start | bytes 786440 | tf_op jit(solution)/shard_map/ppermute | solution.py:223
  200.4 16.1 %collective-permute-start.26 = (bf16[1,64,2048]{2,1,0:T(8,128)(2,1)S(1)}, bf16[1,64,2048]{2,1,0:T(8,128)(2,1)S(1)}, u32[]{:S(2)}, u32[]{:S(2)}) collective-permute-start(bf16[1,64,2048]{2,1,0:T(8,128)(2,1)S(1)} %get-tuple-element.235.refs_1_), channel_id=1, source_target_pairs={{0,8},{2,10},{4,12},{6,14},{8,0},{10,2},{12,4},{14,6},{16,24},{18,... | collective-permute-start | bytes 786440 | tf_op jit(solution)/shard_map/ppermute | solution.py:223
  202.6 14.3 %collective-permute-start.27 = (bf16[1,64,2048]{2,1,0:T(8,128)(2,1)S(1)}, bf16[1,64,2048]{2,1,0:T(8,128)(2,1)S(1)}, u32[]{:S(2)}, u32[]{:S(2)}) collective-permute-start(bf16[1,64,2048]{2,1,0:T(8,128)(2,1)S(1)} %get-tuple-element.236.refs_2_), channel_id=1, source_target_pairs={{0,4},{2,6},{4,0},{6,2},{8,12},{10,14},{12,8},{14,10},{16,20},{18,... | collective-permute-start | bytes 786440 | tf_op jit(solution)/shard_map/ppermute | solution.py:223
  203.2 18.8 %collective-permute-start.23 = (bf16[1,256,1024]{2,1,0:T(8,128)(2,1)S(1)}, bf16[1,256,1024]{2,1,0:T(8,128)(2,1)S(1)}, u32[]{:S(2)}, u32[]{:S(2)}) collective-permute-start(bf16[1,256,1024]{2,1,0:T(8,128)(2,1)S(1)} %get-tuple-element.231.refs_1_), channel_id=1, source_target_pairs={{0,4},{2,6},{4,0},{6,2},{8,12},{10,14},{12,8},{14,10},{16,20},{18,... | collective-permute-start | bytes 1572872 | tf_op jit(solution)/shard_map/ppermute | solution.py:223
  205.2 26.2 %collective-permute-start.24 = (bf16[1,256,1024]{2,1,0:T(8,128)(2,1)S(1)}, bf16[1,256,1024]{2,1,0:T(8,128)(2,1)S(1)}, u32[]{:S(2)}, u32[]{:S(2)}) collective-permute-start(bf16[1,256,1024]{2,1,0:T(8,128)(2,1)S(1)} %get-tuple-element.232.refs_2_), channel_id=1, source_target_pairs={{0,8},{2,10},{4,12},{6,14},{8,0},{10,2},{12,4},{14,6},{16,24},{18,... | collective-permute-start | bytes 1572872 | tf_op jit(solution)/shard_map/ppermute | solution.py:223
  208.1 33.8 %collective-permute-start.31 = (f32[72,128]{1,0:T(8,128)}, f32[72,128]{1,0:T(8,128)}, u32[]{:S(2)}, u32[]{:S(2)}) collective-permute-start(f32[72,128]{1,0:T(8,128)} %maximum_bitcast_fusion.refs_0_), channel_id=1, source_target_pairs={{0,1},{1,0},{2,3},{3,2},{4,5},{5,4},{6,7},{7,6},{8,9},{9,8},{10,11... | collective-permute-start | bytes 110600 | tf_op jit(solution)/shard_map/ppermute | solution.py:223
  216.4 26.2 %collective-permute-start.36 = (bf16[4,128,512]{2,1,0:T(8,128)(2,1)}, bf16[4,128,512]{2,1,0:T(8,128)(2,1)}, u32[]{:S(2)}, u32[]{:S(2)}) collective-permute-start(bf16[4,128,512]{2,1,0:T(8,128)(2,1)} %get-tuple-element.260.refs_0_), channel_id=1, source_target_pairs={{0,16},{2,18},{4,20},{6,22},{8,24},{10,26},{12,28},{14,30},{16,0},... | collective-permute-start | bytes 1572872 | tf_op jit(solution)/shard_map/ppermute | solution.py:223
  218.5 26.3 %collective-permute-start.34 = (bf16[1,128,2048]{2,1,0:T(8,128)(2,1)}, bf16[1,128,2048]{2,1,0:T(8,128)(2,1)}, u32[]{:S(2)}, u32[]{:S(2)}) collective-permute-start(bf16[1,128,2048]{2,1,0:T(8,128)(2,1)} %get-tuple-element.258.refs_1_), channel_id=1, source_target_pairs={{0,4},{2,6},{4,0},{6,2},{8,12},{10,14},{12,8},{14,10},{16,20},{18,... | collective-permute-start | bytes 1572872 | tf_op jit(solution)/shard_map/ppermute | solution.py:223
  222.0 23.4 %collective-permute-start.35 = (bf16[1,128,2048]{2,1,0:T(8,128)(2,1)}, bf16[1,128,2048]{2,1,0:T(8,128)(2,1)}, u32[]{:S(2)}, u32[]{:S(2)}) collective-permute-start(bf16[1,128,2048]{2,1,0:T(8,128)(2,1)} %get-tuple-element.259.refs_2_), channel_id=1, source_target_pairs={{0,8},{2,10},{4,12},{6,14},{8,0},{10,2},{12,4},{14,6},{16,24},{18,... | collective-permute-start | bytes 1572872 | tf_op jit(solution)/shard_map/ppermute | solution.py:223
  232.1 4.2 %collective-permute-start.32 = (bf16[1,1024,1024]{2,1,0:T(8,128)(2,1)S(1)}, bf16[1,1024,1024]{2,1,0:T(8,128)(2,1)S(1)}, u32[]{:S(2)}, u32[]{:S(2)}) collective-permute-start(bf16[1,1024,1024]{2,1,0:T(8,128)(2,1)S(1)} %get-tuple-element.254.refs_1_), channel_id=1, source_target_pairs={{0,2},{2,0},{4,6},{6,4},{8,10},{10,8},{12,14},{14,12},{16,18},{18,... | collective-permute-start | bytes 6291464 | tf_op jit(solution)/shard_map/ppermute | solution.py:223
  236.3 14.4 %collective-permute-start.30 = (bf16[256,1024]{1,0:T(8,128)(2,1)}, bf16[256,1024]{1,0:T(8,128)(2,1)}, u32[]{:S(2)}, u32[]{:S(2)}) collective-permute-start(bf16[256,1024]{1,0:T(8,128)(2,1)} %get-tuple-element.245), channel_id=1, source_target_pairs={{0,1},{1,0},{2,3},{3,2},{4,5},{5,4},{6,7},{7,6},{8,9},{9,8},{10,11... | collective-permute-start | bytes 1572872 | tf_op jit(solution)/shard_map/ppermute | solution.py:223
  242.7 6.5 %collective-permute-start.33 = (f32[72,128]{1,0:T(8,128)S(1)}, f32[72,128]{1,0:T(8,128)S(1)}, u32[]{:S(2)}, u32[]{:S(2)}) collective-permute-start(f32[72,128]{1,0:T(8,128)S(1)} %get-tuple-element.257.refs_0_), channel_id=1, source_target_pairs={{0,2},{2,0},{4,6},{6,4},{8,10},{10,8},{12,14},{14,12},{16,18},{18,... | collective-permute-start | bytes 110600 | tf_op jit(solution)/shard_map/ppermute | solution.py:223
  244.8 11.7 %collective-permute-start.37 = (bf16[4,64,512]{2,1,0:T(8,128)(2,1)}, bf16[4,64,512]{2,1,0:T(8,128)(2,1)}, u32[]{:S(2)}, u32[]{:S(2)}) collective-permute-start(bf16[4,64,512]{2,1,0:T(8,128)(2,1)} %get-tuple-element.266.refs_1_), channel_id=1, source_target_pairs={{0,8},{2,10},{4,12},{6,14},{8,0},{10,2},{12,4},{14,6},{16,24},{18,... | collective-permute-start | bytes 786440 | tf_op jit(solution)/shard_map/ppermute | solution.py:223
  244.8 11.7 %collective-permute-start.38 = (bf16[4,64,512]{2,1,0:T(8,128)(2,1)}, bf16[4,64,512]{2,1,0:T(8,128)(2,1)}, u32[]{:S(2)}, u32[]{:S(2)}) collective-permute-start(bf16[4,64,512]{2,1,0:T(8,128)(2,1)} %get-tuple-element.267.refs_2_), channel_id=1, source_target_pairs={{0,4},{2,6},{4,0},{6,2},{8,12},{10,14},{12,8},{14,10},{16,20},{18,... | collective-permute-start | bytes 786440 | tf_op jit(solution)/shard_map/ppermute | solution.py:223
  248.9 16.3 %collective-permute-start.43 = (bf16[1,512,2048]{2,1,0:T(8,128)(2,1)}, bf16[1,512,2048]{2,1,0:T(8,128)(2,1)}, u32[]{:S(2)}, u32[]{:S(2)}) collective-permute-start(bf16[1,512,2048]{2,1,0:T(8,128)(2,1)} %get-tuple-element.274.refs_1_), channel_id=1, source_target_pairs={{0,2},{2,0},{4,6},{6,4},{8,10},{10,8},{12,14},{14,12},{16,18},{18,... | collective-permute-start | bytes 6291464 | tf_op jit(solution)/shard_map/ppermute | solution.py:223
  249.2 5.5 %collective-permute-start.39 = (f32[72,128]{1,0:T(8,128)S(1)}, f32[72,128]{1,0:T(8,128)S(1)}, u32[]{:S(2)}, u32[]{:S(2)}) collective-permute-start(f32[72,128]{1,0:T(8,128)S(1)} %get-tuple-element.268.refs_0_), channel_id=1, source_target_pairs={{0,4},{2,6},{4,0},{6,2},{8,12},{10,14},{12,8},{14,10},{16,20},{18,... | collective-permute-start | bytes 110600 | tf_op jit(solution)/shard_map/ppermute | solution.py:223
  254.6 4.7 %collective-permute-start.44 = (f32[72,128]{1,0:T(8,128)S(1)}, f32[72,128]{1,0:T(8,128)S(1)}, u32[]{:S(2)}, u32[]{:S(2)}) collective-permute-start(f32[72,128]{1,0:T(8,128)S(1)} %get-tuple-element.275.refs_0_), channel_id=1, source_target_pairs={{0,8},{2,10},{4,12},{6,14},{8,0},{10,2},{12,4},{14,6},{16,24},{18,... | collective-permute-start | bytes 110600 | tf_op jit(solution)/shard_map/ppermute | solution.py:223
  259.3 17.7 %collective-permute-start.47 = (f32[72,128]{1,0:T(8,128)S(1)}, f32[72,128]{1,0:T(8,128)S(1)}, u32[]{:S(2)}, u32[]{:S(2)}) collective-permute-start(f32[72,128]{1,0:T(8,128)S(1)} %get-tuple-element.281.refs_0_), channel_id=1, source_target_pairs={{0,16},{2,18},{4,20},{6,22},{8,24},{10,26},{12,28},{14,30},{16,0},... | collective-permute-start | bytes 110600 | tf_op jit(solution)/shard_map/ppermute | solution.py:223
  263.2 12.7 %collective-permute-start.41 = (bf16[4,128,512]{2,1,0:T(8,128)(2,1)S(1)}, bf16[4,128,512]{2,1,0:T(8,128)(2,1)S(1)}, u32[]{:S(2)}, u32[]{:S(2)}) collective-permute-start(bf16[4,128,512]{2,1,0:T(8,128)(2,1)S(1)} %get-tuple-element.272), channel_id=1, source_target_pairs={{0,4},{2,6},{4,0},{6,2},{8,12},{10,14},{12,8},{14,10},{16,20},{18,... | collective-permute-start | bytes 1572872 | tf_op jit(solution)/shard_map/ppermute | solution.py:223
  264.3 12.7 %collective-permute-start.42 = (bf16[4,128,512]{2,1,0:T(8,128)(2,1)S(1)}, bf16[4,128,512]{2,1,0:T(8,128)(2,1)S(1)}, u32[]{:S(2)}, u32[]{:S(2)}) collective-permute-start(bf16[4,128,512]{2,1,0:T(8,128)(2,1)S(1)} %get-tuple-element.273), channel_id=1, source_target_pairs={{0,8},{2,10},{4,12},{6,14},{8,0},{10,2},{12,4},{14,6},{16,24},{18,... | collective-permute-start | bytes 1572872 | tf_op jit(solution)/shard_map/ppermute | solution.py:223
  265.2 15.9 %collective-permute-start.40 = (bf16[4,256,512]{2,1,0:T(8,128)(2,1)}, bf16[4,256,512]{2,1,0:T(8,128)(2,1)}, u32[]{:S(2)}, u32[]{:S(2)}) collective-permute-start(bf16[4,256,512]{2,1,0:T(8,128)(2,1)} %get-tuple-element.271.refs_1_), channel_id=1, source_target_pairs={{0,2},{2,0},{4,6},{6,4},{8,10},{10,8},{12,14},{14,12},{16,18},{18,... | collective-permute-start | bytes 3145736 | tf_op jit(solution)/shard_map/ppermute | solution.py:223
  278.8 2.3 collective-permute-start.45
  279.0 2.5 collective-permute-start.46
  (33 other events, 100.1 us)
